TPU v7x, 32 devices: a whole 2x2x4 slice. The times are simulated.
32 devices in a mesh: groups: 2 (over x), owners: 16 (over z, y, core).
Axes of the slice: x: 2, y: 2, z: 4, core: 2. Of those that a mesh axis runs over, the one named last changes fastest.
Arguments:
- embeddings: bfloat16 [32768, 1024], P(('groups', 'owners')), parts along dimension 0, may hold values from -30 to 30
- cluster_id: int32 [32768], P(('groups', 'owners')), parts along dimension 0, may hold values from 0 to 127, as said below
- valid: int32 [32768], P(('groups', 'owners')), parts along dimension 0, may hold values 0 or 1
Outputs:
- nearest: float32 [32768], P(('groups', 'owners')), parts along dimension 0
There are 2 independent parts, one for each index of `groups`. A program takes and returns all parts, laid end to end along the dimension named above; each array names one. Nothing has to cross between parts.
Inputs may be any that keep to these rules, and one draw needn't show every extreme that they name: `cluster_id`: among the 1024 rows of one device no cluster appears more than 16 times, and one cluster appears exactly 16 times among the rows of every device.
All inputs are finite; a program needn't handle non-finite values. No bound on the sum of `valid` on one device may be relied on, other than what follows from the above.
Results may differ from a plain program's by a relative error of at most 0.00053.
Values may be sent and summed in bfloat16 or wider, within the bound.
No kernel may reach another device: no remote copies, remote signals or barrier semaphores. Data moves between devices by JAX's collectives and lax.ppermute only.
A program may use at most 128 MiB of HBM per device.

v0:
```python
import jax
import jax.numpy as jnp
from jax import lax
from jax.sharding import PartitionSpec as P

CL_DEV = 8
SLOT = 16


def block_maxima(unit_rows, live_flags):
    members = unit_rows.shape[1]
    step_rows = min(512, members)
    blocks = members // step_rows
    flags = live_flags > 0.5
    results = [
        jnp.full((unit_rows.shape[0], step_rows), -1.0, jnp.float32) for number in range(blocks)
    ]
    for first_block in range(blocks):
        partners = range(blocks)
        for second in partners:
            left_rows = unit_rows[:, first_block * step_rows : (first_block + 1) * step_rows]
            right_rows = unit_rows[:, second * step_rows : (second + 1) * step_rows]
            scores = jnp.einsum(
                "kmd,knd->kmn", left_rows, right_rows, preferred_element_type=jnp.float32
            )
            row_flags = flags[:, first_block * step_rows : (first_block + 1) * step_rows]
            col_flags = flags[:, second * step_rows : (second + 1) * step_rows]
            allowed = row_flags[:, :, None] & col_flags[:, None, :]
            if first_block == second:
                allowed = allowed & ~jnp.eye(step_rows, dtype=bool)[None]
            masked = jnp.where(allowed, scores, -1.0)
            results[first_block] = jnp.maximum(results[first_block], jnp.max(masked, axis=2))
    return jnp.concatenate(results, axis=1)


def shards(embeddings, cluster_id, valid):
    owners = lax.axis_size("owners")
    width = embeddings.shape[1]
    clusters = CL_DEV * owners
    values = embeddings.astype(jnp.float32)
    squares = jnp.sum(values * values, axis=1, keepdims=True)
    scale = lax.rsqrt(squares + 1e-06)
    unit_rows = (values * scale).astype(jnp.bfloat16)
    one_hot = (cluster_id[:, None] == jnp.arange(clusters, dtype=jnp.int32)[None, :]).astype(
        jnp.int32
    )
    ranking = jnp.sum(jnp.cumsum(one_hot, axis=0) * one_hot, axis=1) - 1
    owner_of = cluster_id // CL_DEV
    local_of = cluster_id % CL_DEV
    target = (local_of * owners + owner_of) * SLOT + ranking
    slots_all = clusters * SLOT
    outgoing = (
        jnp.zeros((slots_all, width), jnp.bfloat16)
        .at[target]
        .set(unit_rows)
        .reshape(CL_DEV, owners, SLOT, width)
    )
    live_out = (
        jnp.zeros((slots_all,), jnp.bfloat16)
        .at[target]
        .set(valid.astype(jnp.bfloat16))
        .reshape(CL_DEV, owners, SLOT)
    )
    rows_in, live_in = (
        lax.all_to_all(outgoing, "owners", split_axis=1, concat_axis=1, tiled=True),
        lax.all_to_all(live_out, "owners", split_axis=1, concat_axis=1, tiled=True),
    )
    items = rows_in.shape[0]
    best = block_maxima(
        rows_in.reshape(items, owners * SLOT, width), live_in.reshape(items, owners * SLOT)
    )
    returned = lax.all_to_all(
        best.reshape(items, owners, SLOT), "owners", split_axis=1, concat_axis=1, tiled=True
    )
    nearest = returned.reshape(-1)[target]
    return jnp.where(valid == 1, nearest, 0.0)


def solution(mesh):
    placed = (P(("groups", "owners"), None), P(("groups", "owners")), P(("groups", "owners")))
    return jax.shard_map(
        shards, mesh=mesh, in_specs=placed, out_specs=P(("groups", "owners")), check_vma=False
    )
```

profile of v0, /device:TPU:0, one launch (start us, length us, event | category | flops | bytes accessed | tf_op | source)
XLA Modules:
  0.0 155.7 jit_solution(4527730174793919904)
XLA Ops:
  0.0 0.0 copy-start
  0.0 0.9 copy.10
  0.9 0.2 fusion.7
  1.2 0.1 copy.11
  1.3 1.0 fusion.6
  2.4 0.7 broadcast_clamp_fusion
  3.1 0.7 convert_element_type.15
  3.8 7.6 %scatter_custom_fusion = bf16[2048]{0:T(1024)(128)(2,1)S(1)} fusion(s32[1024]{0:T(1024)S(1)} %get-tuple-element.6, bf16[1024]{0:T(1024)(128)(2,1)S(1)} %convert_element_type.15, bf16[]{:T(256)} %constant.41.clone.1), kind=kCustom, calls=%fused_computation.42 | custom fusion | bytes 4098 | tf_op jit(solution)/shard_map/scatter | solution.py:61
  11.4 0.1 reshape.61
  11.5 0.6 copy.12
  12.1 7.4 %all-to-all-start = ((bf16[8,16,16]{2,0,1:T(8,128)(2,1)}), bf16[8,16,16]{2,0,1:T(8,128)(2,1)S(1)}, u32[]{:S(2)}, u32[]{:S(2)}) async-start(bf16[8,16,16]{2,0,1:T(8,128)(2,1)} %copy.12), calls=%async_computation | async-start | bytes 65536 | tf_op jit(solution)/shard_map/all_to_all | solution.py:66
  19.5 0.0 copy-done
  19.5 0.5 fusion
  20.0 8.3 %scatter_custom_fusion.1 = bf16[2048,1024]{1,0:T(8,128)(2,1)} fusion(s32[1024]{0:T(1024)S(1)} %get-tuple-element.6, bf16[1024,1024]{1,0:T(8,128)(2,1)S(1)} %copy-done, f32[1024]{0:T(1024)S(1)} %add_rsqrt_fusion, bf16[]{:T(256)} %constant.41.clone.1), kind=kCustom, calls=%fused_computation.7 | custom fusion | flops 3145728 | bytes 6295554 | tf_op jit(solution)/shard_map/scatter | solution.py:55
  28.3 5.0 %copy.14 = bf16[8,16,16,1024]{3,2,0,1:T(8,128)(2,1)} copy(bf16[8,16,16,1024]{3,2,1,0:T(8,128)(2,1)} %bitcast.17) | data formatting | bytes 8388608 | tf_op jit(solution)/shard_map/reshape | solution.py:56
  33.3 0.0 all-to-all-done
  33.3 6.1 %all-to-all-start.1 = ((bf16[8,16,16,1024]{3,2,0,1:T(8,128)(2,1)}), bf16[8,16,16,1024]{3,2,0,1:T(8,128)(2,1)}, u32[]{:S(2)}, u32[]{:S(2)}) async-start(bf16[8,16,16,1024]{3,2,0,1:T(8,128)(2,1)} %copy.14), calls=%async_computation.1 | async-start | bytes 8388608 | tf_op jit(solution)/shard_map/all_to_all | solution.py:65
  39.4 0.1 gt.19
  39.5 77.5 %all-to-all-done.1 = bf16[8,16,16,1024]{3,2,0,1:T(8,128)(2,1)} async-done(((bf16[8,16,16,1024]{3,2,0,1:T(8,128)(2,1)}), bf16[8,16,16,1024]{3,2,0,1:T(8,128)(2,1)}, u32[]{:S(2)}, u32[]{:S(2)}) %all-to-all-start.1) | async-done | bytes 4194336 | tf_op jit(solution)/shard_map/all_to_all | solution.py:65
  117.0 2.6 %copy.15 = bf16[8,16,16,1024]{3,2,1,0:T(8,128)(2,1)S(1)} copy(bf16[8,16,16,1024]{3,2,0,1:T(8,128)(2,1)} %all-to-all-done.1) | data formatting | bytes 8388608 | tf_op jit(solution)/shard_map/all_to_all | solution.py:65
  119.6 1.8 %select_reduce_fusion = f32[8,256]{1,0:T(8,128)S(1)} fusion(bf16[8,256,1024]{2,1,0:T(8,128)(2,1)S(1)} %bitcast.18, pred[256,256]{0,1:T(8,128)(4,1)S(1)} %fusion.10, pred[8,256]{1,0:T(8,128)(4,1)S(1)} %gt.19), kind=kOutput, calls=%fused_computation.8 | convolution fusion | flops 1075836928 | bytes 4270080 | tf_op jit(solution)/shard_map/kmd,knd->kmn/dot_general | solution.py:23
  121.5 0.0 copy-start.1
  121.5 0.1 max_broadcast_in_dim.8
  121.6 0.1 reshape.96
  121.7 25.8 %all_to_all.15 = f32[16,1,128]{2,1,0:T(1,128)S(1)} all-to-all(f32[16,1,128]{2,1,0:T(1,128)S(1)} %reshape.96), channel_id=1, replica_groups=mesh['groups'=2,'owners'=16] {'owners'}, dimensions={0} | all-to-all | bytes 16384 | tf_op jit(solution)/shard_map/all_to_all | solution.py:72
  147.6 0.5 broadcast.81
  148.1 0.7 reduce
  148.7 0.1 reshape.97
  148.8 0.1 reshape.64
  148.9 6.1 %gather_fusion = f32[1024]{0:T(1024)S(1)} fusion(f32[2048]{0:T(1024)S(1)} %reshape.64, s32[1024]{0:T(1024)S(1)} %get-tuple-element.5), kind=kCustom, calls=%fused_computation | custom fusion | bytes 12288 | tf_op jit(solution)/shard_map/gather | solution.py:75
  155.1 0.0 copy-done.1
  155.1 0.6 compare_select_fusion.1
  (11 shorter events, 0.2 us)
Async XLA Ops:
  0.0 19.5 %copy-start = (bf16[1024,1024]{1,0:T(8,128)(2,1)S(1)}, bf16[1024,1024]{1,0:T(8,128)(2,1)}, u32[]{:S(2)}) copy-start(bf16[1024,1024]{1,0:T(8,128)(2,1)} %param.3) | copy-start | bytes 6291460
  12.1 21.2 %all-to-all-start = ((bf16[8,16,16]{2,0,1:T(8,128)(2,1)}), bf16[8,16,16]{2,0,1:T(8,128)(2,1)S(1)}, u32[]{:S(2)}, u32[]{:S(2)}) async-start(bf16[8,16,16]{2,0,1:T(8,128)(2,1)} %copy.12), calls=%async_computation | async-start | bytes 65536 | tf_op jit(solution)/shard_map/all_to_all | solution.py:66
  33.3 83.7 %all-to-all-start.1 = ((bf16[8,16,16,1024]{3,2,0,1:T(8,128)(2,1)}), bf16[8,16,16,1024]{3,2,0,1:T(8,128)(2,1)}, u32[]{:S(2)}, u32[]{:S(2)}) async-start(bf16[8,16,16,1024]{3,2,0,1:T(8,128)(2,1)} %copy.14), calls=%async_computation.1 | async-start | bytes 8388608 | tf_op jit(solution)/shard_map/all_to_all | solution.py:65
  121.5 33.6 %copy-start.1 = (s32[1024]{0:T(1024)S(1)}, s32[1024]{0:T(1024)}, u32[]{:S(2)}) copy-start(s32[1024]{0:T(1024)} %param.5) | copy-start | bytes 12292
where the time goes:
time: 156 us
  waiting for transfers between devices  77.5 us (50%)
  blocking collectives  25.8 us (17%)
  local copies, waits for them, and re-layouts  24 us (15%)
  starting transfers between devices  13.4 us (9%)
  other arithmetic  12.8 us (8%)
  matrix products  1.82 us (1%)
    all_to_all x1, waiting for transfers between devices, shards(): lax.all_to_all(outgoing, 'owners', split_axis=1, concat_axis=1, tiled=True)  77.5 us
    all_to_all x1, blocking collectives, shards(): lax.all_to_all(best.reshape(items, owners, SLOT), 'owners', split_axis=1,...  25.8 us
    scatter x1, other arithmetic, shards(): outgoing = jnp.zeros((slots_all, width), jnp.bfloat16).at[target].set(uni...  8.33 us
    scatter x1, local copies, waits for them, and re-layouts, shards(): live_out = jnp.zeros((slots_all,), jnp.bfloat16).at[target].set(valid.ast...  7.58 us
    all_to_all x1, starting transfers between devices, shards(): lax.all_to_all(live_out, 'owners', split_axis=1, concat_axis=1, tiled=True)  7.39 us
    gather x1, local copies, waits for them, and re-layouts, shards(): nearest = returned.reshape(-1)[target]  6.15 us
    all_to_all x1, starting transfers between devices, shards(): lax.all_to_all(outgoing, 'owners', split_axis=1, concat_axis=1, tiled=True)  6.06 us
    reshape x1, local copies, waits for them, and re-layouts, shards(): outgoing = jnp.zeros((slots_all, width), jnp.bfloat16).at[target].set(uni...  4.95 us
  transfers between devices with their start and end apart: 2, of which 1 were waited for; matrix products, arithmetic and copies ran while one was open for 9% of the time, Pallas kernels for 0%

commit v1 on v0

v1 whole, which is shorter than its diff:
```python
import functools

import jax
import jax.numpy as jnp
from jax import lax
from jax.experimental import pallas as pl
from jax.experimental.pallas import tpu as pltpu
from jax.sharding import PartitionSpec as P

CL_DEV = 8
SLOT = 16
LANES = 128
FAST = 64
SPILL = 32
STEP = 256
VMEM = 48 * 1024 * 1024
BF = jnp.bfloat16
F32 = jnp.float32


def iota(shape, dim):
    return lax.broadcasted_iota(jnp.int32, shape, dim)


def ahead(chunk):
    return (iota((chunk, chunk), 0) < iota((chunk, chunk), 1)).astype(BF)


def count_ahead(flags):
    rows = flags.shape[1]
    chunk = min(rows, 1024)
    before = ahead(chunk)
    offset = jnp.zeros((flags.shape[0], 1), F32)
    pieces = []
    for start in range(0, rows, chunk):
        part = flags[:, start : start + chunk]
        pieces.append(jnp.dot(part, before, preferred_element_type=F32) + offset)
        offset = offset + jnp.sum(part.astype(F32), axis=1, keepdims=True)
    return jnp.concatenate(pieces, axis=1) if len(pieces) > 1 else pieces[0]


def pack_kernel(
    owners, cid_ref, valid_ref, rows_ref, blocks_ref, spill_ref, code_ref, unit_ref, dest_ref, meta_ref
):
    rows = rows_ref.shape[0]
    step = pl.program_id(0)

    @pl.when(step == 0)
    def _():
        cid = cid_ref[...]
        live = valid_ref[...] == 1
        owner = lax.shift_right_logical(cid, 3)
        local = cid & (CL_DEV - 1)
        mine = (iota((owners, rows), 0) == owner) & live
        mine_f = mine.astype(F32)
        rank = count_ahead(mine_f.astype(BF))
        pos = jnp.sum(mine_f * rank, axis=0, keepdims=True).astype(jnp.int32)
        fits = live & (pos < FAST - 1)
        over = live & (pos >= FAST - 1)
        over_f = jnp.broadcast_to(over.astype(F32), (8, rows))
        spot = count_ahead(over_f.astype(BF))[0:1].astype(jnp.int32)
        spilled = over & (spot < SPILL)
        lost = jnp.max((over & (spot >= SPILL)).astype(F32), axis=1, keepdims=True)
        code = jnp.where(fits, pos, jnp.where(spilled, FAST + spot, LANES - 1))
        code_ref[...] = code
        dest = jnp.where(
            fits, owner * FAST + pos, jnp.where(spilled, owners * FAST + spot, -1)
        )
        dest_ref[...] = dest
        names = jnp.where(mine, (local + 1).astype(F32), 0.0).astype(BF)
        places = (iota((LANES, rows), 0) == code).astype(F32).astype(BF)
        meta = lax.dot_general(
            names, places, (((1,), (1,)), ((), ())), preferred_element_type=F32
        )
        meta_ref[...] = jnp.where(iota((owners, LANES), 1) == LANES - 1, lost, meta)

        def one_chunk(index, carry):
            at = pl.ds(pl.multiple_of(index * LANES, LANES), LANES)
            values = rows_ref[at, :].astype(F32)
            squares = jnp.sum(values * values, axis=1, keepdims=True)
            unit_ref[at, :] = (values * lax.rsqrt(squares + 1e-06)).astype(BF)
            return carry

        lax.fori_loop(0, rows // LANES, one_chunk, 0)
        choose = (iota((SPILL, rows), 0) + owners * FAST == dest).astype(F32).astype(BF)
        spill_ref[...] = jnp.dot(choose, unit_ref[...], preferred_element_type=F32).astype(BF)

    choose = (iota((STEP, rows), 0) + step * STEP == dest_ref[...]).astype(F32).astype(BF)
    packed = jnp.dot(choose, unit_ref[...], preferred_element_type=F32)
    blocks_ref[...] = packed.astype(BF)
    per_step = STEP // FAST
    for block in range(per_step):
        end = (block + 1) * FAST
        meta = meta_ref[pl.ds(step * per_step + block, 1), :]
        tail = packed[end - 16 : end, :LANES]
        blocks_ref[end - 16 : end, :LANES] = jnp.where(
            iota((16, LANES), 0) == 15, meta, tail
        ).astype(BF)


def pack(embeddings, cluster_id, valid, owners):
    rows, width = embeddings.shape
    return pl.pallas_call(
        functools.partial(pack_kernel, owners),
        grid=(owners * FAST // STEP,),
        out_shape=(
            jax.ShapeDtypeStruct((owners * FAST, width), BF),
            jax.ShapeDtypeStruct((SPILL, width), BF),
            jax.ShapeDtypeStruct((1, rows), jnp.int32),
        ),
        in_specs=[
            pl.BlockSpec((1, rows), lambda i: (0, 0)),
            pl.BlockSpec((1, rows), lambda i: (0, 0)),
            pl.BlockSpec((rows, width), lambda i: (0, 0)),
        ],
        out_specs=(
            pl.BlockSpec((STEP, width), lambda i: (i, 0)),
            pl.BlockSpec((SPILL, width), lambda i: (0, 0)),
            pl.BlockSpec((1, rows), lambda i: (0, 0)),
        ),
        scratch_shapes=[
            pltpu.VMEM((rows, width), BF),
            pltpu.VMEM((1, rows), jnp.int32),
            pltpu.VMEM((owners, LANES), F32),
        ],
        compiler_params=pltpu.CompilerParams(vmem_limit_bytes=VMEM),
        name="pack",
    )(cluster_id.reshape(1, rows), valid.reshape(1, rows), embeddings)


def score_kernel(
    owners, got_ref, extra_ref, best_ref, lost_ref, all_ref, side_ref, top_ref, line_ref, sems
):
    step = pl.program_id(0)
    slots = owners * FAST
    total = all_ref.shape[0]

    @pl.when(step == 0)
    def _():
        first = pltpu.make_async_copy(got_ref, all_ref.at[pl.ds(0, slots)], sems.at[0])
        second = pltpu.make_async_copy(
            extra_ref, all_ref.at[pl.ds(slots, owners * SPILL)], sems.at[1]
        )
        first.start()
        second.start()
        first.wait()
        second.wait()
        last = iota((owners, 1), 0) * FAST + (FAST - 1)
        pick = (iota((owners, slots), 1) == last).astype(F32).astype(BF)
        names = jnp.dot(pick, all_ref[pl.ds(0, slots), pl.ds(0, LANES)], preferred_element_type=F32)
        lost_ref[0, 0] = jnp.max(
            jnp.where(iota((owners, LANES), 1) == LANES - 1, names, 0.0)
        ).astype(jnp.int32)
        names = names.astype(BF)
        ones = jnp.ones((LANES, LANES), BF)
        for start, size, first_lane in ((0, FAST, 0), (slots, SPILL, FAST)):
            count = owners * size
            base = iota((count, 1), 0)
            source = base // size
            lane = first_lane + base - source * size
            of_source = (iota((count, owners), 1) == source).astype(F32).astype(BF)
            spread = jnp.dot(of_source, names, preferred_element_type=F32)
            spread = jnp.where(iota((count, LANES), 1) == lane, spread, 0.0).astype(BF)
            side = jnp.dot(spread, ones, preferred_element_type=F32)
            side_ref[pl.ds(start, count), :] = jnp.where(side == 0.0, -1.0, side)
            base = iota((1, count), 1)
            source = base // size
            lane = first_lane + base - source * size
            at_lane = (iota((LANES, count), 0) == lane).astype(F32).astype(BF)
            spread = jnp.dot(names, at_lane, preferred_element_type=F32)
            spread = jnp.where(iota((owners, count), 0) == source, spread, 0.0)
            top_ref[:, pl.ds(start, count)] = jnp.sum(spread, axis=0, keepdims=True)

    here = pl.ds(pl.multiple_of(step * STEP, STEP), STEP)
    right = all_ref[here, :]
    top = top_ref[:, here]
    apart = iota((STEP, STEP), 0) - iota((STEP, STEP), 1)
    result = jnp.full((1, STEP), -1.0, F32)
    for block in range(total // STEP):
        at = slice(block * STEP, (block + 1) * STEP)
        scores = lax.dot_general(
            all_ref[at, :], right, (((1,), (1,)), ((), ())), preferred_element_type=F32
        )
        side = jnp.concatenate([side_ref[at, :]] * (STEP // LANES), axis=1)
        allowed = (side == top) & (apart != (step - block) * STEP)
        masked = jnp.where(allowed, scores, -1.0)
        result = jnp.maximum(result, jnp.max(masked, axis=0, keepdims=True))
    line_ref[:, here] = result

    @pl.when(step == pl.num_programs(0) - 1)
    def _():
        lanes = iota((1, LANES), 1)
        for source in range(owners):
            row, shift = divmod(source * FAST, LANES)
            main = pltpu.roll(line_ref[:, row * LANES : (row + 1) * LANES], (LANES - shift) % LANES, 1)
            row, shift = divmod(slots + source * SPILL, LANES)
            extra = pltpu.roll(
                line_ref[:, row * LANES : (row + 1) * LANES], (LANES + FAST - shift) % LANES, 1
            )
            best_ref[source] = jnp.where(lanes < FAST, main, extra)


def score(got, extra, owners):
    width = got.shape[1]
    total = owners * (FAST + SPILL)
    return pl.pallas_call(
        functools.partial(score_kernel, owners),
        grid=(total // STEP,),
        out_shape=(
            jax.ShapeDtypeStruct((owners, 1, LANES), F32),
            jax.ShapeDtypeStruct((1, 1), jnp.int32),
        ),
        in_specs=[pl.BlockSpec(memory_space=pl.ANY), pl.BlockSpec(memory_space=pl.ANY)],
        out_specs=(
            pl.BlockSpec((owners, 1, LANES), lambda i: (0, 0, 0)),
            pl.BlockSpec(memory_space=pltpu.SMEM),
        ),
        scratch_shapes=[
            pltpu.VMEM((total, width), BF),
            pltpu.VMEM((total, LANES), F32),
            pltpu.VMEM((1, total), F32),
            pltpu.VMEM((1, total), F32),
            pltpu.SemaphoreType.DMA((2,)),
        ],
        compiler_params=pltpu.CompilerParams(vmem_limit_bytes=VMEM),
        name="score",
    )(got, extra)


def place_kernel(owners, back_ref, cid_ref, code_ref, valid_ref, out_ref):
    for start in range(0, cid_ref.shape[0], 8):
        at = slice(start, start + 8)
        owner = lax.shift_right_logical(cid_ref[at, :], 3)
        code = code_ref[at, :]
        result = jnp.zeros((8, LANES), F32)
        for source in range(owners):
            line = jnp.broadcast_to(back_ref[source], (8, LANES))
            value = jnp.take_along_axis(line, code, axis=1, mode="promise_in_bounds")
            result = jnp.where(owner == source, value, result)
        out_ref[at, :] = jnp.where(valid_ref[at, :] == 1, result, 0.0)


def place(back, cluster_id, code, valid, owners):
    rows = cluster_id.shape[0]
    shape = (rows // LANES, LANES)
    return pl.pallas_call(
        functools.partial(place_kernel, owners),
        out_shape=jax.ShapeDtypeStruct(shape, F32),
        name="place",
    )(back, cluster_id.reshape(shape), code.reshape(shape), valid.reshape(shape)).reshape(rows)


def every_slot(embeddings, cluster_id, valid, owners):
    width = embeddings.shape[1]
    clusters = CL_DEV * owners
    values = embeddings.astype(F32)
    squares = jnp.sum(values * values, axis=1, keepdims=True)
    unit_rows = (values * lax.rsqrt(squares + 1e-06)).astype(BF)
    one_hot = (cluster_id[:, None] == jnp.arange(clusters, dtype=jnp.int32)[None, :]).astype(jnp.int32)
    ranking = jnp.sum(jnp.cumsum(one_hot, axis=0) * one_hot, axis=1) - 1
    target = cluster_id * SLOT + ranking
    outgoing = jnp.zeros((clusters * SLOT, width), BF).at[target].set(unit_rows)
    live_out = jnp.zeros((clusters * SLOT,), BF).at[target].set(valid.astype(BF))
    got = lax.all_to_all(
        outgoing.reshape(owners, CL_DEV * SLOT, width), "owners", split_axis=0, concat_axis=0, tiled=True
    )
    live = lax.all_to_all(
        live_out.reshape(owners, CL_DEV, SLOT), "owners", split_axis=0, concat_axis=0, tiled=True
    )
    got = got.reshape(owners, CL_DEV, SLOT, width).transpose(1, 0, 2, 3)
    got = got.reshape(CL_DEV, owners * SLOT, width)
    live = live.transpose(1, 0, 2).reshape(CL_DEV, owners * SLOT) > 0.5
    diagonal = jnp.eye(owners * SLOT, dtype=bool)

    def one_cluster(args):
        rows, flags = args
        scores = jnp.einsum("md,nd->mn", rows, rows, preferred_element_type=F32)
        allowed = flags[:, None] & flags[None, :] & ~diagonal
        return jnp.max(jnp.where(allowed, scores, -1.0), axis=1)

    best = lax.map(one_cluster, (got, live)).reshape(CL_DEV, owners, SLOT).transpose(1, 0, 2)
    back = lax.all_to_all(best, "owners", split_axis=0, concat_axis=0, tiled=True)
    return jnp.where(valid == 1, back.reshape(-1)[target], 0.0)


def shards(embeddings, cluster_id, valid):
    owners = lax.axis_size("owners")
    width = embeddings.shape[1]
    blocks, spill, code = pack(embeddings, cluster_id, valid, owners)
    extra = lax.all_gather(spill, "owners", axis=0, tiled=True)
    got = lax.all_to_all(
        blocks.reshape(owners, FAST, width), "owners", split_axis=0, concat_axis=0, tiled=True
    )
    best, lost = score(got.reshape(owners * FAST, width), extra, owners)
    back = lax.all_to_all(best, "owners", split_axis=0, concat_axis=0, tiled=True)
    nearest = place(back, cluster_id, code, valid, owners)
    return lax.cond(
        lost[0, 0] > 0,
        lambda: every_slot(embeddings, cluster_id, valid, owners),
        lambda: nearest,
    )


def solution(mesh):
    placed = (P(("groups", "owners"), None), P(("groups", "owners")), P(("groups", "owners")))
    return jax.shard_map(
        shards, mesh=mesh, in_specs=placed, out_specs=P(("groups", "owners")), check_vma=False
    )
```

time: 156 us -> 111 us (0.71)
  blocking collectives: 25.8 us -> 0 us
  local copies, waits for them, and re-layouts: 24 us -> 4.34 us
  Pallas kernels: 0 us -> 16.4 us
  between operations: 0.19 us -> 14.1 us
  waiting for transfers between devices: 77.5 us -> 64.1 us
  other arithmetic: 12.8 us -> 0 us
  starting transfers between devices: 13.4 us -> 11.2 us
  matrix products: 1.82 us -> 0 us
    all_to_all x2, waiting for transfers between devices: 77.5 us -> 5.76 us  [the longest x1 5.76 us: shards(): lax.all_to_all(best, 'owners', split_axis=0, concat_axis=0, tiled=True)]
    all_gather x0 -> x1, waiting for transfers between devices: none -> 57.6 us  [shards(): extra = lax.all_gather(spill, 'owners', axis=0, tiled=True)]
    all_to_all x1 -> x0, blocking collectives: 25.8 us -> none  [shards(): lax.all_to_all(best.reshape(items, owners, SLOT), 'owners', split_axis=1,...]
    pallas_call x0 -> x3, Pallas kernels: none -> 16.4 us  [the longest x1 8.49 us: score(): pl.pallas_call(functools.partial(score_kernel, owners), grid=(total // ST...]
    scatter x1 -> x0, other arithmetic: 8.33 us -> none  [shards(): outgoing = jnp.zeros((slots_all, width), jnp.bfloat16).at[target].set(uni...]
    scatter x1 -> x0, local copies, waits for them, and re-layouts: 7.58 us -> none  [shards(): live_out = jnp.zeros((slots_all,), jnp.bfloat16).at[target].set(valid.ast...]
    gather x1 -> x0, local copies, waits for them, and re-layouts: 6.15 us -> none  [shards(): nearest = returned.reshape(-1)[target]]
    reshape x4 -> x0, local copies, waits for them, and re-layouts: 5.73 us -> none  [the longest x1 4.95 us: shards(): outgoing = jnp.zeros((slots_all, width), jnp.bfloat16).at[target].set(uni...]
  transfers between devices with their start and end apart: 2 -> 3, of which waited for: 1 -> 2; matrix products, arithmetic and copies ran while one was open for 9% -> 0% of each run, Pallas kernels for 0% -> 0%
where the time goes in v1:
time: 111 us; the launch traced here: 110 us
  waiting for transfers between devices  64.1 us (58%)
  Pallas kernels  16.4 us (15%)
  between operations  14.1 us (13%)
  starting transfers between devices  11.2 us (10%)
  local copies, waits for them, and re-layouts  4.34 us (4%)
    all_gather x1, waiting for transfers between devices, shards(): extra = lax.all_gather(spill, 'owners', axis=0, tiled=True)  57.6 us
    pallas_call x1, Pallas kernels, score(): pl.pallas_call(functools.partial(score_kernel, owners), grid=(total // ST...  8.49 us
    all_to_all x1, starting transfers between devices, shards(): lax.all_to_all(blocks.reshape(owners, FAST, width), 'owners', split_axis=...  7.51 us
    pallas_call x1, Pallas kernels, pack(): pl.pallas_call(functools.partial(pack_kernel, owners), grid=(owners * FAS...  7.11 us
    all_to_all x1, waiting for transfers between devices, shards(): lax.all_to_all(best, 'owners', split_axis=0, concat_axis=0, tiled=True)  5.76 us
    unnamed x14, local copies, waits for them, and re-layouts  4.34 us
    all_to_all x1, starting transfers between devices, shards(): lax.all_to_all(best, 'owners', split_axis=0, concat_axis=0, tiled=True)  3.67 us
  transfers between devices with their start and end apart: 3, of which 2 were waited for; matrix products, arithmetic and copies ran while one was open for 0% of the time, Pallas kernels for 0%

profile of v1, /device:TPU:0, one launch (start us, length us, event | category | flops | bytes accessed | tf_op | source)
XLA Modules:
  0.0 110.3 jit_solution(11992436951415221088)
XLA Ops:
  6.5 7.1 %pack.1 = (bf16[1024,1024]{1,0:T(8,128)(2,1)S(1)}, bf16[32,1024]{1,0:T(8,128)(2,1)}, s32[1,1024]{1,0:T(1,128)S(1)}) custom-call(s32[1,1024]{1,0:T(1,128)} %bitcast.42, s32[1,1024]{1,0:T(1,128)} %bitcast.45, bf16[1024,1024]{1,0:T(8,128)(2,1)} %rows_ref.1), custom_call_target="tpu_custom_call" | custom-call | tf_op jit(solution)/shard_map/pack/pallas_call | solution.py:103
  13.7 0.0 copy-start
  13.7 1.3 %copy-done = bf16[1024,1024]{1,0:T(8,128)(2,1)} copy-done((bf16[1024,1024]{1,0:T(8,128)(2,1)}, bf16[1024,1024]{1,0:T(8,128)(2,1)S(1)}, u32[]{:S(2)}) %copy-start) | copy-done | bytes 2097176
  15.0 0.0 copy-start.2
  15.0 0.6 copy-done.2
  15.6 0.0 copy-start.4
  15.6 0.0 copy-start.5
  15.6 7.5 %all-to-all-start.3 = ((bf16[16,64,1024]{2,1,0:T(8,128)(2,1)}), bf16[16,64,1024]{2,1,0:T(8,128)(2,1)S(1)}, u32[]{:S(2)}, u32[]{:S(2)}) async-start(bf16[16,64,1024]{2,1,0:T(8,128)(2,1)} %bitcast.37), calls=%async_computation.3 | async-start | bytes 4194304 | tf_op jit(solution)/shard_map/all_to_all | solution.py:291
  23.1 0.0 all-gather.2.cloned.1.call-start
  23.2 0.7 all-gather.2.cloned.1.call-update
  23.8 57.6 %all-gather.2.cloned.1.call-done.extra_ref = bf16[512,1024]{1,0:T(8,128)(2,1)} async-done(((bf16[32,1024]{1,0:T(8,128)(2,1)}), bf16[512,1024]{1,0:T(8,128)(2,1)}) %all-gather.2.cloned.1.call-update) | async-done | bytes 1048592 | tf_op jit(solution)/shard_map/all_gather | solution.py:290
  81.5 0.0 all-to-all-done.3
  81.5 0.0 copy-start.1
  81.5 1.2 %copy-done.1 = bf16[512,1024]{1,0:T(8,128)(2,1)S(1)} copy-done((bf16[512,1024]{1,0:T(8,128)(2,1)S(1)}, bf16[512,1024]{1,0:T(8,128)(2,1)}, u32[]{:S(2)}) %copy-start.1) | copy-done | bytes 1048600
  82.7 8.5 %score.1 = (f32[16,1,128]{2,1,0:T(1,128)}, s32[1,1]{1,0:T(1,128)}) custom-call(bf16[1024,1024]{1,0:T(8,128)(2,1)S(1)} %bitcast.36, bf16[512,1024]{1,0:T(8,128)(2,1)S(1)} %copy-done.1), custom_call_target="tpu_custom_call" | custom-call | tf_op jit(solution)/shard_map/score/pallas_call | solution.py:206
  91.2 3.7 %all-to-all-start.4 = ((f32[16,1,128]{2,1,0:T(1,128)}), f32[16,1,128]{2,1,0:T(1,128)S(1)}, u32[]{:S(2)}, u32[]{:S(2)}) async-start(f32[16,1,128]{2,1,0:T(1,128)} %get-tuple-element.89), calls=%async_computation.4 | async-start | bytes 16384 | tf_op jit(solution)/shard_map/all_to_all | solution.py:295
  95.5 5.8 %all-to-all-done.4.back_ref = f32[16,1,128]{2,1,0:T(1,128)S(1)} async-done(((f32[16,1,128]{2,1,0:T(1,128)}), f32[16,1,128]{2,1,0:T(1,128)S(1)}, u32[]{:S(2)}, u32[]{:S(2)}) %all-to-all-start.4) | async-done | bytes 8224 | tf_op jit(solution)/shard_map/all_to_all | solution.py:295
  101.3 0.0 copy-start.6
  101.3 0.6 copy-done.6
  101.9 0.0 copy-done.4
  101.9 0.0 copy-done.5
  101.9 0.8 place.1
  102.7 0.2 conditional.1
  102.9 0.0 copy-start.7
  102.9 0.6 copy-done.7
Async XLA Ops:
  13.7 1.3 %copy-start = (bf16[1024,1024]{1,0:T(8,128)(2,1)}, bf16[1024,1024]{1,0:T(8,128)(2,1)S(1)}, u32[]{:S(2)}) copy-start(bf16[1024,1024]{1,0:T(8,128)(2,1)S(1)} %get-tuple-element.86) | copy-start | bytes 6291460
  15.0 0.6 copy-start.2
  15.6 86.3 %copy-start.4 = (s32[1024]{0:T(1024)S(1)}, s32[1024]{0:T(1024)}, u32[]{:S(2)}) copy-start(s32[1024]{0:T(1024)} %param.8) | copy-start | bytes 12292
  15.6 86.3 %copy-start.5 = (s32[1024]{0:T(1024)S(1)}, s32[1024]{0:T(1024)}, u32[]{:S(2)}) copy-start(s32[1024]{0:T(1024)} %param.9) | copy-start | bytes 12292
  15.6 65.9 %all-to-all-start.3 = ((bf16[16,64,1024]{2,1,0:T(8,128)(2,1)}), bf16[16,64,1024]{2,1,0:T(8,128)(2,1)S(1)}, u32[]{:S(2)}, u32[]{:S(2)}) async-start(bf16[16,64,1024]{2,1,0:T(8,128)(2,1)} %bitcast.37), calls=%async_computation.3 | async-start | bytes 4194304 | tf_op jit(solution)/shard_map/all_to_all | solution.py:291
  23.1 58.4 %all-gather.2.cloned.1.call-start = ((), (), s32[]{:S(2)}) async-start(), calls=%async_computation.5 | async-start | bytes 1114112 | tf_op jit(solution)/shard_map/all_gather | solution.py:290
  81.5 1.2 %copy-start.1 = (bf16[512,1024]{1,0:T(8,128)(2,1)S(1)}, bf16[512,1024]{1,0:T(8,128)(2,1)}, u32[]{:S(2)}) copy-start(bf16[512,1024]{1,0:T(8,128)(2,1)} %all-gather.2.cloned.1.call-done.extra_ref) | copy-start | bytes 3145732
  91.2 10.1 %all-to-all-start.4 = ((f32[16,1,128]{2,1,0:T(1,128)}), f32[16,1,128]{2,1,0:T(1,128)S(1)}, u32[]{:S(2)}, u32[]{:S(2)}) async-start(f32[16,1,128]{2,1,0:T(1,128)} %get-tuple-element.89), calls=%async_computation.4 | async-start | bytes 16384 | tf_op jit(solution)/shard_map/all_to_all | solution.py:295
  101.3 0.6 copy-start.6
  102.9 0.6 copy-start.7
Sparse Core Ops, SparseCore 0:
  26.1 55.3 all-gather.1

commit v2 on v1

v2 whole, which is shorter than its diff:
```python
import functools

import jax
import jax.numpy as jnp
from jax import lax
from jax.experimental import pallas as pl
from jax.experimental.pallas import tpu as pltpu
from jax.sharding import PartitionSpec as P

CL_DEV = 8
SLOT = 16
LANES = 128
FAST = 64
SPILL = 32
KEPT = 8
TILE = 1024
STEP = 256
SPAN = 384
VMEM = 48 * 1024 * 1024
BF = jnp.bfloat16
F32 = jnp.float32


def iota(shape, dim):
    return lax.broadcasted_iota(jnp.int32, shape, dim)


def bits(mask):
    return mask.astype(F32).astype(BF)


def product(left, right):
    return jnp.dot(left, right, preferred_element_type=F32)


def product_t(left, right):
    return lax.dot_general(left, right, (((1,), (1,)), ((), ())), preferred_element_type=F32)


def before():
    return bits(iota((LANES, LANES), 0) < iota((LANES, LANES), 1))


def running(flags):
    inside = product(flags, before())
    whole = product(flags, jnp.ones((LANES, LANES), BF))
    rows = flags.shape[0]
    offset = jnp.zeros((1, LANES), F32)
    offsets = []
    for row in range(rows):
        offsets.append(offset)
        offset = offset + whole[row : row + 1]
    return inside + jnp.concatenate(offsets, axis=0)


def pack_kernel(
    owners, cid_ref, valid_ref, rows_ref, blocks_ref, spill_ref, code_ref, held, unit, choose, out, in_sems, out_sems
):
    rows, width = held.shape
    lines = rows // LANES
    parts = rows // STEP
    slots = owners * FAST
    tile = min(slots, TILE)
    loads = []
    for part in range(parts):
        at = pl.ds(part * STEP, STEP)
        loads.append(pltpu.make_async_copy(rows_ref.at[at], held.at[at], in_sems.at[part]))
        loads[-1].start()

    cid = cid_ref[...]
    live = valid_ref[...] == 1
    owner = lax.shift_right_logical(cid, 3)
    name = (cid & (CL_DEV - 1)) + 1
    target = jnp.where(live, owner, -1)
    index = iota((owners, LANES), 0)
    mine = [(index == target[line : line + 1]).astype(F32) for line in range(lines)]
    stacked = jnp.concatenate(mine, axis=0).astype(BF)
    inside = product(stacked, before())
    whole = product(stacked, jnp.ones((LANES, LANES), BF))
    offset = jnp.zeros((owners, LANES), F32)
    ranks = []
    for line in range(lines):
        at = slice(line * owners, (line + 1) * owners)
        ranks.append(jnp.sum(mine[line] * (inside[at] + offset), axis=0, keepdims=True))
        offset = offset + whole[at]
    pos = jnp.concatenate(ranks, axis=0).astype(jnp.int32)
    fits = live & (pos < FAST - 1)
    over = live & (pos >= FAST - 1)
    spot = running(bits(over)).astype(jnp.int32)
    spilled = over & (spot < SPILL)
    lost = jnp.max((over & (spot >= SPILL)).astype(F32))
    code = jnp.where(fits, pos, jnp.where(spilled, FAST + spot, LANES - 1))
    code_ref[...] = code
    slot = owner * FAST + pos
    slot = jnp.where(slot < tile, slot, slot + SPILL)
    dest = jnp.where(fits, slot, jnp.where(spilled, tile + spot, -1))

    names = jnp.concatenate(
        [mine[line] * name[line : line + 1].astype(F32) for line in range(lines)], axis=1
    ).astype(BF)
    index = iota((LANES, LANES), 0)
    places = jnp.concatenate([bits(index == code[line : line + 1]) for line in range(lines)], axis=1)
    meta = product_t(names, places)
    lane = iota((owners, LANES), 1)
    spills = jnp.where((lane >= FAST) & (lane < FAST + SPILL) & (meta > 0.0), 1.0, 0.0)
    if owners < LANES:
        spills = jnp.concatenate([spills, jnp.zeros((LANES - owners, LANES), F32)], axis=0)
    counts = product_t(jnp.ones((8, LANES), BF), spills.astype(BF))[0:1]
    meta = jnp.where(lane == LANES - 1, lost, meta)
    meta = jnp.concatenate([meta, jnp.broadcast_to(counts, (owners, LANES))], axis=1).astype(BF)

    def fill(begin, count):
        index = iota((count, LANES), 0) + begin
        for line in range(lines):
            at = slice(line * LANES, (line + 1) * LANES)
            choose[:count, at] = bits(index == dest[line : line + 1])

    fill(0, tile + SPILL)
    for part in range(parts):
        loads[part].wait()

        def one_chunk(number, carry):
            at = pl.ds(pl.multiple_of(part * STEP + number * 64, 64), 64)
            values = held[at, :].astype(F32)
            squares = jnp.sum(values * values, axis=1, keepdims=True)
            unit[at, :] = (values * lax.rsqrt(squares + 1e-06)).astype(BF)
            return carry

        lax.fori_loop(0, STEP // 64, one_chunk, 0)

    stores = []
    for first in range(0, slots, tile):
        count = tile
        base = first + SPILL
        if first == 0:
            count = tile + SPILL
            base = 0
        else:
            fill(base, count)
        for column in range(0, width, STEP):
            at = slice(column, column + STEP)
            packed = product(choose[:count, :], unit[:, at])
            if column == 0:
                line = iota((count, owners), 0) + first
                line = jnp.where(line < first + tile, line, -1)
                last = iota((count, owners), 1) * FAST + (FAST - 1)
                packed = packed + product(bits(line == last), meta)
            out[pl.ds(base, count), at] = packed.astype(BF)
            moves = [(out.at[pl.ds(base, tile), at], blocks_ref.at[pl.ds(first, tile), at])]
            if first == 0:
                moves.append((out.at[pl.ds(tile, SPILL), at], spill_ref.at[:, at]))
            for source, sink in moves:
                stores.append(pltpu.make_async_copy(source, sink, out_sems.at[len(stores)]))
                stores[-1].start()
    for store in stores:
        store.wait()


def pack(embeddings, cluster_id, valid, owners):
    rows, width = embeddings.shape
    slots = owners * FAST
    tile = min(slots, TILE)
    lines = (rows // LANES, LANES)
    return pl.pallas_call(
        functools.partial(pack_kernel, owners),
        out_shape=(
            pltpu.HBM((slots, width), BF),
            pltpu.HBM((SPILL, width), BF),
            jax.ShapeDtypeStruct(lines, jnp.int32),
        ),
        in_specs=[
            pl.BlockSpec(memory_space=pltpu.VMEM),
            pl.BlockSpec(memory_space=pltpu.VMEM),
            pl.BlockSpec(memory_space=pltpu.HBM),
        ],
        out_specs=(
            pl.BlockSpec(memory_space=pltpu.HBM),
            pl.BlockSpec(memory_space=pltpu.HBM),
            pl.BlockSpec(memory_space=pltpu.VMEM),
        ),
        scratch_shapes=[
            pltpu.VMEM((rows, width), BF),
            pltpu.VMEM((rows, width), BF),
            pltpu.VMEM((tile + SPILL, rows), BF),
            pltpu.VMEM((slots + SPILL, width), BF),
            pltpu.SemaphoreType.DMA((rows // STEP,)),
            pltpu.SemaphoreType.DMA(((slots // tile + 1) * (width // STEP),)),
        ],
        compiler_params=pltpu.CompilerParams(vmem_limit_bytes=VMEM),
        name="pack",
    )(cluster_id.reshape(lines), valid.reshape(lines), embeddings)


def spread(spill, owners):
    bit = owners // 2
    while bit:
        other = lax.ppermute(spill, "owners", [(i, i ^ bit) for i in range(owners)])
        spill = jnp.concatenate([spill, other], axis=0)
        bit //= 2
    return spill


def spread_source(place, owners, me):
    source = jnp.zeros_like(place)
    width = owners.bit_length() - 1
    for bit in range(width):
        source = source + lax.shift_left(lax.shift_right_logical(place, bit) & 1, width - 1 - bit)
    return source ^ me


def score_kernel(owners, got_ref, extra_ref, best_ref, lost_ref, tags, rows, extra, side, top, line, sems):
    slots = owners * FAST
    total, width = rows.shape
    kept = total - slots
    spills = owners * SPILL
    me = lax.axis_index("owners")
    tag_copy = pltpu.make_async_copy(
        got_ref.at[:, pl.ds(FAST - 16, 16), pl.ds(0, 2 * LANES)], tags, sems.at[0]
    )
    tag_copy.start()
    extra_copy = pltpu.make_async_copy(extra_ref, extra, sems.at[1])
    extra_copy.start()
    moves = []
    for source in range(owners):
        moves.append(
            pltpu.make_async_copy(
                got_ref.at[source], rows.at[pl.ds(source * FAST, FAST)], sems.at[2 + source]
            )
        )
        moves[-1].start()
    tag_copy.wait()
    flat = tags[...].reshape(owners * 16, 2 * LANES)
    pick = bits(iota((owners, owners * 16), 1) == iota((owners, owners * 16), 0) * 16 + 15)
    picked = product(pick, flat)
    names, counts = picked[:, :LANES], picked[:, LANES:]
    lane = iota((owners, LANES), 1)
    lost = jnp.max(jnp.where(lane == LANES - 1, names, 0.0))
    crowded = jnp.max(jnp.sum(counts, axis=0, keepdims=True)) > kept
    lost_ref[0, 0] = ((lost > 0.0) | crowded).astype(jnp.int32)
    in_spill = (lane >= FAST) & (lane < FAST + SPILL) & (names > 0.0)
    rank = running(bits(in_spill))
    names_b = names.astype(BF)

    def along_rows(count, size, source, first_lane):
        base = iota((count, 1), 0)
        of_source = bits(iota((count, owners), 1) == source)
        wide = product(of_source, names_b)
        here = iota((count, LANES), 1) == first_lane + base % size
        return product(jnp.where(here, wide, 0.0).astype(BF), jnp.ones((LANES, LANES), BF))

    def along_lanes(values, count, size, source, first_lane):
        at_lane = (iota((LANES, count), 0) == first_lane + iota((1, count), 1) % size).astype(F32)
        wide = jnp.dot(values, at_lane, preferred_element_type=F32, precision=lax.Precision.HIGHEST)
        wide = jnp.where(iota((owners, count), 0) == source, wide, 0.0)
        return jnp.sum(wide, axis=0, keepdims=True)

    found = along_rows(slots, FAST, iota((slots, 1), 0) // FAST, 0)
    side[pl.ds(0, slots), :] = jnp.where(found == 0.0, -1.0, found)
    lines_of = iota((1, slots), 1) // FAST
    top[:, pl.ds(0, slots)] = along_lanes(names, slots, FAST, lines_of, 0)

    sources = spread_source(iota((1, spills), 1) // SPILL, owners, me)
    ranks = along_lanes(jnp.where(in_spill, rank + 1.0, 0.0), spills, SPILL, sources, FAST)
    select = bits(iota((kept, spills), 0).astype(F32) + 1.0 == ranks)
    sources = spread_source(iota((spills, 1), 0) // SPILL, owners, me)
    found = along_rows(spills, SPILL, sources, FAST)
    found = product(select, found.astype(BF))
    side[pl.ds(slots, kept), :] = jnp.where(found == 0.0, -1.0, found)
    sources = spread_source(iota((1, spills), 1) // SPILL, owners, me)
    found = along_lanes(names, spills, SPILL, sources, FAST)
    found = product_t(jnp.broadcast_to(found, (8, spills)).astype(BF), select)
    top[:, pl.ds(slots, kept)] = found[0:1]
    extra_copy.wait()
    rows[pl.ds(slots, kept), :] = product(select, extra[...]).astype(BF)
    for move in moves:
        move.wait()

    unlike = iota((LANES, LANES), 0) != iota((LANES, LANES), 1)

    def columns(first, square):
        here = pl.ds(first, SPAN)
        scores = product_t(rows[...], rows[here, :])
        tops = top[:, here]
        result = [jnp.full((1, LANES), -1.0, F32)] * (SPAN // LANES)
        for block in range(total // LANES):
            at = slice(block * LANES, (block + 1) * LANES)
            for part in range(SPAN // LANES):
                lanes = slice(part * LANES, (part + 1) * LANES)
                allowed = side[at, :] == tops[:, lanes]
                diagonal = square(block, part)
                if diagonal is not None:
                    allowed = allowed & (unlike | diagonal)
                masked = jnp.where(allowed, scores[at, lanes], -1.0)
                result[part] = jnp.maximum(result[part], jnp.max(masked, axis=0, keepdims=True))
        line[:, here] = jnp.concatenate(result, axis=1)

    if total // SPAN <= 4:
        for number in range(total // SPAN):
            columns(
                number * SPAN,
                lambda block, part: False if block == number * (SPAN // LANES) + part else None,
            )
    else:

        @pl.loop(0, total // SPAN)
        def _(number):
            columns(
                pl.multiple_of(number * SPAN, SPAN),
                lambda block, part: block != number * (SPAN // LANES) + part,
            )

    back = [jnp.full((8, LANES), -1.0, F32)] * (owners // 8)
    for piece in range(kept // LANES):
        lines = line[:, slots + piece * LANES : slots + (piece + 1) * LANES]
        lines = jnp.broadcast_to(lines, (8, LANES))
        where = rank.astype(jnp.int32) - piece * LANES
        inside = (where >= 0) & (where < LANES)
        where = jnp.where(inside, where, 0)
        for number in range(owners // 8):
            at = slice(number * 8, number * 8 + 8)
            value = jnp.take_along_axis(lines, where[at], axis=1, mode="promise_in_bounds")
            back[number] = jnp.where(inside[at], value, back[number])
    back = jnp.concatenate(back, axis=0)
    lanes = iota((1, LANES), 1)
    for source in range(owners):
        row, shift = divmod(source * FAST, LANES)
        main = line[:, row * LANES : (row + 1) * LANES]
        if shift:
            main = pltpu.roll(main, LANES - shift, 1)
        best_ref[source] = jnp.where(lanes < FAST, main, back[source : source + 1])


def score(got, extra, owners):
    width = got.shape[2]
    total = owners * FAST + owners * KEPT
    return pl.pallas_call(
        functools.partial(score_kernel, owners),
        out_shape=(
            jax.ShapeDtypeStruct((owners, 1, LANES), F32),
            jax.ShapeDtypeStruct((1, 1), jnp.int32),
        ),
        in_specs=[pl.BlockSpec(memory_space=pltpu.HBM), pl.BlockSpec(memory_space=pltpu.HBM)],
        out_specs=(
            pl.BlockSpec(memory_space=pltpu.VMEM),
            pl.BlockSpec(memory_space=pltpu.SMEM),
        ),
        scratch_shapes=[
            pltpu.VMEM((owners, 16, 2 * LANES), BF),
            pltpu.VMEM((total, width), BF),
            pltpu.VMEM((owners * SPILL, width), BF),
            pltpu.VMEM((total, LANES), F32),
            pltpu.VMEM((1, total), F32),
            pltpu.VMEM((1, total), F32),
            pltpu.SemaphoreType.DMA((2 + owners,)),
        ],
        compiler_params=pltpu.CompilerParams(vmem_limit_bytes=VMEM),
        name="score",
    )(got, extra)


def place_kernel(owners, back_ref, cid_ref, code_ref, valid_ref, out_ref):
    for start in range(0, cid_ref.shape[0], 8):
        at = slice(start, start + 8)
        owner = lax.shift_right_logical(cid_ref[at, :], 3)
        code = code_ref[at, :]
        result = jnp.zeros((8, LANES), F32)
        for source in range(owners):
            line = jnp.broadcast_to(back_ref[source], (8, LANES))
            value = jnp.take_along_axis(line, code, axis=1, mode="promise_in_bounds")
            result = jnp.where(owner == source, value, result)
        out_ref[at, :] = jnp.where(valid_ref[at, :] == 1, result, 0.0)


def place(back, cluster_id, code, valid, owners):
    rows = cluster_id.shape[0]
    shape = (rows // LANES, LANES)
    return pl.pallas_call(
        functools.partial(place_kernel, owners),
        out_shape=jax.ShapeDtypeStruct(shape, F32),
        name="place",
    )(back, cluster_id.reshape(shape), code, valid.reshape(shape)).reshape(rows)


def every_slot(embeddings, cluster_id, valid, owners):
    width = embeddings.shape[1]
    clusters = CL_DEV * owners
    values = embeddings.astype(F32)
    squares = jnp.sum(values * values, axis=1, keepdims=True)
    unit_rows = (values * lax.rsqrt(squares + 1e-06)).astype(BF)
    one_hot = (cluster_id[:, None] == jnp.arange(clusters, dtype=jnp.int32)[None, :]).astype(jnp.int32)
    ranking = jnp.sum(jnp.cumsum(one_hot, axis=0) * one_hot, axis=1) - 1
    target = cluster_id * SLOT + ranking
    outgoing = jnp.zeros((clusters * SLOT, width), BF).at[target].set(unit_rows)
    live_out = jnp.zeros((clusters * SLOT,), BF).at[target].set(valid.astype(BF))
    got = lax.all_to_all(
        outgoing.reshape(owners, CL_DEV * SLOT, width), "owners", split_axis=0, concat_axis=0, tiled=True
    )
    live = lax.all_to_all(
        live_out.reshape(owners, CL_DEV, SLOT), "owners", split_axis=0, concat_axis=0, tiled=True
    )
    got = got.reshape(owners, CL_DEV, SLOT, width).transpose(1, 0, 2, 3)
    got = got.reshape(CL_DEV, owners * SLOT, width)
    live = live.transpose(1, 0, 2).reshape(CL_DEV, owners * SLOT) > 0.5
    diagonal = jnp.eye(owners * SLOT, dtype=bool)

    def one_cluster(args):
        rows, flags = args
        scores = jnp.einsum("md,nd->mn", rows, rows, preferred_element_type=F32)
        allowed = flags[:, None] & flags[None, :] & ~diagonal
        return jnp.max(jnp.where(allowed, scores, -1.0), axis=1)

    best = lax.map(one_cluster, (got, live)).reshape(CL_DEV, owners, SLOT).transpose(1, 0, 2)
    back = lax.all_to_all(best, "owners", split_axis=0, concat_axis=0, tiled=True)
    return jnp.where(valid == 1, back.reshape(-1)[target], 0.0)


def shards(embeddings, cluster_id, valid):
    owners = lax.axis_size("owners")
    width = embeddings.shape[1]
    blocks, spill, code = pack(embeddings, cluster_id, valid, owners)
    extra = spread(spill, owners)
    got = lax.all_to_all(
        blocks.reshape(owners, FAST, width), "owners", split_axis=0, concat_axis=0, tiled=True
    )
    best, lost = score(got, extra, owners)
    back = lax.all_to_all(best, "owners", split_axis=0, concat_axis=0, tiled=True)
    nearest = place(back, cluster_id, code, valid, owners)
    return lax.cond(
        lost[0, 0] > 0,
        lambda: every_slot(embeddings, cluster_id, valid, owners),
        lambda: nearest,
    )


def solution(mesh):
    placed = (P(("groups", "owners"), None), P(("groups", "owners")), P(("groups", "owners")))
    return jax.shard_map(
        shards, mesh=mesh, in_specs=placed, out_specs=P(("groups", "owners")), check_vma=False
    )
```

time: 111 us -> 104 us (0.937)
  between operations: 14.1 us -> 0.8 us
  starting transfers between devices: 11.2 us -> 15.8 us
  waiting for transfers between devices: 64.1 us -> 67 us
  local copies, waits for them, and re-layouts: 4.34 us -> 1.86 us
  Pallas kernels: 16.4 us -> 18.1 us
    ppermute x0 -> x4, waiting for transfers between devices: none -> 61.2 us  [spread(): other = lax.ppermute(spill, 'owners', [(i, i ^ bit) for i in range(owners)])]
    all_gather x1 -> x0, waiting for transfers between devices: 57.6 us -> none  [shards(): extra = lax.all_gather(spill, 'owners', axis=0, tiled=True)]
    ppermute x0 -> x4, starting transfers between devices: none -> 4.61 us  [spread(): other = lax.ppermute(spill, 'owners', [(i, i ^ bit) for i in range(owners)])]
    unnamed x14 -> x16, local copies, waits for them, and re-layouts: 4.34 us -> 1.82 us
    pallas_call x2, Pallas kernels: 15.6 us -> 17.3 us  [the longest x1 9.12 us: score(): pl.pallas_call(functools.partial(score_kernel, owners), out_shape=(jax.Sh...]
  transfers between devices with their start and end apart: 3 -> 6, of which waited for: 2 -> 5; matrix products, arithmetic and copies ran while one was open for 0% -> 0% of each run, Pallas kernels for 0% -> 0%
where the time goes in v2:
time: 104 us
  waiting for transfers between devices  67 us (64%)
  Pallas kernels  18.1 us (17%)
  starting transfers between devices  15.8 us (15%)
  local copies, waits for them, and re-layouts  1.86 us (2%)
    ppermute x4, waiting for transfers between devices, spread(): other = lax.ppermute(spill, 'owners', [(i, i ^ bit) for i in range(owners)])  61.2 us
    pallas_call x1, Pallas kernels, score(): pl.pallas_call(functools.partial(score_kernel, owners), out_shape=(jax.Sh...  9.12 us
    pallas_call x1, Pallas kernels, pack(): pl.pallas_call(functools.partial(pack_kernel, owners), out_shape=(pltpu.H...  8.19 us
    all_to_all x1, starting transfers between devices, shards(): lax.all_to_all(blocks.reshape(owners, FAST, width), 'owners', split_axis=...  7.52 us
    all_to_all x1, waiting for transfers between devices, shards(): lax.all_to_all(best, 'owners', split_axis=0, concat_axis=0, tiled=True)  5.76 us
    ppermute x4, starting transfers between devices, spread(): other = lax.ppermute(spill, 'owners', [(i, i ^ bit) for i in range(owners)])  4.61 us
    all_to_all x1, starting transfers between devices, shards(): lax.all_to_all(best, 'owners', split_axis=0, concat_axis=0, tiled=True)  3.69 us
  transfers between devices with their start and end apart: 6, of which 5 were waited for; matrix products, arithmetic and copies ran while one was open for 0% of the time, Pallas kernels for 0%

profile of v2, /device:TPU:0, one launch (start us, length us, event | category | flops | bytes accessed | tf_op | source)
XLA Modules:
  0.0 103.9 jit_solution(1679199844977019886)
XLA Ops:
  0.0 8.2 %pack.1 = (bf16[1024,1024]{1,0:T(8,128)(2,1)}, bf16[32,1024]{1,0:T(8,128)(2,1)}, s32[8,128]{1,0:T(8,128)S(1)}) custom-call(s32[8,128]{1,0:T(8,128)} %bitcast.36, s32[8,128]{1,0:T(8,128)} %bitcast.39, bf16[1024,1024]{1,0:T(8,128)(2,1)} %rows_ref.1), custom_call_target="tpu_custom_call" | custom-call | tf_op jit(solution)/shard_map/pack/pallas_call | solution.py:164
  8.2 0.0 copy-start
  8.2 0.6 copy-done
  8.8 0.0 copy-start.2
  8.8 7.5 %all-to-all-start.3 = ((bf16[16,64,1024]{2,1,0:T(8,128)(2,1)}), bf16[16,64,1024]{2,1,0:T(8,128)(2,1)S(1)}, u32[]{:S(2)}, u32[]{:S(2)}) async-start(bf16[16,64,1024]{2,1,0:T(8,128)(2,1)} %bitcast.34), calls=%async_computation.3 | async-start | bytes 4194304 | tf_op jit(solution)/shard_map/all_to_all | solution.py:422
  16.3 0.0 copy-start.3
  16.3 0.0 copy-start.4
  16.4 0.0 copy-done.2
  16.4 2.9 %collective-permute-start = (bf16[32,1024]{1,0:T(8,128)(2,1)S(1)}, bf16[32,1024]{1,0:T(8,128)(2,1)S(1)}, u32[]{:S(2)}, u32[]{:S(2)}) collective-permute-start(bf16[32,1024]{1,0:T(8,128)(2,1)S(1)} %copy-done.2), channel_id=1, source_target_pairs={{0,8},{1,9},{2,10},{3,11},{4,12},{5,13},{6,14},{7,15},{8,0},{9,1},... | collective-permute-start | bytes 196616 | tf_op jit(solution)/shard_map/ppermute | solution.py:197
  19.3 48.9 %collective-permute-done = bf16[32,1024]{1,0:T(8,128)(2,1)S(1)} collective-permute-done((bf16[32,1024]{1,0:T(8,128)(2,1)S(1)}, bf16[32,1024]{1,0:T(8,128)(2,1)S(1)}, u32[]{:S(2)}, u32[]{:S(2)}) %collective-permute-start) | collective-permute-done | bytes 65568 | tf_op jit(solution)/shard_map/ppermute | solution.py:197
  68.2 0.1 collective-permute-start.1
  68.3 5.0 %collective-permute-done.1 = bf16[64,1024]{1,0:T(8,128)(2,1)S(1)} collective-permute-done((bf16[64,1024]{1,0:T(8,128)(2,1)S(1)}, bf16[64,1024]{1,0:T(8,128)(2,1)S(1)}, u32[]{:S(2)}, u32[]{:S(2)}) %collective-permute-start.1) | collective-permute-done | bytes 131104 | tf_op jit(solution)/shard_map/ppermute | solution.py:197
  73.3 1.6 %collective-permute-start.2 = (bf16[128,1024]{1,0:T(8,128)(2,1)S(1)}, bf16[128,1024]{1,0:T(8,128)(2,1)S(1)}, u32[]{:S(2)}, u32[]{:S(2)}) collective-permute-start(bf16[128,1024]{1,0:T(8,128)(2,1)S(1)} %pad_maximum_fusion.1), channel_id=1, source_target_pairs={{0,2},{1,3},{2,0},{3,1},{4,6},{5,7},{6,4},{7,5},{8,10},{9,11},{10,... | collective-permute-start | bytes 786440 | tf_op jit(solution)/shard_map/ppermute | solution.py:197
  74.9 5.4 %collective-permute-done.2 = bf16[128,1024]{1,0:T(8,128)(2,1)S(1)} collective-permute-done((bf16[128,1024]{1,0:T(8,128)(2,1)S(1)}, bf16[128,1024]{1,0:T(8,128)(2,1)S(1)}, u32[]{:S(2)}, u32[]{:S(2)}) %collective-permute-start.2) | collective-permute-done | bytes 262176 | tf_op jit(solution)/shard_map/ppermute | solution.py:197
  80.4 0.1 collective-permute-start.3
  80.5 1.8 %collective-permute-done.3 = bf16[256,1024]{1,0:T(8,128)(2,1)S(1)} collective-permute-done((bf16[256,1024]{1,0:T(8,128)(2,1)S(1)}, bf16[256,1024]{1,0:T(8,128)(2,1)S(1)}, u32[]{:S(2)}, u32[]{:S(2)}) %collective-permute-start.3) | collective-permute-done | bytes 524320 | tf_op jit(solution)/shard_map/ppermute | solution.py:197
  82.4 0.0 all-to-all-done.3.got_ref
  82.4 9.1 %score.1 = (f32[16,1,128]{2,1,0:T(1,128)}, s32[1,1]{1,0:T(1,128)}) custom-call(bf16[16,64,1024]{2,1,0:T(8,128)(2,1)S(1)} %all-to-all-done.3.got_ref, bf16[512,1024]{1,0:T(8,128)(2,1)S(1)} %constant_dynamic-update-slice_fusion.extra_ref), custom_call_target="tpu_custom_call" | custom-call | tf_op jit(solution)/shard_map/score/pallas_call | solution.py:336
  91.5 3.7 %all-to-all-start.4 = ((f32[16,1,128]{2,1,0:T(1,128)}), f32[16,1,128]{2,1,0:T(1,128)S(1)}, u32[]{:S(2)}, u32[]{:S(2)}) async-start(f32[16,1,128]{2,1,0:T(1,128)} %get-tuple-element.89), calls=%async_computation.4 | async-start | bytes 16384 | tf_op jit(solution)/shard_map/all_to_all | solution.py:426
  95.9 5.8 %all-to-all-done.4.back_ref = f32[16,1,128]{2,1,0:T(1,128)S(1)} async-done(((f32[16,1,128]{2,1,0:T(1,128)}), f32[16,1,128]{2,1,0:T(1,128)S(1)}, u32[]{:S(2)}, u32[]{:S(2)}) %all-to-all-start.4) | async-done | bytes 8224 | tf_op jit(solution)/shard_map/all_to_all | solution.py:426
  101.6 0.0 copy-start.5
  101.7 0.6 copy-done.5
  102.2 0.0 copy-done.3
  102.2 0.0 copy-done.4
  102.2 0.8 place.1
  103.0 0.2 conditional.1
  103.3 0.0 copy-start.6
  103.3 0.6 copy-done.6
  (8 shorter events, 0.1 us)
Async XLA Ops:
  8.2 0.6 copy-start
  8.8 7.6 %copy-start.2 = (bf16[32,1024]{1,0:T(8,128)(2,1)S(1)}, bf16[32,1024]{1,0:T(8,128)(2,1)}, u32[]{:S(2)}) copy-start(bf16[32,1024]{1,0:T(8,128)(2,1)} %get-tuple-element.87) | copy-start | bytes 196612
  8.8 73.6 %all-to-all-start.3 = ((bf16[16,64,1024]{2,1,0:T(8,128)(2,1)}), bf16[16,64,1024]{2,1,0:T(8,128)(2,1)S(1)}, u32[]{:S(2)}, u32[]{:S(2)}) async-start(bf16[16,64,1024]{2,1,0:T(8,128)(2,1)} %bitcast.34), calls=%async_computation.3 | async-start | bytes 4194304 | tf_op jit(solution)/shard_map/all_to_all | solution.py:422
  16.3 85.9 %copy-start.3 = (s32[1024]{0:T(1024)S(1)}, s32[1024]{0:T(1024)}, u32[]{:S(2)}) copy-start(s32[1024]{0:T(1024)} %param.8) | copy-start | bytes 12292
  16.3 85.9 %copy-start.4 = (s32[1024]{0:T(1024)S(1)}, s32[1024]{0:T(1024)}, u32[]{:S(2)}) copy-start(s32[1024]{0:T(1024)} %param.9) | copy-start | bytes 12292
  16.4 51.8 %collective-permute-start = (bf16[32,1024]{1,0:T(8,128)(2,1)S(1)}, bf16[32,1024]{1,0:T(8,128)(2,1)S(1)}, u32[]{:S(2)}, u32[]{:S(2)}) collective-permute-start(bf16[32,1024]{1,0:T(8,128)(2,1)S(1)} %copy-done.2), channel_id=1, source_target_pairs={{0,8},{1,9},{2,10},{3,11},{4,12},{5,13},{6,14},{7,15},{8,0},{9,1},... | collective-permute-start | bytes 196616 | tf_op jit(solution)/shard_map/ppermute | solution.py:197
  68.2 5.1 %collective-permute-start.1 = (bf16[64,1024]{1,0:T(8,128)(2,1)S(1)}, bf16[64,1024]{1,0:T(8,128)(2,1)S(1)}, u32[]{:S(2)}, u32[]{:S(2)}) collective-permute-start(bf16[64,1024]{1,0:T(8,128)(2,1)S(1)} %pad_maximum_fusion.2), channel_id=1, source_target_pairs={{0,4},{1,5},{2,6},{3,7},{4,0},{5,1},{6,2},{7,3},{8,12},{9,13},{10,... | collective-permute-start | bytes 393224 | tf_op jit(solution)/shard_map/ppermute | solution.py:197
  73.3 7.0 %collective-permute-start.2 = (bf16[128,1024]{1,0:T(8,128)(2,1)S(1)}, bf16[128,1024]{1,0:T(8,128)(2,1)S(1)}, u32[]{:S(2)}, u32[]{:S(2)}) collective-permute-start(bf16[128,1024]{1,0:T(8,128)(2,1)S(1)} %pad_maximum_fusion.1), channel_id=1, source_target_pairs={{0,2},{1,3},{2,0},{3,1},{4,6},{5,7},{6,4},{7,5},{8,10},{9,11},{10,... | collective-permute-start | bytes 786440 | tf_op jit(solution)/shard_map/ppermute | solution.py:197
  80.4 2.0 %collective-permute-start.3 = (bf16[256,1024]{1,0:T(8,128)(2,1)S(1)}, bf16[256,1024]{1,0:T(8,128)(2,1)S(1)}, u32[]{:S(2)}, u32[]{:S(2)}) collective-permute-start(bf16[256,1024]{1,0:T(8,128)(2,1)S(1)} %pad_maximum_fusion), channel_id=1, source_target_pairs={{0,1},{1,0},{2,3},{3,2},{4,5},{5,4},{6,7},{7,6},{8,9},{9,8},{10,11... | collective-permute-start | bytes 1572872 | tf_op jit(solution)/shard_map/ppermute | solution.py:197
  91.5 10.1 %all-to-all-start.4 = ((f32[16,1,128]{2,1,0:T(1,128)}), f32[16,1,128]{2,1,0:T(1,128)S(1)}, u32[]{:S(2)}, u32[]{:S(2)}) async-start(f32[16,1,128]{2,1,0:T(1,128)} %get-tuple-element.89), calls=%async_computation.4 | async-start | bytes 16384 | tf_op jit(solution)/shard_map/all_to_all | solution.py:426
  101.6 0.6 copy-start.5
  103.3 0.6 copy-start.6

commit v3 on v2

v3 whole, which is shorter than its diff:
```python
import functools

import jax
import jax.numpy as jnp
from jax import lax
from jax.experimental import pallas as pl
from jax.experimental.pallas import tpu as pltpu
from jax.sharding import PartitionSpec as P

CL_DEV = 8
SLOT = 16
LANES = 128
NEAR = 96
FAR = 80
TILE = 1408
STEP = 256
VMEM = 56 * 1024 * 1024
BF = jnp.bfloat16
F32 = jnp.float32


def iota(shape, dim):
    return lax.broadcasted_iota(jnp.int32, shape, dim)


def bits(mask):
    return mask.astype(F32).astype(BF)


def product(left, right):
    return jnp.dot(left, right, preferred_element_type=F32)


def product_t(left, right):
    return lax.dot_general(left, right, (((1,), (1,)), ((), ())), preferred_element_type=F32)


def before():
    return bits(iota((LANES, LANES), 0) < iota((LANES, LANES), 1))


def size_of(owners, k):
    half = owners // 2
    return (NEAR, k * NEAR) if k < half else (FAR, half * NEAR + (k - half) * FAR)


def regions(owners):
    half = owners // 2
    return ((0, half, NEAR, 0), (half, half, FAR, half * NEAR))


def start_of(owners, k):
    half = owners // 2
    return jnp.where(k < half, k * NEAR, half * NEAR + (k - half) * FAR)


def pack_kernel(owners, cid_ref, valid_ref, rows_ref, *refs):
    blocks = refs[:owners]
    code_ref, held, unit, choose, out, in_sems, out_sems = refs[owners:]
    rows, width = held.shape
    lines = rows // LANES
    parts = rows // STEP
    total = out.shape[0]
    tile = choose.shape[0]
    me = lax.axis_index("owners")
    loads = []
    for part in range(parts):
        at = pl.ds(part * STEP, STEP)
        loads.append(pltpu.make_async_copy(rows_ref.at[at], held.at[at], in_sems.at[part]))
        loads[-1].start()

    cid = cid_ref[...]
    live = valid_ref[...] == 1
    step = lax.shift_right_logical(cid, 3) ^ me
    name = (cid & (CL_DEV - 1)) + 1
    target = jnp.where(live, step, -1)
    index = iota((owners, LANES), 0)
    mine = [(index == target[line : line + 1]).astype(F32) for line in range(lines)]
    stacked = jnp.concatenate(mine, axis=0).astype(BF)
    inside = product(stacked, before())
    whole = product(stacked, jnp.ones((LANES, LANES), BF))
    offset = jnp.zeros((owners, LANES), F32)
    ranks = []
    for line in range(lines):
        at = slice(line * owners, (line + 1) * owners)
        ranks.append(jnp.sum(mine[line] * (inside[at] + offset), axis=0, keepdims=True))
        offset = offset + whole[at]
    pos = jnp.concatenate(ranks, axis=0).astype(jnp.int32)
    room = jnp.where(step < owners // 2, NEAR - 1, FAR - 1)
    fits = live & (pos < room)
    lost = jnp.max((live & (pos >= room)).astype(F32))
    code = jnp.where(fits, pos, LANES - 1)
    code_ref[...] = code
    dest = jnp.where(fits, start_of(owners, step) + pos, -1)

    names = jnp.concatenate(
        [mine[line] * name[line : line + 1].astype(F32) for line in range(lines)], axis=1
    ).astype(BF)
    index = iota((LANES, LANES), 0)
    places = jnp.concatenate([bits(index == code[line : line + 1]) for line in range(lines)], axis=1)
    meta = product_t(names, places)
    meta = jnp.where(iota((owners, LANES), 1) == LANES - 1, lost, meta).astype(BF)

    def fill(begin, count):
        index = iota((count, LANES), 0) + begin
        for line in range(lines):
            at = slice(line * LANES, (line + 1) * LANES)
            choose[:, at] = bits(index == dest[line : line + 1])

    fill(0, tile)
    for part in range(parts):
        loads[part].wait()

        def one_chunk(number, carry):
            at = pl.ds(pl.multiple_of(part * STEP + number * 64, 64), 64)
            values = held[at, :].astype(F32)
            squares = jnp.sum(values * values, axis=1, keepdims=True)
            unit[at, :] = (values * lax.rsqrt(squares + 1e-06)).astype(BF)
            return carry

        lax.fori_loop(0, STEP // 64, one_chunk, 0)

    stores = []
    for first in range(0, total, tile):
        if first:
            fill(first, tile)
        for column in range(0, width, STEP):
            at = slice(column, column + STEP)
            packed = product(choose[...], unit[:, at])
            if column == 0:
                line = iota((tile, owners), 0) + first
                last = start_of(owners, iota((1, owners), 1) + 1) - 1
                packed = jnp.concatenate(
                    [packed[:, :LANES] + product(bits(line == last), meta), packed[:, LANES:]], axis=1
                )
            out[pl.ds(first, tile), at] = packed.astype(BF)
            for k in range(owners):
                size, start = size_of(owners, k)
                if first < start + size <= first + tile:
                    stores.append(
                        pltpu.make_async_copy(
                            out.at[pl.ds(start, size), at], blocks[k].at[:, at], out_sems.at[len(stores)]
                        )
                    )
                    stores[-1].start()
    for store in stores:
        store.wait()


def total_of(owners):
    return owners // 2 * (NEAR + FAR)


def pack(embeddings, cluster_id, valid, owners):
    rows, width = embeddings.shape
    total = total_of(owners)
    tile = min(total, TILE)
    lines = (rows // LANES, LANES)
    sizes = [size_of(owners, k)[0] for k in range(owners)]
    *blocks, code = pl.pallas_call(
        functools.partial(pack_kernel, owners),
        out_shape=[pltpu.HBM((size, width), BF) for size in sizes]
        + [jax.ShapeDtypeStruct(lines, jnp.int32)],
        in_specs=[
            pl.BlockSpec(memory_space=pltpu.VMEM),
            pl.BlockSpec(memory_space=pltpu.VMEM),
            pl.BlockSpec(memory_space=pltpu.HBM),
        ],
        out_specs=[pl.BlockSpec(memory_space=pltpu.HBM)] * owners
        + [pl.BlockSpec(memory_space=pltpu.VMEM)],
        scratch_shapes=[
            pltpu.VMEM((rows, width), BF),
            pltpu.VMEM((rows, width), BF),
            pltpu.VMEM((tile, rows), BF),
            pltpu.VMEM((total, width), BF),
            pltpu.SemaphoreType.DMA((rows // STEP,)),
            pltpu.SemaphoreType.DMA((owners * (width // STEP),)),
        ],
        compiler_params=pltpu.CompilerParams(vmem_limit_bytes=VMEM),
        name="pack",
    )(cluster_id.reshape(lines), valid.reshape(lines), embeddings)
    return blocks, code


def swap(block, k, owners):
    if k == 0:
        return block
    return lax.ppermute(block, "owners", [(i, i ^ k) for i in range(owners)])


def score_kernel(owners, *refs):
    got = refs[:owners]
    best = refs[owners : 2 * owners]
    lost_ref, tags, rows, side, top, line, tag_sems, sems = refs[2 * owners :]
    total, width = rows.shape
    tag_copies, moves = [], []
    for k in range(owners):
        size, start = size_of(owners, k)
        tag_copies.append(
            pltpu.make_async_copy(
                got[k].at[pl.ds(size - 16, 16), pl.ds(0, LANES)], tags.at[k], tag_sems.at[k]
            )
        )
        tag_copies[-1].start()
    for k in range(owners):
        size, start = size_of(owners, k)
        moves.append(pltpu.make_async_copy(got[k], rows.at[pl.ds(start, size)], sems.at[k]))
        moves[-1].start()
    for copy in tag_copies:
        copy.wait()
    flat = tags[...].reshape(owners * 16, LANES)
    pick = bits(iota((owners, owners * 16), 1) == iota((owners, owners * 16), 0) * 16 + 15)
    names = product(pick, flat)
    lost = jnp.max(jnp.where(iota((owners, LANES), 1) == LANES - 1, names, 0.0))
    lost_ref[0, 0] = (lost > 0.0).astype(jnp.int32)
    names = names.astype(BF)
    for first, blocks, size, start in regions(owners):
        count = blocks * size
        base = iota((count, 1), 0)
        wide = product(bits(iota((count, owners), 1) == first + base // size), names)
        wide = jnp.where(iota((count, LANES), 1) == base % size, wide, 0.0).astype(BF)
        found = product(wide, jnp.ones((LANES, LANES), BF))
        side[pl.ds(start, count), :] = jnp.where(found == 0.0, -1.0, found)
        base = iota((1, count), 1)
        wide = product(names, bits(iota((LANES, count), 0) == base % size))
        wide = jnp.where(iota((owners, count), 0) == first + base // size, wide, 0.0)
        top[:, pl.ds(start, count)] = jnp.sum(wide, axis=0, keepdims=True)
    for move in moves:
        move.wait()

    unlike = iota((LANES, LANES), 0) != iota((LANES, LANES), 1)

    def columns(first, span, square):
        here = pl.ds(first, span)
        scores = product_t(rows[...], rows[here, :])
        tops = top[:, here]
        result = [jnp.full((1, LANES), -1.0, F32)] * (span // LANES)
        for block in range(total // LANES):
            at = slice(block * LANES, (block + 1) * LANES)
            for part in range(span // LANES):
                lanes = slice(part * LANES, (part + 1) * LANES)
                allowed = side[at, :] == tops[:, lanes]
                diagonal = square(block, part)
                if diagonal is not None:
                    allowed = allowed & (unlike | diagonal)
                masked = jnp.where(allowed, scores[at, lanes], -1.0)
                result[part] = jnp.maximum(result[part], jnp.max(masked, axis=0, keepdims=True))
        line[:, here] = jnp.concatenate(result, axis=1)

    if total <= 2048:
        for first in range(0, total, STEP):
            columns(
                first,
                min(STEP, total - first),
                lambda block, part: False if block == first // LANES + part else None,
            )
    else:

        @pl.loop(0, total // STEP)
        def _(number):
            columns(
                pl.multiple_of(number * STEP, STEP),
                STEP,
                lambda block, part: block != number * (STEP // LANES) + part,
            )

    for k in range(owners):
        size, start = size_of(owners, k)
        base, shift = divmod(start, LANES)
        base *= LANES
        piece = line[:, base : min(base + 2 * LANES, total)]
        if shift:
            piece = pltpu.roll(piece, piece.shape[1] - shift, 1)
        best[k][...] = piece[:, :LANES]


def score(got, owners):
    width = got[0].shape[1]
    total = total_of(owners)
    *best, lost = pl.pallas_call(
        functools.partial(score_kernel, owners),
        out_shape=[jax.ShapeDtypeStruct((1, LANES), F32)] * owners
        + [jax.ShapeDtypeStruct((1, 1), jnp.int32)],
        in_specs=[pl.BlockSpec(memory_space=pltpu.HBM)] * owners,
        out_specs=[pl.BlockSpec(memory_space=pltpu.VMEM)] * owners
        + [pl.BlockSpec(memory_space=pltpu.SMEM)],
        scratch_shapes=[
            pltpu.VMEM((owners, 16, LANES), BF),
            pltpu.VMEM((total, width), BF),
            pltpu.VMEM((total, LANES), F32),
            pltpu.VMEM((1, total), F32),
            pltpu.VMEM((1, total), F32),
            pltpu.SemaphoreType.DMA((owners,)),
            pltpu.SemaphoreType.DMA((owners,)),
        ],
        compiler_params=pltpu.CompilerParams(vmem_limit_bytes=VMEM),
        name="score",
    )(*got)
    return best, lost


def place_kernel(owners, *refs):
    back = refs[:owners]
    cid_ref, code_ref, valid_ref, out_ref = refs[owners:]
    me = lax.axis_index("owners")
    for start in range(0, cid_ref.shape[0], 8):
        at = slice(start, start + 8)
        step = lax.shift_right_logical(cid_ref[at, :], 3) ^ me
        code = code_ref[at, :]
        result = jnp.zeros((8, LANES), F32)
        for k in range(owners):
            line = jnp.broadcast_to(back[k][...], (8, LANES))
            value = jnp.take_along_axis(line, code, axis=1, mode="promise_in_bounds")
            result = jnp.where(step == k, value, result)
        out_ref[at, :] = jnp.where(valid_ref[at, :] == 1, result, 0.0)


def place(back, cluster_id, code, valid, owners):
    rows = cluster_id.shape[0]
    shape = (rows // LANES, LANES)
    return pl.pallas_call(
        functools.partial(place_kernel, owners),
        out_shape=jax.ShapeDtypeStruct(shape, F32),
        name="place",
    )(*back, cluster_id.reshape(shape), code, valid.reshape(shape)).reshape(rows)


def every_slot(embeddings, cluster_id, valid, owners):
    width = embeddings.shape[1]
    clusters = CL_DEV * owners
    values = embeddings.astype(F32)
    squares = jnp.sum(values * values, axis=1, keepdims=True)
    unit_rows = (values * lax.rsqrt(squares + 1e-06)).astype(BF)
    one_hot = (cluster_id[:, None] == jnp.arange(clusters, dtype=jnp.int32)[None, :]).astype(jnp.int32)
    ranking = jnp.sum(jnp.cumsum(one_hot, axis=0) * one_hot, axis=1) - 1
    target = cluster_id * SLOT + ranking
    outgoing = jnp.zeros((clusters * SLOT, width), BF).at[target].set(unit_rows)
    live_out = jnp.zeros((clusters * SLOT,), BF).at[target].set(valid.astype(BF))
    got = lax.all_to_all(
        outgoing.reshape(owners, CL_DEV * SLOT, width), "owners", split_axis=0, concat_axis=0, tiled=True
    )
    live = lax.all_to_all(
        live_out.reshape(owners, CL_DEV, SLOT), "owners", split_axis=0, concat_axis=0, tiled=True
    )
    got = got.reshape(owners, CL_DEV, SLOT, width).transpose(1, 0, 2, 3)
    got = got.reshape(CL_DEV, owners * SLOT, width)
    live = live.transpose(1, 0, 2).reshape(CL_DEV, owners * SLOT) > 0.5
    diagonal = jnp.eye(owners * SLOT, dtype=bool)

    def one_cluster(args):
        rows, flags = args
        scores = jnp.einsum("md,nd->mn", rows, rows, preferred_element_type=F32)
        allowed = flags[:, None] & flags[None, :] & ~diagonal
        return jnp.max(jnp.where(allowed, scores, -1.0), axis=1)

    best = lax.map(one_cluster, (got, live)).reshape(CL_DEV, owners, SLOT).transpose(1, 0, 2)
    back = lax.all_to_all(best, "owners", split_axis=0, concat_axis=0, tiled=True)
    return jnp.where(valid == 1, back.reshape(-1)[target], 0.0)


def shards(embeddings, cluster_id, valid):
    owners = lax.axis_size("owners")
    blocks, code = pack(embeddings, cluster_id, valid, owners)
    got = list(blocks)
    for k in reversed(range(owners)):
        got[k] = swap(blocks[k], k, owners)
    best, lost = score(got, owners)
    back = [swap(best[k], k, owners) for k in range(owners)]
    nearest = place(back, cluster_id, code, valid, owners)
    return lax.cond(
        lost[0, 0] > 0,
        lambda: every_slot(embeddings, cluster_id, valid, owners),
        lambda: nearest,
    )


def solution(mesh):
    placed = (P(("groups", "owners"), None), P(("groups", "owners")), P(("groups", "owners")))
    return jax.shard_map(
        shards, mesh=mesh, in_specs=placed, out_specs=P(("groups", "owners")), check_vma=False
    )
```

time: 104 us -> 128 us (1.23)
  starting transfers between devices: 15.8 us -> 63.5 us
  waiting for transfers between devices: 67 us -> 41.4 us
  Pallas kernels: 18.1 us -> 19.9 us
    ppermute x4 -> x30, starting transfers between devices: 4.61 us -> 63.5 us  [swap(): return lax.ppermute(block, 'owners', [(i, i ^ k) for i in range(owners)])]
    ppermute x4 -> x30, waiting for transfers between devices: 61.2 us -> 41.4 us  [swap(): return lax.ppermute(block, 'owners', [(i, i ^ k) for i in range(owners)])]
    all_to_all x2 -> x0, starting transfers between devices: 11.2 us -> none  [the longest x1 7.52 us: shards(): lax.all_to_all(blocks.reshape(owners, FAST, width), 'owners', split_axis=...]
    all_to_all x2 -> x0, waiting for transfers between devices: 5.76 us -> none  [the longest x1 5.76 us: shards(): lax.all_to_all(best, 'owners', split_axis=0, concat_axis=0, tiled=True)]
    pallas_call x2, Pallas kernels: 17.3 us -> 19 us  [the longest x1 10.6 us: pack(): pl.pallas_call(functools.partial(pack_kernel, owners), out_shape=[pltpu.H...]
  transfers between devices with their start and end apart: 6 -> 30, of which waited for: 5 -> 9; matrix products, arithmetic and copies ran while one was open for 0% -> 0% of each run, Pallas kernels for 0% -> 0%
where the time goes in v3:
time: 128 us
  starting transfers between devices  63.5 us (50%)
  waiting for transfers between devices  41.4 us (32%)
  Pallas kernels  19.9 us (16%)
  local copies, waits for them, and re-layouts  1.74 us (1%)
    ppermute x30, starting transfers between devices, swap(): return lax.ppermute(block, 'owners', [(i, i ^ k) for i in range(owners)])  63.5 us
    ppermute x30, waiting for transfers between devices, swap(): return lax.ppermute(block, 'owners', [(i, i ^ k) for i in range(owners)])  41.4 us
    pallas_call x1, Pallas kernels, pack(): pl.pallas_call(functools.partial(pack_kernel, owners), out_shape=[pltpu.H...  10.6 us
    pallas_call x1, Pallas kernels, score(): pl.pallas_call(functools.partial(score_kernel, owners), out_shape=[jax.Sh...  8.39 us
  transfers between devices with their start and end apart: 30, of which 9 were waited for; matrix products, arithmetic and copies ran while one was open for 0% of the time, Pallas kernels for 0%

profile of v3, /device:TPU:0, one launch (start us, length us, event | category | flops | bytes accessed | tf_op | source)
XLA Modules:
  0.0 127.6 jit_solution(3218177995144642275)
XLA Ops:
  0.0 10.6 %pack.1 = (bf16[96,1024]{1,0:T(8,128)(2,1)}, bf16[96,1024]{1,0:T(8,128)(2,1)}, bf16[96,1024]{1,0:T(8,128)(2,1)}, bf16[96,1024]{1,0:T(8,128)(2,1)}, bf16[96,1024]...) custom-call(s32[8,128]{1,0:T(8,128)} %bitcast.34, ...), custom_call_target="tpu_custom_call" | custom-call | tf_op jit(solution)/shard_map/pack/pallas_call | solution.py:160
  10.6 4.5 %collective-permute-start.10 = (bf16[80,1024]{1,0:T(8,128)(2,1)}, bf16[80,1024]{1,0:T(8,128)(2,1)S(1)}, u32[]{:S(2)}, u32[]{:S(2)}) collective-permute-start(bf16[80,1024]{1,0:T(8,128)(2,1)} %get-tuple-element.126), channel_id=1, source_target_pairs={{0,11},{1,10},{2,9},{3,8},{4,15},{5,14},{6,13},{7,12},{8,3},{9,2},... | collective-permute-start | bytes 491528 | tf_op jit(solution)/shard_map/ppermute | solution.py:188
  15.2 1.3 %collective-permute-start.11 = (bf16[80,1024]{1,0:T(8,128)(2,1)}, bf16[80,1024]{1,0:T(8,128)(2,1)S(1)}, u32[]{:S(2)}, u32[]{:S(2)}) collective-permute-start(bf16[80,1024]{1,0:T(8,128)(2,1)} %get-tuple-element.127), channel_id=1, source_target_pairs={{0,12},{1,13},{2,14},{3,15},{4,8},{5,9},{6,10},{7,11},{8,4},{9,5},... | collective-permute-start | bytes 491528 | tf_op jit(solution)/shard_map/ppermute | solution.py:188
  16.5 2.5 %collective-permute-start.12 = (bf16[80,1024]{1,0:T(8,128)(2,1)}, bf16[80,1024]{1,0:T(8,128)(2,1)S(1)}, u32[]{:S(2)}, u32[]{:S(2)}) collective-permute-start(bf16[80,1024]{1,0:T(8,128)(2,1)} %get-tuple-element.128), channel_id=1, source_target_pairs={{0,13},{1,12},{2,15},{3,14},{4,9},{5,8},{6,11},{7,10},{8,5},{9,4},... | collective-permute-start | bytes 491528 | tf_op jit(solution)/shard_map/ppermute | solution.py:188
  19.0 1.3 %collective-permute-start.13 = (bf16[80,1024]{1,0:T(8,128)(2,1)}, bf16[80,1024]{1,0:T(8,128)(2,1)S(1)}, u32[]{:S(2)}, u32[]{:S(2)}) collective-permute-start(bf16[80,1024]{1,0:T(8,128)(2,1)} %get-tuple-element.129), channel_id=1, source_target_pairs={{0,14},{1,15},{2,12},{3,13},{4,10},{5,11},{6,8},{7,9},{8,6},{9,7},... | collective-permute-start | bytes 491528 | tf_op jit(solution)/shard_map/ppermute | solution.py:188
  20.3 2.9 %collective-permute-start.14 = (bf16[80,1024]{1,0:T(8,128)(2,1)}, bf16[80,1024]{1,0:T(8,128)(2,1)S(1)}, u32[]{:S(2)}, u32[]{:S(2)}) collective-permute-start(bf16[80,1024]{1,0:T(8,128)(2,1)} %get-tuple-element.130), channel_id=1, source_target_pairs={{0,15},{1,14},{2,13},{3,12},{4,11},{5,10},{6,9},{7,8},{8,7},{9,6},... | collective-permute-start | bytes 491528 | tf_op jit(solution)/shard_map/ppermute | solution.py:188
  23.2 13.7 %collective-permute-done.10.refs_11_ = bf16[80,1024]{1,0:T(8,128)(2,1)S(1)} collective-permute-done((bf16[80,1024]{1,0:T(8,128)(2,1)}, bf16[80,1024]{1,0:T(8,128)(2,1)S(1)}, u32[]{:S(2)}, u32[]{:S(2)}) %collective-permute-start.10) | collective-permute-done | bytes 163872 | tf_op jit(solution)/shard_map/ppermute | solution.py:188
  36.9 1.5 %collective-permute-start = (bf16[96,1024]{1,0:T(8,128)(2,1)}, bf16[96,1024]{1,0:T(8,128)(2,1)S(1)}, u32[]{:S(2)}, u32[]{:S(2)}) collective-permute-start(bf16[96,1024]{1,0:T(8,128)(2,1)} %get-tuple-element.116), channel_id=1, source_target_pairs={{0,1},{1,0},{2,3},{3,2},{4,5},{5,4},{6,7},{7,6},{8,9},{9,8},{10,11... | collective-permute-start | bytes 589832 | tf_op jit(solution)/shard_map/ppermute | solution.py:188
  38.4 1.6 %collective-permute-start.1 = (bf16[96,1024]{1,0:T(8,128)(2,1)}, bf16[96,1024]{1,0:T(8,128)(2,1)S(1)}, u32[]{:S(2)}, u32[]{:S(2)}) collective-permute-start(bf16[96,1024]{1,0:T(8,128)(2,1)} %get-tuple-element.117), channel_id=1, source_target_pairs={{0,2},{1,3},{2,0},{3,1},{4,6},{5,7},{6,4},{7,5},{8,10},{9,11},{10,... | collective-permute-start | bytes 589832 | tf_op jit(solution)/shard_map/ppermute | solution.py:188
  39.9 0.0 collective-permute-done.12.refs_13_
  39.9 8.0 %collective-permute-start.7 = (bf16[80,1024]{1,0:T(8,128)(2,1)}, bf16[80,1024]{1,0:T(8,128)(2,1)S(1)}, u32[]{:S(2)}, u32[]{:S(2)}) collective-permute-start(bf16[80,1024]{1,0:T(8,128)(2,1)} %get-tuple-element.123), channel_id=1, source_target_pairs={{0,8},{1,9},{2,10},{3,11},{4,12},{5,13},{6,14},{7,15},{8,0},{9,1},... | collective-permute-start | bytes 491528 | tf_op jit(solution)/shard_map/ppermute | solution.py:188
  47.9 3.2 %collective-permute-start.8 = (bf16[80,1024]{1,0:T(8,128)(2,1)}, bf16[80,1024]{1,0:T(8,128)(2,1)S(1)}, u32[]{:S(2)}, u32[]{:S(2)}) collective-permute-start(bf16[80,1024]{1,0:T(8,128)(2,1)} %get-tuple-element.124), channel_id=1, source_target_pairs={{0,9},{1,8},{2,11},{3,10},{4,13},{5,12},{6,15},{7,14},{8,1},{9,0},... | collective-permute-start | bytes 491528 | tf_op jit(solution)/shard_map/ppermute | solution.py:188
  51.1 11.8 %collective-permute-start.9 = (bf16[80,1024]{1,0:T(8,128)(2,1)}, bf16[80,1024]{1,0:T(8,128)(2,1)S(1)}, u32[]{:S(2)}, u32[]{:S(2)}) collective-permute-start(bf16[80,1024]{1,0:T(8,128)(2,1)} %get-tuple-element.125), channel_id=1, source_target_pairs={{0,10},{1,11},{2,8},{3,9},{4,14},{5,15},{6,12},{7,13},{8,2},{9,3},... | collective-permute-start | bytes 491528 | tf_op jit(solution)/shard_map/ppermute | solution.py:188
  62.9 0.0 collective-permute-done.7.refs_8_
  62.9 7.0 %collective-permute-done.8.refs_9_ = bf16[80,1024]{1,0:T(8,128)(2,1)S(1)} collective-permute-done((bf16[80,1024]{1,0:T(8,128)(2,1)}, bf16[80,1024]{1,0:T(8,128)(2,1)S(1)}, u32[]{:S(2)}, u32[]{:S(2)}) %collective-permute-start.8) | collective-permute-done | bytes 163872 | tf_op jit(solution)/shard_map/ppermute | solution.py:188
  69.9 0.8 collective-permute-start.3
  70.7 2.3 %collective-permute-done.9.refs_10_ = bf16[80,1024]{1,0:T(8,128)(2,1)S(1)} collective-permute-done((bf16[80,1024]{1,0:T(8,128)(2,1)}, bf16[80,1024]{1,0:T(8,128)(2,1)S(1)}, u32[]{:S(2)}, u32[]{:S(2)}) %collective-permute-start.9) | collective-permute-done | bytes 163872 | tf_op jit(solution)/shard_map/ppermute | solution.py:188
  73.0 0.9 collective-permute-start.4
  74.0 2.1 %collective-permute-start.5 = (bf16[96,1024]{1,0:T(8,128)(2,1)}, bf16[96,1024]{1,0:T(8,128)(2,1)S(1)}, u32[]{:S(2)}, u32[]{:S(2)}) collective-permute-start(bf16[96,1024]{1,0:T(8,128)(2,1)} %get-tuple-element.121), channel_id=1, source_target_pairs={{0,6},{1,7},{2,4},{3,5},{4,2},{5,3},{6,0},{7,1},{8,14},{9,15},{10,... | collective-permute-start | bytes 589832 | tf_op jit(solution)/shard_map/ppermute | solution.py:188
  76.1 0.5 collective-permute-start.6
  76.6 1.3 %collective-permute-done.3.refs_4_ = bf16[96,1024]{1,0:T(8,128)(2,1)S(1)} collective-permute-done((bf16[96,1024]{1,0:T(8,128)(2,1)}, bf16[96,1024]{1,0:T(8,128)(2,1)S(1)}, u32[]{:S(2)}, u32[]{:S(2)}) %collective-permute-start.3) | collective-permute-done | bytes 196640 | tf_op jit(solution)/shard_map/ppermute | solution.py:188
  77.9 3.7 %collective-permute-done.4.refs_5_ = bf16[96,1024]{1,0:T(8,128)(2,1)S(1)} collective-permute-done((bf16[96,1024]{1,0:T(8,128)(2,1)}, bf16[96,1024]{1,0:T(8,128)(2,1)S(1)}, u32[]{:S(2)}, u32[]{:S(2)}) %collective-permute-start.4) | collective-permute-done | bytes 196640 | tf_op jit(solution)/shard_map/ppermute | solution.py:188
  81.6 4.6 %collective-permute-done.5.refs_6_ = bf16[96,1024]{1,0:T(8,128)(2,1)S(1)} collective-permute-done((bf16[96,1024]{1,0:T(8,128)(2,1)}, bf16[96,1024]{1,0:T(8,128)(2,1)S(1)}, u32[]{:S(2)}, u32[]{:S(2)}) %collective-permute-start.5) | collective-permute-done | bytes 196640 | tf_op jit(solution)/shard_map/ppermute | solution.py:188
  86.3 3.8 %collective-permute-done.6.refs_7_ = bf16[96,1024]{1,0:T(8,128)(2,1)S(1)} collective-permute-done((bf16[96,1024]{1,0:T(8,128)(2,1)}, bf16[96,1024]{1,0:T(8,128)(2,1)S(1)}, u32[]{:S(2)}, u32[]{:S(2)}) %collective-permute-start.6) | collective-permute-done | bytes 196640 | tf_op jit(solution)/shard_map/ppermute | solution.py:188
  90.2 0.6 copy-done.7
  90.7 8.4 %score.1 = (f32[1,128]{1,0:T(1,128)}, f32[1,128]{1,0:T(1,128)}, f32[1,128]{1,0:T(1,128)}, f32[1,128]{1,0:T(1,128)}, f32[1,128]{1,0:T(1,128)}, /*index=5*/f32[1,1...) custom-call(bf16[96,1024]{1,0:T(8,128)(2,1)} %get-tuple-element.115., ...), custom_call_target="tpu_custom_call" | custom-call | tf_op jit(solution)/shard_map/score/pallas_call | solution.py:280
  99.1 0.2 collective-permute-start.15
  99.3 1.5 %collective-permute-start.16 = (f32[1,128]{1,0:T(1,128)}, f32[1,128]{1,0:T(1,128)S(1)}, u32[]{:S(2)}, u32[]{:S(2)}) collective-permute-start(f32[1,128]{1,0:T(1,128)} %get-tuple-element.134), channel_id=1, source_target_pairs={{0,2},{1,3},{2,0},{3,1},{4,6},{5,7},{6,4},{7,5},{8,10},{9,11},{10,... | collective-permute-start | bytes 1544 | tf_op jit(solution)/shard_map/ppermute | solution.py:188
  100.8 0.3 collective-permute-start.17
  101.1 0.1 collective-permute-start.18
  101.2 1.6 %collective-permute-start.19 = (f32[1,128]{1,0:T(1,128)}, f32[1,128]{1,0:T(1,128)S(1)}, u32[]{:S(2)}, u32[]{:S(2)}) collective-permute-start(f32[1,128]{1,0:T(1,128)} %get-tuple-element.137), channel_id=1, source_target_pairs={{0,5},{1,4},{2,7},{3,6},{4,1},{5,0},{6,3},{7,2},{8,13},{9,12},{10,... | collective-permute-start | bytes 1544 | tf_op jit(solution)/shard_map/ppermute | solution.py:188
  102.8 1.3 %collective-permute-start.20 = (f32[1,128]{1,0:T(1,128)}, f32[1,128]{1,0:T(1,128)S(1)}, u32[]{:S(2)}, u32[]{:S(2)}) collective-permute-start(f32[1,128]{1,0:T(1,128)} %get-tuple-element.138), channel_id=1, source_target_pairs={{0,6},{1,7},{2,4},{3,5},{4,2},{5,3},{6,0},{7,1},{8,14},{9,15},{10,... | collective-permute-start | bytes 1544 | tf_op jit(solution)/shard_map/ppermute | solution.py:188
  104.1 1.4 %collective-permute-start.21 = (f32[1,128]{1,0:T(1,128)}, f32[1,128]{1,0:T(1,128)S(1)}, u32[]{:S(2)}, u32[]{:S(2)}) collective-permute-start(f32[1,128]{1,0:T(1,128)} %get-tuple-element.139), channel_id=1, source_target_pairs={{0,7},{1,6},{2,5},{3,4},{4,3},{5,2},{6,1},{7,0},{8,15},{9,14},{10,... | collective-permute-start | bytes 1544 | tf_op jit(solution)/shard_map/ppermute | solution.py:188
  105.5 2.4 %collective-permute-start.22 = (f32[1,128]{1,0:T(1,128)}, f32[1,128]{1,0:T(1,128)S(1)}, u32[]{:S(2)}, u32[]{:S(2)}) collective-permute-start(f32[1,128]{1,0:T(1,128)} %get-tuple-element.140), channel_id=1, source_target_pairs={{0,8},{1,9},{2,10},{3,11},{4,12},{5,13},{6,14},{7,15},{8,0},{9,1},... | collective-permute-start | bytes 1544 | tf_op jit(solution)/shard_map/ppermute | solution.py:188
  107.9 0.2 collective-permute-start.23
  108.2 3.3 %collective-permute-start.24 = (f32[1,128]{1,0:T(1,128)}, f32[1,128]{1,0:T(1,128)S(1)}, u32[]{:S(2)}, u32[]{:S(2)}) collective-permute-start(f32[1,128]{1,0:T(1,128)} %get-tuple-element.142), channel_id=1, source_target_pairs={{0,10},{1,11},{2,8},{3,9},{4,14},{5,15},{6,12},{7,13},{8,2},{9,3},... | collective-permute-start | bytes 1544 | tf_op jit(solution)/shard_map/ppermute | solution.py:188
  111.5 0.3 collective-permute-start.25
  111.8 3.6 %collective-permute-start.26 = (f32[1,128]{1,0:T(1,128)}, f32[1,128]{1,0:T(1,128)S(1)}, u32[]{:S(2)}, u32[]{:S(2)}) collective-permute-start(f32[1,128]{1,0:T(1,128)} %get-tuple-element.144), channel_id=1, source_target_pairs={{0,12},{1,13},{2,14},{3,15},{4,8},{5,9},{6,10},{7,11},{8,4},{9,5},... | collective-permute-start | bytes 1544 | tf_op jit(solution)/shard_map/ppermute | solution.py:188
  115.4 0.0 collective-permute-start.27
  115.4 4.2 %collective-permute-start.28 = (f32[1,128]{1,0:T(1,128)}, f32[1,128]{1,0:T(1,128)S(1)}, u32[]{:S(2)}, u32[]{:S(2)}) collective-permute-start(f32[1,128]{1,0:T(1,128)} %get-tuple-element.146), channel_id=1, source_target_pairs={{0,14},{1,15},{2,12},{3,13},{4,10},{5,11},{6,8},{7,9},{8,6},{9,7},... | collective-permute-start | bytes 1544 | tf_op jit(solution)/shard_map/ppermute | solution.py:188
  119.6 0.1 collective-permute-start.29
  120.5 1.3 %collective-permute-done.28.refs_14_ = f32[1,128]{1,0:T(1,128)S(1)} collective-permute-done((f32[1,128]{1,0:T(1,128)}, f32[1,128]{1,0:T(1,128)S(1)}, u32[]{:S(2)}, u32[]{:S(2)}) %collective-permute-start.28) | collective-permute-done | bytes 544 | tf_op jit(solution)/shard_map/ppermute | solution.py:188
  121.8 3.6 %collective-permute-done.29.refs_15_ = f32[1,128]{1,0:T(1,128)S(1)} collective-permute-done((f32[1,128]{1,0:T(1,128)}, f32[1,128]{1,0:T(1,128)S(1)}, u32[]{:S(2)}, u32[]{:S(2)}) %collective-permute-start.29) | collective-permute-done | bytes 544 | tf_op jit(solution)/shard_map/ppermute | solution.py:188
  125.5 0.5 copy-done.33
  125.9 0.8 place.1
  126.8 0.2 conditional.1
  127.0 0.0 copy-start.18
  127.1 0.6 copy-done.18
  (84 shorter events, 0.2 us)
Async XLA Ops:
  0.0 125.9 %copy-start.16 = (s32[1024]{0:T(1024)S(1)}, s32[1024]{0:T(1024)}, u32[]{:S(2)}) copy-start(s32[1024]{0:T(1024)} %param.8) | copy-start | bytes 12292
  0.0 125.9 %copy-start.17 = (s32[1024]{0:T(1024)S(1)}, s32[1024]{0:T(1024)}, u32[]{:S(2)}) copy-start(s32[1024]{0:T(1024)} %param.9) | copy-start | bytes 12292
  0.0 126.8 %copy-start = (bf16[1024,1024]{1,0:T(8,128)(2,1)S(1)}, bf16[1024,1024]{1,0:T(8,128)(2,1)}, u32[]{:S(2)}) copy-start(bf16[1024,1024]{1,0:T(8,128)(2,1)} %rows_ref.1) | copy-start | bytes 6291460
  10.6 26.2 %collective-permute-start.10 = (bf16[80,1024]{1,0:T(8,128)(2,1)}, bf16[80,1024]{1,0:T(8,128)(2,1)S(1)}, u32[]{:S(2)}, u32[]{:S(2)}) collective-permute-start(bf16[80,1024]{1,0:T(8,128)(2,1)} %get-tuple-element.126), channel_id=1, source_target_pairs={{0,11},{1,10},{2,9},{3,8},{4,15},{5,14},{6,13},{7,12},{8,3},{9,2},... | collective-permute-start | bytes 491528 | tf_op jit(solution)/shard_map/ppermute | solution.py:188
  15.2 23.2 %collective-permute-start.11 = (bf16[80,1024]{1,0:T(8,128)(2,1)}, bf16[80,1024]{1,0:T(8,128)(2,1)S(1)}, u32[]{:S(2)}, u32[]{:S(2)}) collective-permute-start(bf16[80,1024]{1,0:T(8,128)(2,1)} %get-tuple-element.127), channel_id=1, source_target_pairs={{0,12},{1,13},{2,14},{3,15},{4,8},{5,9},{6,10},{7,11},{8,4},{9,5},... | collective-permute-start | bytes 491528 | tf_op jit(solution)/shard_map/ppermute | solution.py:188
  16.5 23.4 %collective-permute-start.12 = (bf16[80,1024]{1,0:T(8,128)(2,1)}, bf16[80,1024]{1,0:T(8,128)(2,1)S(1)}, u32[]{:S(2)}, u32[]{:S(2)}) collective-permute-start(bf16[80,1024]{1,0:T(8,128)(2,1)} %get-tuple-element.128), channel_id=1, source_target_pairs={{0,13},{1,12},{2,15},{3,14},{4,9},{5,8},{6,11},{7,10},{8,5},{9,4},... | collective-permute-start | bytes 491528 | tf_op jit(solution)/shard_map/ppermute | solution.py:188
  19.0 28.9 %collective-permute-start.13 = (bf16[80,1024]{1,0:T(8,128)(2,1)}, bf16[80,1024]{1,0:T(8,128)(2,1)S(1)}, u32[]{:S(2)}, u32[]{:S(2)}) collective-permute-start(bf16[80,1024]{1,0:T(8,128)(2,1)} %get-tuple-element.129), channel_id=1, source_target_pairs={{0,14},{1,15},{2,12},{3,13},{4,10},{5,11},{6,8},{7,9},{8,6},{9,7},... | collective-permute-start | bytes 491528 | tf_op jit(solution)/shard_map/ppermute | solution.py:188
  20.3 30.9 %collective-permute-start.14 = (bf16[80,1024]{1,0:T(8,128)(2,1)}, bf16[80,1024]{1,0:T(8,128)(2,1)S(1)}, u32[]{:S(2)}, u32[]{:S(2)}) collective-permute-start(bf16[80,1024]{1,0:T(8,128)(2,1)} %get-tuple-element.130), channel_id=1, source_target_pairs={{0,15},{1,14},{2,13},{3,12},{4,11},{5,10},{6,9},{7,8},{8,7},{9,6},... | collective-permute-start | bytes 491528 | tf_op jit(solution)/shard_map/ppermute | solution.py:188
  36.9 53.2 %copy-start.8 = (bf16[80,1024]{1,0:T(8,128)(2,1)}, bf16[80,1024]{1,0:T(8,128)(2,1)S(1)}, u32[]{:S(2)}) copy-start(bf16[80,1024]{1,0:T(8,128)(2,1)S(1)} %collective-permute-done.10.refs_11_) | copy-start | bytes 491524
  36.9 37.1 %collective-permute-start = (bf16[96,1024]{1,0:T(8,128)(2,1)}, bf16[96,1024]{1,0:T(8,128)(2,1)S(1)}, u32[]{:S(2)}, u32[]{:S(2)}) collective-permute-start(bf16[96,1024]{1,0:T(8,128)(2,1)} %get-tuple-element.116), channel_id=1, source_target_pairs={{0,1},{1,0},{2,3},{3,2},{4,5},{5,4},{6,7},{7,6},{8,9},{9,8},{10,11... | collective-permute-start | bytes 589832 | tf_op jit(solution)/shard_map/ppermute | solution.py:188
  38.3 51.7 %copy-start.9 = (bf16[80,1024]{1,0:T(8,128)(2,1)}, bf16[80,1024]{1,0:T(8,128)(2,1)S(1)}, u32[]{:S(2)}) copy-start(bf16[80,1024]{1,0:T(8,128)(2,1)S(1)} %collective-permute-done.11.refs_12_) | copy-start | bytes 491524
  38.4 37.7 %collective-permute-start.1 = (bf16[96,1024]{1,0:T(8,128)(2,1)}, bf16[96,1024]{1,0:T(8,128)(2,1)S(1)}, u32[]{:S(2)}, u32[]{:S(2)}) collective-permute-start(bf16[96,1024]{1,0:T(8,128)(2,1)} %get-tuple-element.117), channel_id=1, source_target_pairs={{0,2},{1,3},{2,0},{3,1},{4,6},{5,7},{6,4},{7,5},{8,10},{9,11},{10,... | collective-permute-start | bytes 589832 | tf_op jit(solution)/shard_map/ppermute | solution.py:188
  39.9 50.1 %copy-start.10 = (bf16[80,1024]{1,0:T(8,128)(2,1)}, bf16[80,1024]{1,0:T(8,128)(2,1)S(1)}, u32[]{:S(2)}) copy-start(bf16[80,1024]{1,0:T(8,128)(2,1)S(1)} %collective-permute-done.12.refs_13_) | copy-start | bytes 491524
  39.9 23.0 %collective-permute-start.7 = (bf16[80,1024]{1,0:T(8,128)(2,1)}, bf16[80,1024]{1,0:T(8,128)(2,1)S(1)}, u32[]{:S(2)}, u32[]{:S(2)}) collective-permute-start(bf16[80,1024]{1,0:T(8,128)(2,1)} %get-tuple-element.123), channel_id=1, source_target_pairs={{0,8},{1,9},{2,10},{3,11},{4,12},{5,13},{6,14},{7,15},{8,0},{9,1},... | collective-permute-start | bytes 491528 | tf_op jit(solution)/shard_map/ppermute | solution.py:188
  47.9 42.1 %copy-start.11 = (bf16[80,1024]{1,0:T(8,128)(2,1)}, bf16[80,1024]{1,0:T(8,128)(2,1)S(1)}, u32[]{:S(2)}) copy-start(bf16[80,1024]{1,0:T(8,128)(2,1)S(1)} %collective-permute-done.13.refs_14_) | copy-start | bytes 491524
  47.9 22.0 %collective-permute-start.8 = (bf16[80,1024]{1,0:T(8,128)(2,1)}, bf16[80,1024]{1,0:T(8,128)(2,1)S(1)}, u32[]{:S(2)}, u32[]{:S(2)}) collective-permute-start(bf16[80,1024]{1,0:T(8,128)(2,1)} %get-tuple-element.124), channel_id=1, source_target_pairs={{0,9},{1,8},{2,11},{3,10},{4,13},{5,12},{6,15},{7,14},{8,1},{9,0},... | collective-permute-start | bytes 491528 | tf_op jit(solution)/shard_map/ppermute | solution.py:188
  51.1 38.9 %copy-start.12 = (bf16[80,1024]{1,0:T(8,128)(2,1)}, bf16[80,1024]{1,0:T(8,128)(2,1)S(1)}, u32[]{:S(2)}) copy-start(bf16[80,1024]{1,0:T(8,128)(2,1)S(1)} %collective-permute-done.14.refs_15_) | copy-start | bytes 491524
  51.1 21.9 %collective-permute-start.9 = (bf16[80,1024]{1,0:T(8,128)(2,1)}, bf16[80,1024]{1,0:T(8,128)(2,1)S(1)}, u32[]{:S(2)}, u32[]{:S(2)}) collective-permute-start(bf16[80,1024]{1,0:T(8,128)(2,1)} %get-tuple-element.125), channel_id=1, source_target_pairs={{0,10},{1,11},{2,8},{3,9},{4,14},{5,15},{6,12},{7,13},{8,2},{9,3},... | collective-permute-start | bytes 491528 | tf_op jit(solution)/shard_map/ppermute | solution.py:188
  62.9 27.1 %copy-start.13 = (bf16[80,1024]{1,0:T(8,128)(2,1)}, bf16[80,1024]{1,0:T(8,128)(2,1)S(1)}, u32[]{:S(2)}) copy-start(bf16[80,1024]{1,0:T(8,128)(2,1)S(1)} %collective-permute-done.7.refs_8_) | copy-start | bytes 491524
  62.9 13.7 %collective-permute-start.2 = (bf16[96,1024]{1,0:T(8,128)(2,1)}, bf16[96,1024]{1,0:T(8,128)(2,1)S(1)}, u32[]{:S(2)}, u32[]{:S(2)}) collective-permute-start(bf16[96,1024]{1,0:T(8,128)(2,1)} %get-tuple-element.118), channel_id=1, source_target_pairs={{0,3},{1,2},{2,1},{3,0},{4,7},{5,6},{6,5},{7,4},{8,11},{9,10},{10,... | collective-permute-start | bytes 589832 | tf_op jit(solution)/shard_map/ppermute | solution.py:188
  69.9 20.2 %copy-start.14 = (bf16[80,1024]{1,0:T(8,128)(2,1)}, bf16[80,1024]{1,0:T(8,128)(2,1)S(1)}, u32[]{:S(2)}) copy-start(bf16[80,1024]{1,0:T(8,128)(2,1)S(1)} %collective-permute-done.8.refs_9_) | copy-start | bytes 491524
  69.9 8.0 %collective-permute-start.3 = (bf16[96,1024]{1,0:T(8,128)(2,1)}, bf16[96,1024]{1,0:T(8,128)(2,1)S(1)}, u32[]{:S(2)}, u32[]{:S(2)}) collective-permute-start(bf16[96,1024]{1,0:T(8,128)(2,1)} %get-tuple-element.119), channel_id=1, source_target_pairs={{0,4},{1,5},{2,6},{3,7},{4,0},{5,1},{6,2},{7,3},{8,12},{9,13},{10,... | collective-permute-start | bytes 589832 | tf_op jit(solution)/shard_map/ppermute | solution.py:188
  73.0 17.1 %copy-start.15 = (bf16[80,1024]{1,0:T(8,128)(2,1)}, bf16[80,1024]{1,0:T(8,128)(2,1)S(1)}, u32[]{:S(2)}) copy-start(bf16[80,1024]{1,0:T(8,128)(2,1)S(1)} %collective-permute-done.9.refs_10_) | copy-start | bytes 491524
  73.0 8.6 %collective-permute-start.4 = (bf16[96,1024]{1,0:T(8,128)(2,1)}, bf16[96,1024]{1,0:T(8,128)(2,1)S(1)}, u32[]{:S(2)}, u32[]{:S(2)}) collective-permute-start(bf16[96,1024]{1,0:T(8,128)(2,1)} %get-tuple-element.120), channel_id=1, source_target_pairs={{0,5},{1,4},{2,7},{3,6},{4,1},{5,0},{6,3},{7,2},{8,13},{9,12},{10,... | collective-permute-start | bytes 589832 | tf_op jit(solution)/shard_map/ppermute | solution.py:188
  74.0 16.1 %copy-start.1 = (bf16[96,1024]{1,0:T(8,128)(2,1)}, bf16[96,1024]{1,0:T(8,128)(2,1)S(1)}, u32[]{:S(2)}) copy-start(bf16[96,1024]{1,0:T(8,128)(2,1)S(1)} %collective-permute-done.refs_1_) | copy-start | bytes 589828
  74.0 12.3 %collective-permute-start.5 = (bf16[96,1024]{1,0:T(8,128)(2,1)}, bf16[96,1024]{1,0:T(8,128)(2,1)S(1)}, u32[]{:S(2)}, u32[]{:S(2)}) collective-permute-start(bf16[96,1024]{1,0:T(8,128)(2,1)} %get-tuple-element.121), channel_id=1, source_target_pairs={{0,6},{1,7},{2,4},{3,5},{4,2},{5,3},{6,0},{7,1},{8,14},{9,15},{10,... | collective-permute-start | bytes 589832 | tf_op jit(solution)/shard_map/ppermute | solution.py:188
  76.1 14.0 %copy-start.2 = (bf16[96,1024]{1,0:T(8,128)(2,1)}, bf16[96,1024]{1,0:T(8,128)(2,1)S(1)}, u32[]{:S(2)}) copy-start(bf16[96,1024]{1,0:T(8,128)(2,1)S(1)} %collective-permute-done.1.refs_2_) | copy-start | bytes 589828
  76.1 13.9 %collective-permute-start.6 = (bf16[96,1024]{1,0:T(8,128)(2,1)}, bf16[96,1024]{1,0:T(8,128)(2,1)S(1)}, u32[]{:S(2)}, u32[]{:S(2)}) collective-permute-start(bf16[96,1024]{1,0:T(8,128)(2,1)} %get-tuple-element.122), channel_id=1, source_target_pairs={{0,7},{1,6},{2,5},{3,4},{4,3},{5,2},{6,1},{7,0},{8,15},{9,14},{10,... | collective-permute-start | bytes 589832 | tf_op jit(solution)/shard_map/ppermute | solution.py:188
  99.1 3.7 %collective-permute-start.15 = (f32[1,128]{1,0:T(1,128)}, f32[1,128]{1,0:T(1,128)S(1)}, u32[]{:S(2)}, u32[]{:S(2)}) collective-permute-start(f32[1,128]{1,0:T(1,128)} %get-tuple-element.133), channel_id=1, source_target_pairs={{0,1},{1,0},{2,3},{3,2},{4,5},{5,4},{6,7},{7,6},{8,9},{9,8},{10,11... | collective-permute-start | bytes 1544 | tf_op jit(solution)/shard_map/ppermute | solution.py:188
  99.3 4.8 %collective-permute-start.16 = (f32[1,128]{1,0:T(1,128)}, f32[1,128]{1,0:T(1,128)S(1)}, u32[]{:S(2)}, u32[]{:S(2)}) collective-permute-start(f32[1,128]{1,0:T(1,128)} %get-tuple-element.134), channel_id=1, source_target_pairs={{0,2},{1,3},{2,0},{3,1},{4,6},{5,7},{6,4},{7,5},{8,10},{9,11},{10,... | collective-permute-start | bytes 1544 | tf_op jit(solution)/shard_map/ppermute | solution.py:188
  100.8 4.7 %collective-permute-start.17 = (f32[1,128]{1,0:T(1,128)}, f32[1,128]{1,0:T(1,128)S(1)}, u32[]{:S(2)}, u32[]{:S(2)}) collective-permute-start(f32[1,128]{1,0:T(1,128)} %get-tuple-element.135), channel_id=1, source_target_pairs={{0,3},{1,2},{2,1},{3,0},{4,7},{5,6},{6,5},{7,4},{8,11},{9,10},{10,... | collective-permute-start | bytes 1544 | tf_op jit(solution)/shard_map/ppermute | solution.py:188
  101.1 6.8 %collective-permute-start.18 = (f32[1,128]{1,0:T(1,128)}, f32[1,128]{1,0:T(1,128)S(1)}, u32[]{:S(2)}, u32[]{:S(2)}) collective-permute-start(f32[1,128]{1,0:T(1,128)} %get-tuple-element.136), channel_id=1, source_target_pairs={{0,4},{1,5},{2,6},{3,7},{4,0},{5,1},{6,2},{7,3},{8,12},{9,13},{10,... | collective-permute-start | bytes 1544 | tf_op jit(solution)/shard_map/ppermute | solution.py:188
  101.2 7.0 %collective-permute-start.19 = (f32[1,128]{1,0:T(1,128)}, f32[1,128]{1,0:T(1,128)S(1)}, u32[]{:S(2)}, u32[]{:S(2)}) collective-permute-start(f32[1,128]{1,0:T(1,128)} %get-tuple-element.137), channel_id=1, source_target_pairs={{0,5},{1,4},{2,7},{3,6},{4,1},{5,0},{6,3},{7,2},{8,13},{9,12},{10,... | collective-permute-start | bytes 1544 | tf_op jit(solution)/shard_map/ppermute | solution.py:188
  102.8 22.5 %copy-start.19 = (f32[1,128]{1,0:T(1,128)}, f32[1,128]{1,0:T(1,128)S(1)}, u32[]{:S(2)}) copy-start(f32[1,128]{1,0:T(1,128)S(1)} %collective-permute-done.15.refs_1_) | copy-start | bytes 1540
  102.8 8.6 %collective-permute-start.20 = (f32[1,128]{1,0:T(1,128)}, f32[1,128]{1,0:T(1,128)S(1)}, u32[]{:S(2)}, u32[]{:S(2)}) collective-permute-start(f32[1,128]{1,0:T(1,128)} %get-tuple-element.138), channel_id=1, source_target_pairs={{0,6},{1,7},{2,4},{3,5},{4,2},{5,3},{6,0},{7,1},{8,14},{9,15},{10,... | collective-permute-start | bytes 1544 | tf_op jit(solution)/shard_map/ppermute | solution.py:188
  104.1 21.2 %copy-start.20 = (f32[1,128]{1,0:T(1,128)}, f32[1,128]{1,0:T(1,128)S(1)}, u32[]{:S(2)}) copy-start(f32[1,128]{1,0:T(1,128)S(1)} %collective-permute-done.16.refs_2_) | copy-start | bytes 1540
  104.1 7.6 %collective-permute-start.21 = (f32[1,128]{1,0:T(1,128)}, f32[1,128]{1,0:T(1,128)S(1)}, u32[]{:S(2)}, u32[]{:S(2)}) collective-permute-start(f32[1,128]{1,0:T(1,128)} %get-tuple-element.139), channel_id=1, source_target_pairs={{0,7},{1,6},{2,5},{3,4},{4,3},{5,2},{6,1},{7,0},{8,15},{9,14},{10,... | collective-permute-start | bytes 1544 | tf_op jit(solution)/shard_map/ppermute | solution.py:188
  105.5 19.8 %copy-start.21 = (f32[1,128]{1,0:T(1,128)}, f32[1,128]{1,0:T(1,128)S(1)}, u32[]{:S(2)}) copy-start(f32[1,128]{1,0:T(1,128)S(1)} %collective-permute-done.17.refs_3_) | copy-start | bytes 1540
  105.5 9.9 %collective-permute-start.22 = (f32[1,128]{1,0:T(1,128)}, f32[1,128]{1,0:T(1,128)S(1)}, u32[]{:S(2)}, u32[]{:S(2)}) collective-permute-start(f32[1,128]{1,0:T(1,128)} %get-tuple-element.140), channel_id=1, source_target_pairs={{0,8},{1,9},{2,10},{3,11},{4,12},{5,13},{6,14},{7,15},{8,0},{9,1},... | collective-permute-start | bytes 1544 | tf_op jit(solution)/shard_map/ppermute | solution.py:188
  107.9 17.5 %copy-start.22 = (f32[1,128]{1,0:T(1,128)}, f32[1,128]{1,0:T(1,128)S(1)}, u32[]{:S(2)}) copy-start(f32[1,128]{1,0:T(1,128)S(1)} %collective-permute-done.18.refs_4_) | copy-start | bytes 1540
  107.9 7.5 %collective-permute-start.23 = (f32[1,128]{1,0:T(1,128)}, f32[1,128]{1,0:T(1,128)S(1)}, u32[]{:S(2)}, u32[]{:S(2)}) collective-permute-start(f32[1,128]{1,0:T(1,128)} %get-tuple-element.141), channel_id=1, source_target_pairs={{0,9},{1,8},{2,11},{3,10},{4,13},{5,12},{6,15},{7,14},{8,1},{9,0},... | collective-permute-start | bytes 1544 | tf_op jit(solution)/shard_map/ppermute | solution.py:188
  108.2 17.2 %copy-start.23 = (f32[1,128]{1,0:T(1,128)}, f32[1,128]{1,0:T(1,128)S(1)}, u32[]{:S(2)}) copy-start(f32[1,128]{1,0:T(1,128)S(1)} %collective-permute-done.19.refs_5_) | copy-start | bytes 1540
  108.2 11.5 %collective-permute-start.24 = (f32[1,128]{1,0:T(1,128)}, f32[1,128]{1,0:T(1,128)S(1)}, u32[]{:S(2)}, u32[]{:S(2)}) collective-permute-start(f32[1,128]{1,0:T(1,128)} %get-tuple-element.142), channel_id=1, source_target_pairs={{0,10},{1,11},{2,8},{3,9},{4,14},{5,15},{6,12},{7,13},{8,2},{9,3},... | collective-permute-start | bytes 1544 | tf_op jit(solution)/shard_map/ppermute | solution.py:188
  111.5 8.9 %collective-permute-start.25 = (f32[1,128]{1,0:T(1,128)}, f32[1,128]{1,0:T(1,128)S(1)}, u32[]{:S(2)}, u32[]{:S(2)}) collective-permute-start(f32[1,128]{1,0:T(1,128)} %get-tuple-element.143), channel_id=1, source_target_pairs={{0,11},{1,10},{2,9},{3,8},{4,15},{5,14},{6,13},{7,12},{8,3},{9,2},... | collective-permute-start | bytes 1544 | tf_op jit(solution)/shard_map/ppermute | solution.py:188
  111.8 8.7 %collective-permute-start.26 = (f32[1,128]{1,0:T(1,128)}, f32[1,128]{1,0:T(1,128)S(1)}, u32[]{:S(2)}, u32[]{:S(2)}) collective-permute-start(f32[1,128]{1,0:T(1,128)} %get-tuple-element.144), channel_id=1, source_target_pairs={{0,12},{1,13},{2,14},{3,15},{4,8},{5,9},{6,10},{7,11},{8,4},{9,5},... | collective-permute-start | bytes 1544 | tf_op jit(solution)/shard_map/ppermute | solution.py:188
  115.4 5.0 %collective-permute-start.27 = (f32[1,128]{1,0:T(1,128)}, f32[1,128]{1,0:T(1,128)S(1)}, u32[]{:S(2)}, u32[]{:S(2)}) collective-permute-start(f32[1,128]{1,0:T(1,128)} %get-tuple-element.145), channel_id=1, source_target_pairs={{0,13},{1,12},{2,15},{3,14},{4,9},{5,8},{6,11},{7,10},{8,5},{9,4},... | collective-permute-start | bytes 1544 | tf_op jit(solution)/shard_map/ppermute | solution.py:188
  115.4 6.3 %collective-permute-start.28 = (f32[1,128]{1,0:T(1,128)}, f32[1,128]{1,0:T(1,128)S(1)}, u32[]{:S(2)}, u32[]{:S(2)}) collective-permute-start(f32[1,128]{1,0:T(1,128)} %get-tuple-element.146), channel_id=1, source_target_pairs={{0,14},{1,15},{2,12},{3,13},{4,10},{5,11},{6,8},{7,9},{8,6},{9,7},... | collective-permute-start | bytes 1544 | tf_op jit(solution)/shard_map/ppermute | solution.py:188
  119.6 5.7 %collective-permute-start.29 = (f32[1,128]{1,0:T(1,128)}, f32[1,128]{1,0:T(1,128)S(1)}, u32[]{:S(2)}, u32[]{:S(2)}) collective-permute-start(f32[1,128]{1,0:T(1,128)} %get-tuple-element.147), channel_id=1, source_target_pairs={{0,15},{1,14},{2,13},{3,12},{4,11},{5,10},{6,9},{7,8},{8,7},{9,6},... | collective-permute-start | bytes 1544 | tf_op jit(solution)/shard_map/ppermute | solution.py:188
  (16 other events, 112.2 us)

commit v4 on v3

v4 whole, which is shorter than its diff:
```python
import functools

import jax
import jax.numpy as jnp
from jax import lax
from jax.experimental import pallas as pl
from jax.experimental.pallas import tpu as pltpu
from jax.sharding import PartitionSpec as P

CL_DEV = 8
SLOT = 16
LANES = 128
SIZE = 80
TILE = 1280
STEP = 256
MB = 1024 * 1024
BF = jnp.bfloat16
F32 = jnp.float32
ANY = pl.BlockSpec(memory_space=pltpu.HBM)
IN_VMEM = pl.BlockSpec(memory_space=pltpu.VMEM)


def iota(shape, dim):
    return lax.broadcasted_iota(jnp.int32, shape, dim)


def bits(mask):
    return mask.astype(F32).astype(BF)


def product(left, right):
    return jnp.dot(left, right, preferred_element_type=F32)


def product_t(left, right):
    return lax.dot_general(left, right, (((1,), (1,)), ((), ())), preferred_element_type=F32)


def before():
    return bits(iota((LANES, LANES), 0) < iota((LANES, LANES), 1))


def fill(choose, dest, begin):
    index = iota((choose.shape[0], LANES), 0) + begin
    for line in range(dest.shape[0]):
        at = slice(line * LANES, (line + 1) * LANES)
        choose[:, at] = bits(index == dest[line : line + 1])


def first_kernel(
    owners, cid_ref, valid_ref, rows_ref, blocks_ref, rest_ref, dest_ref, code_ref, held, unit, choose, out, in_sems, out_sems
):
    rows, width = held.shape
    total, early = out.shape
    tile = choose.shape[0]
    lines = rows // LANES
    parts = rows // STEP
    loads = []
    for part in range(parts):
        at = pl.ds(part * STEP, STEP)
        loads.append(pltpu.make_async_copy(rows_ref.at[at], held.at[at], in_sems.at[part]))
        loads[-1].start()

    cid = cid_ref[...]
    live = valid_ref[...] == 1
    owner = lax.shift_right_logical(cid, 3)
    name = (cid & (CL_DEV - 1)) + 1
    target = jnp.where(live, owner, -1)
    index = iota((owners, LANES), 0)
    mine = [(index == target[line : line + 1]).astype(F32) for line in range(lines)]
    stacked = jnp.concatenate(mine, axis=0).astype(BF)
    inside = product(stacked, before())
    whole = product(stacked, jnp.ones((LANES, LANES), BF))
    offset = jnp.zeros((owners, LANES), F32)
    ranks = []
    for line in range(lines):
        at = slice(line * owners, (line + 1) * owners)
        ranks.append(jnp.sum(mine[line] * (inside[at] + offset), axis=0, keepdims=True))
        offset = offset + whole[at]
    pos = jnp.concatenate(ranks, axis=0).astype(jnp.int32)
    fits = live & (pos < SIZE - 1)
    lost = jnp.max((live & (pos >= SIZE - 1)).astype(F32))
    code = jnp.where(fits, pos, LANES - 1)
    code_ref[...] = code
    dest = jnp.where(fits, owner * SIZE + pos, -1)
    dest_ref[...] = dest

    names = jnp.concatenate(
        [mine[line] * name[line : line + 1].astype(F32) for line in range(lines)], axis=1
    ).astype(BF)
    index = iota((LANES, LANES), 0)
    places = jnp.concatenate([bits(index == code[line : line + 1]) for line in range(lines)], axis=1)
    meta = product_t(names, places)
    meta = jnp.where(iota((owners, LANES), 1) == LANES - 1, lost, meta).astype(BF)

    fill(choose, dest, 0)
    for part in range(parts):
        loads[part].wait()

        def one_chunk(number, carry):
            at = pl.ds(pl.multiple_of(part * STEP + number * 64, 64), 64)
            values = held[at, :].astype(F32)
            squares = jnp.sum(values * values, axis=1, keepdims=True)
            unit[at, :] = (values * lax.rsqrt(squares + 1e-06)).astype(BF)
            return carry

        lax.fori_loop(0, STEP // 64, one_chunk, 0)

    stores = [pltpu.make_async_copy(unit.at[:, pl.ds(early, width - early)], rest_ref, out_sems.at[0])]
    stores[0].start()
    for first in range(0, total, tile):
        if first:
            fill(choose, dest, first)
        for column in range(0, early, STEP):
            at = slice(column, column + STEP)
            packed = product(choose[...], unit[:, at])
            if column == 0:
                line = iota((tile, owners), 0) + first
                last = (iota((1, owners), 1) + 1) * SIZE - 1
                packed = jnp.concatenate(
                    [packed[:, :LANES] + product(bits(line == last), meta), packed[:, LANES:]], axis=1
                )
            out[pl.ds(first, tile), at] = packed.astype(BF)
            where = (pl.ds(first, tile), at)
            stores.append(
                pltpu.make_async_copy(out.at[where], blocks_ref.at[where], out_sems.at[len(stores)])
            )
            stores[-1].start()
    for store in stores:
        store.wait()


def second_kernel(dest_ref, unit_ref, blocks_ref, choose, out, sems):
    total, late = out.shape
    tile = choose.shape[0]
    stores = []
    for first in range(0, total, tile):
        fill(choose, dest_ref[...], first)
        out[pl.ds(first, tile), :] = product(choose[...], unit_ref[...]).astype(BF)
        at = pl.ds(first, tile)
        stores.append(pltpu.make_async_copy(out.at[at], blocks_ref.at[at], sems.at[len(stores)]))
        stores[-1].start()
    for store in stores:
        store.wait()


def early_of(width):
    return width * 3 // 4


def pack(embeddings, cluster_id, valid, owners):
    rows, width = embeddings.shape
    early = early_of(width)
    total = owners * SIZE
    tile = min(total, TILE)
    lines = (rows // LANES, LANES)
    blocks, rest, dest, code = pl.pallas_call(
        functools.partial(first_kernel, owners),
        out_shape=(
            pltpu.HBM((total, early), BF),
            pltpu.HBM((rows, width - early), BF),
            jax.ShapeDtypeStruct(lines, jnp.int32),
            jax.ShapeDtypeStruct(lines, jnp.int32),
        ),
        in_specs=[IN_VMEM, IN_VMEM, ANY],
        out_specs=(ANY, ANY, IN_VMEM, IN_VMEM),
        scratch_shapes=[
            pltpu.VMEM((rows, width), BF),
            pltpu.VMEM((rows, width), BF),
            pltpu.VMEM((tile, rows), BF),
            pltpu.VMEM((total, early), BF),
            pltpu.SemaphoreType.DMA((rows // STEP,)),
            pltpu.SemaphoreType.DMA((1 + total // tile * (early // STEP),)),
        ],
        compiler_params=pltpu.CompilerParams(vmem_limit_bytes=48 * MB),
        name="pack_first",
    )(cluster_id.reshape(lines), valid.reshape(lines), embeddings)
    later = pl.pallas_call(
        second_kernel,
        out_shape=pltpu.HBM((total, width - early), BF),
        in_specs=[IN_VMEM, IN_VMEM],
        out_specs=ANY,
        scratch_shapes=[
            pltpu.VMEM((tile, rows), BF),
            pltpu.VMEM((total, width - early), BF),
            pltpu.SemaphoreType.DMA((total // tile,)),
        ],
        compiler_params=pltpu.CompilerParams(vmem_limit_bytes=40 * MB),
        name="pack_second",
    )(dest, rest)
    return blocks, later, code


def load_tags(owners, got_ref, tags, sem):
    return pltpu.make_async_copy(got_ref.at[:, pl.ds(SIZE - 16, 16), pl.ds(0, LANES)], tags, sem)


def read_tags(owners, tags, lost_ref, side, top):
    flat = tags[...].reshape(owners * 16, LANES)
    pick = bits(iota((owners, owners * 16), 1) == iota((owners, owners * 16), 0) * 16 + 15)
    names = product(pick, flat)
    lost = jnp.max(jnp.where(iota((owners, LANES), 1) == LANES - 1, names, 0.0))
    lost_ref[0, 0] = (lost > 0.0).astype(jnp.int32)
    names = names.astype(BF)
    count = owners * SIZE
    base = iota((count, 1), 0)
    wide = product(bits(iota((count, owners), 1) == base // SIZE), names)
    wide = jnp.where(iota((count, LANES), 1) == base % SIZE, wide, 0.0).astype(BF)
    found = product(wide, jnp.ones((LANES, LANES), BF))
    side[...] = jnp.where(found == 0.0, -1.0, found)
    base = iota((1, count), 1)
    wide = product(names, bits(iota((LANES, count), 0) == base % SIZE))
    wide = jnp.where(iota((owners, count), 0) == base // SIZE, wide, 0.0)
    top[...] = jnp.sum(wide, axis=0, keepdims=True)


def masked(scores, side, tops, block, part, square):
    allowed = side[block * LANES : (block + 1) * LANES, :] == tops[:, part * LANES : (part + 1) * LANES]
    if square is not None:
        unlike = iota((LANES, LANES), 0) != iota((LANES, LANES), 1)
        allowed = allowed & (unlike | square)
    here = scores[block * LANES : (block + 1) * LANES, part * LANES : (part + 1) * LANES]
    return jnp.where(allowed, here, -4.0)


def fetch_rows(got_ref, rows, sems):
    moves = []
    for source in range(got_ref.shape[0]):
        moves.append(
            pltpu.make_async_copy(
                got_ref.at[source], rows.at[pl.ds(source * SIZE, SIZE)], sems.at[source]
            )
        )
        moves[-1].start()
    return moves


def give_back(owners, line, best_ref):
    total = line.shape[1]
    for source in range(owners):
        base, shift = divmod(source * SIZE, LANES)
        base *= LANES
        piece = line[:, base : min(base + 2 * LANES, total)]
        if shift:
            piece = pltpu.roll(piece, piece.shape[1] - shift, 1)
        best_ref[source] = piece[:, :LANES]


def spans(total):
    return [(first, min(STEP, total - first)) for first in range(0, total, STEP)]


def part_kernel(owners, got_ref, part_ref, lost_ref, tags, rows, side, top, sems):
    total = rows.shape[0]
    tag_copy = load_tags(owners, got_ref, tags, sems.at[owners])
    tag_copy.start()
    moves = fetch_rows(got_ref, rows, sems)
    tag_copy.wait()
    read_tags(owners, tags, lost_ref, side, top)
    for move in moves:
        move.wait()
    for first, span in spans(total):
        scores = product_t(rows[...], rows[first : first + span, :])
        tops = top[:, first : first + span]
        for block in range(total // LANES):
            for part in range(span // LANES):
                square = False if block * LANES == first + part * LANES else None
                part_ref[
                    block * LANES : (block + 1) * LANES,
                    first + part * LANES : first + (part + 1) * LANES,
                ] = masked(scores, side, tops, block, part, square)


def last_kernel(owners, got_ref, part_ref, best_ref, rows, line, sems):
    total = rows.shape[0]
    for move in fetch_rows(got_ref, rows, sems):
        move.wait()
    for first, span in spans(total):
        scores = product_t(rows[...], rows[first : first + span, :])
        result = jnp.full((8, span), -1.0, F32)
        for block in range(total // 8):
            at = slice(block * 8, (block + 1) * 8)
            result = jnp.maximum(result, scores[at] + part_ref[at, first : first + span])
        line[:, first : first + span] = jnp.max(result, axis=0, keepdims=True)
    give_back(owners, line, best_ref)


def score(got, later, owners):
    early, late = got.shape[2], later.shape[2]
    total = owners * SIZE
    part, lost = pl.pallas_call(
        functools.partial(part_kernel, owners),
        out_shape=(
            jax.ShapeDtypeStruct((total, total), F32),
            jax.ShapeDtypeStruct((1, 1), jnp.int32),
        ),
        in_specs=[ANY],
        out_specs=(IN_VMEM, pl.BlockSpec(memory_space=pltpu.SMEM)),
        scratch_shapes=[
            pltpu.VMEM((owners, 16, LANES), BF),
            pltpu.VMEM((total, early), BF),
            pltpu.VMEM((total, LANES), F32),
            pltpu.VMEM((1, total), F32),
            pltpu.SemaphoreType.DMA((owners + 1,)),
        ],
        compiler_params=pltpu.CompilerParams(vmem_limit_bytes=32 * MB),
        name="score_first",
    )(got)
    best = pl.pallas_call(
        functools.partial(last_kernel, owners),
        out_shape=jax.ShapeDtypeStruct((owners, 1, LANES), F32),
        in_specs=[ANY, IN_VMEM],
        out_specs=IN_VMEM,
        scratch_shapes=[
            pltpu.VMEM((total, late), BF),
            pltpu.VMEM((1, total), F32),
            pltpu.SemaphoreType.DMA((owners,)),
        ],
        compiler_params=pltpu.CompilerParams(vmem_limit_bytes=32 * MB),
        name="score_second",
    )(later, part)
    return best, lost


def whole_kernel(owners, got_ref, later_ref, best_ref, lost_ref, tags, rows, rest, side, top, line, sems, late_sems):
    total = rows.shape[0]
    tag_copy = load_tags(owners, got_ref, tags, sems.at[owners])
    tag_copy.start()
    moves = fetch_rows(got_ref, rows, sems) + fetch_rows(later_ref, rest, late_sems)
    tag_copy.wait()
    read_tags(owners, tags, lost_ref, side, top)
    for move in moves:
        move.wait()

    @pl.loop(0, total // STEP)
    def _(number):
        here = pl.ds(pl.multiple_of(number * STEP, STEP), STEP)
        tops = top[:, here]
        scores = product_t(rows[...], rows[here, :]) + product_t(rest[...], rest[here, :])
        pieces = []
        for part in range(STEP // LANES):
            result = jnp.full((1, LANES), -1.0, F32)
            for block in range(total // LANES):
                square = block != number * (STEP // LANES) + part
                found = masked(scores, side, tops, block, part, square)
                result = jnp.maximum(result, jnp.max(found, axis=0, keepdims=True))
            pieces.append(result)
        line[:, here] = jnp.concatenate(pieces, axis=1)

    give_back(owners, line, best_ref)


def score_whole(got, later, owners):
    early, late = got.shape[2], later.shape[2]
    total = owners * SIZE
    return pl.pallas_call(
        functools.partial(whole_kernel, owners),
        out_shape=(
            jax.ShapeDtypeStruct((owners, 1, LANES), F32),
            jax.ShapeDtypeStruct((1, 1), jnp.int32),
        ),
        in_specs=[ANY, ANY],
        out_specs=(IN_VMEM, pl.BlockSpec(memory_space=pltpu.SMEM)),
        scratch_shapes=[
            pltpu.VMEM((owners, 16, LANES), BF),
            pltpu.VMEM((total, early), BF),
            pltpu.VMEM((total, late), BF),
            pltpu.VMEM((total, LANES), F32),
            pltpu.VMEM((1, total), F32),
            pltpu.VMEM((1, total), F32),
            pltpu.SemaphoreType.DMA((owners + 1,)),
            pltpu.SemaphoreType.DMA((owners,)),
        ],
        compiler_params=pltpu.CompilerParams(vmem_limit_bytes=48 * MB),
        name="score_whole",
    )(got, later)


def place_kernel(owners, back_ref, cid_ref, code_ref, valid_ref, out_ref):
    for start in range(0, cid_ref.shape[0], 8):
        at = slice(start, start + 8)
        owner = lax.shift_right_logical(cid_ref[at, :], 3)
        code = code_ref[at, :]
        result = jnp.zeros((8, LANES), F32)
        for source in range(owners):
            line = jnp.broadcast_to(back_ref[source], (8, LANES))
            value = jnp.take_along_axis(line, code, axis=1, mode="promise_in_bounds")
            result = jnp.where(owner == source, value, result)
        out_ref[at, :] = jnp.where(valid_ref[at, :] == 1, result, 0.0)


def place(back, cluster_id, code, valid, owners):
    rows = cluster_id.shape[0]
    shape = (rows // LANES, LANES)
    return pl.pallas_call(
        functools.partial(place_kernel, owners),
        out_shape=jax.ShapeDtypeStruct(shape, F32),
        name="place",
    )(back, cluster_id.reshape(shape), code, valid.reshape(shape)).reshape(rows)


def every_slot(embeddings, cluster_id, valid, owners):
    width = embeddings.shape[1]
    clusters = CL_DEV * owners
    values = embeddings.astype(F32)
    squares = jnp.sum(values * values, axis=1, keepdims=True)
    unit_rows = (values * lax.rsqrt(squares + 1e-06)).astype(BF)
    one_hot = (cluster_id[:, None] == jnp.arange(clusters, dtype=jnp.int32)[None, :]).astype(jnp.int32)
    ranking = jnp.sum(jnp.cumsum(one_hot, axis=0) * one_hot, axis=1) - 1
    target = cluster_id * SLOT + ranking
    outgoing = jnp.zeros((clusters * SLOT, width), BF).at[target].set(unit_rows)
    live_out = jnp.zeros((clusters * SLOT,), BF).at[target].set(valid.astype(BF))
    got = lax.all_to_all(
        outgoing.reshape(owners, CL_DEV * SLOT, width), "owners", split_axis=0, concat_axis=0, tiled=True
    )
    live = lax.all_to_all(
        live_out.reshape(owners, CL_DEV, SLOT), "owners", split_axis=0, concat_axis=0, tiled=True
    )
    got = got.reshape(owners, CL_DEV, SLOT, width).transpose(1, 0, 2, 3)
    got = got.reshape(CL_DEV, owners * SLOT, width)
    live = live.transpose(1, 0, 2).reshape(CL_DEV, owners * SLOT) > 0.5
    diagonal = jnp.eye(owners * SLOT, dtype=bool)

    def one_cluster(args):
        rows, flags = args
        scores = jnp.einsum("md,nd->mn", rows, rows, preferred_element_type=F32)
        allowed = flags[:, None] & flags[None, :] & ~diagonal
        return jnp.max(jnp.where(allowed, scores, -1.0), axis=1)

    best = lax.map(one_cluster, (got, live)).reshape(CL_DEV, owners, SLOT).transpose(1, 0, 2)
    back = lax.all_to_all(best, "owners", split_axis=0, concat_axis=0, tiled=True)
    return jnp.where(valid == 1, back.reshape(-1)[target], 0.0)


def swap(blocks, owners):
    split = blocks.reshape(owners, blocks.shape[0] // owners, blocks.shape[1])
    return lax.all_to_all(split, "owners", split_axis=0, concat_axis=0, tiled=True)


def shards(embeddings, cluster_id, valid):
    owners = lax.axis_size("owners")
    blocks, later, code = pack(embeddings, cluster_id, valid, owners)
    got = swap(blocks, owners)
    later = swap(later, owners)
    scoring = score if owners * SIZE <= 2048 else score_whole
    best, lost = scoring(got, later, owners)
    back = lax.all_to_all(best, "owners", split_axis=0, concat_axis=0, tiled=True)
    nearest = place(back, cluster_id, code, valid, owners)
    return lax.cond(
        lost[0, 0] > 0,
        lambda: every_slot(embeddings, cluster_id, valid, owners),
        lambda: nearest,
    )


def solution(mesh):
    placed = (P(("groups", "owners"), None), P(("groups", "owners")), P(("groups", "owners")))
    return jax.shard_map(
        shards, mesh=mesh, in_specs=placed, out_specs=P(("groups", "owners")), check_vma=False
    )
```

time: 128 us -> 102 us (0.80)
  starting transfers between devices: 63.5 us -> 23 us
  waiting for transfers between devices: 41.4 us -> 50.3 us
  local copies, waits for them, and re-layouts: 1.74 us -> 7.37 us
    ppermute x30 -> x0, starting transfers between devices: 63.5 us -> none  [swap(): return lax.ppermute(block, 'owners', [(i, i ^ k) for i in range(owners)])]
    all_to_all x0 -> x3, waiting for transfers between devices: none -> 50.3 us  [the longest x2 44.6 us: swap(): lax.all_to_all(split, 'owners', split_axis=0, concat_axis=0, tiled=True)]
    ppermute x30 -> x0, waiting for transfers between devices: 41.4 us -> none  [swap(): return lax.ppermute(block, 'owners', [(i, i ^ k) for i in range(owners)])]
    all_to_all x0 -> x3, starting transfers between devices: none -> 23 us  [the longest x2 18.2 us: swap(): lax.all_to_all(split, 'owners', split_axis=0, concat_axis=0, tiled=True)]
    unnamed x68 -> x16, local copies, waits for them, and re-layouts: 1.74 us -> 7.37 us
    pallas_call x2 -> x4, Pallas kernels: 19 us -> 18.7 us  [the longest x1 7.91 us: pack(): pl.pallas_call(functools.partial(first_kernel, owners), out_shape=(pltpu....]
  transfers between devices with their start and end apart: 30 -> 3, of which waited for: 9 -> 3; matrix products, arithmetic and copies ran while one was open for 0% -> 0% of each run, Pallas kernels for 0% -> 8%
where the time goes in v4:
time: 102 us; the launch traced here: 101 us
  waiting for transfers between devices  50.3 us (49%)
  starting transfers between devices  23 us (23%)
  Pallas kernels  19.5 us (19%)
  local copies, waits for them, and re-layouts  7.37 us (7%)
    all_to_all x2, waiting for transfers between devices, swap(): lax.all_to_all(split, 'owners', split_axis=0, concat_axis=0, tiled=True)  44.6 us
    all_to_all x2, starting transfers between devices, swap(): lax.all_to_all(split, 'owners', split_axis=0, concat_axis=0, tiled=True)  18.2 us
    pallas_call x1, Pallas kernels, pack(): pl.pallas_call(functools.partial(first_kernel, owners), out_shape=(pltpu....  7.91 us
    unnamed x16, local copies, waits for them, and re-layouts  7.37 us
    pallas_call x1, Pallas kernels, score(): pl.pallas_call(functools.partial(part_kernel, owners), out_shape=(jax.Sha...  6.13 us
    all_to_all x1, waiting for transfers between devices, shards(): lax.all_to_all(best, 'owners', split_axis=0, concat_axis=0, tiled=True)  5.72 us
    all_to_all x1, starting transfers between devices, shards(): lax.all_to_all(best, 'owners', split_axis=0, concat_axis=0, tiled=True)  4.79 us
    pallas_call x1, Pallas kernels, score(): pl.pallas_call(functools.partial(last_kernel, owners), out_shape=jax.Shap...  2.72 us
  transfers between devices with their start and end apart: 3, of which 3 were waited for; matrix products, arithmetic and copies ran while one was open for 0% of the time, Pallas kernels for 8%

profile of v4, /device:TPU:0, one launch (start us, length us, event | category | flops | bytes accessed | tf_op | source)
XLA Modules:
  0.0 101.2 jit_solution(3770318287635702410)
XLA Ops:
  0.0 7.9 %pack_first.1 = (bf16[1280,768]{1,0:T(8,128)(2,1)}, bf16[1024,256]{1,0:T(8,128)(2,1)}, s32[8,128]{1,0:T(8,128)S(1)}, s32[8,128]{1,0:T(8,128)S(1)}) custom-call(s32[8,128]{1,0:T(8,128)} %bitcast.38, s32[8,128]{1,0:T(8,128)} %bitcast.41, bf16[1024,1024]{1,0:T(8,128)(2,1)} %rows_ref.1), custom_call_target="tpu_custom_call" | custom-call | tf_op jit(solution)/shard_map/pack_first/pallas_call | solution.py:157
  7.9 0.0 copy-start.3
  7.9 0.6 copy-done.3
  8.5 0.0 copy-start.2
  8.5 7.5 %all-to-all-start.3 = ((bf16[16,80,768]{2,1,0:T(8,128)(2,1)}), bf16[16,80,768]{2,1,0:T(8,128)(2,1)S(1)}, u32[]{:S(2)}, u32[]{:S(2)}) async-start(bf16[16,80,768]{2,1,0:T(8,128)(2,1)} %bitcast.36), calls=%async_computation.3 | async-start | bytes 3932160 | tf_op jit(solution)/shard_map/all_to_all | solution.py:437
  16.0 0.0 copy-done.2
  16.1 1.9 %pack_second.1 = bf16[1280,256]{1,0:T(8,128)(2,1)} custom-call(s32[8,128]{1,0:T(8,128)S(1)} %get-tuple-element.89.dest_ref, bf16[1024,256]{1,0:T(8,128)(2,1)S(1)} %copy-done.2), custom_call_target="tpu_custom_call" | custom-call | tf_op jit(solution)/shard_map/pack_second/pallas_call | solution.py:178
  18.0 36.9 %all-to-all-done.3.got_ref = bf16[16,80,768]{2,1,0:T(8,128)(2,1)S(1)} async-done(((bf16[16,80,768]{2,1,0:T(8,128)(2,1)}), bf16[16,80,768]{2,1,0:T(8,128)(2,1)S(1)}, u32[]{:S(2)}, u32[]{:S(2)}) %all-to-all-start.3) | async-done | bytes 1966112 | tf_op jit(solution)/shard_map/all_to_all | solution.py:437
  54.9 10.7 %all-to-all-start.4 = ((bf16[16,80,256]{2,1,0:T(8,128)(2,1)}), bf16[16,80,256]{2,1,0:T(8,128)(2,1)S(1)}, u32[]{:S(2)}, u32[]{:S(2)}) async-start(bf16[16,80,256]{2,1,0:T(8,128)(2,1)} %bitcast.35), calls=%async_computation.4 | async-start | bytes 1310720 | tf_op jit(solution)/shard_map/all_to_all | solution.py:437
  65.6 0.0 copy-start.5
  65.6 0.0 copy-start.6
  65.6 6.1 %score_first.1 = (f32[1280,1280]{1,0:T(8,128)S(1)}, s32[1,1]{1,0:T(1,128)}) custom-call(bf16[16,80,768]{2,1,0:T(8,128)(2,1)S(1)} %all-to-all-done.3.got_ref), custom_call_target="tpu_custom_call" | custom-call | tf_op jit(solution)/shard_map/score_first/pallas_call | solution.py:291
  71.7 0.0 copy-start
  71.7 2.7 %copy-done = f32[1280,1280]{1,0:T(8,128)} copy-done((f32[1280,1280]{1,0:T(8,128)}, f32[1280,1280]{1,0:T(8,128)S(1)}, u32[]{:S(2)}) %copy-start) | copy-done | bytes 6553624
  74.5 7.7 %all-to-all-done.4.got_ref = bf16[16,80,256]{2,1,0:T(8,128)(2,1)S(1)} async-done(((bf16[16,80,256]{2,1,0:T(8,128)(2,1)}), bf16[16,80,256]{2,1,0:T(8,128)(2,1)S(1)}, u32[]{:S(2)}, u32[]{:S(2)}) %all-to-all-start.4) | async-done | bytes 655392 | tf_op jit(solution)/shard_map/all_to_all | solution.py:437
  82.2 0.0 copy-start.1
  82.2 2.9 %copy-done.1 = f32[1280,1280]{1,0:T(8,128)S(1)} copy-done((f32[1280,1280]{1,0:T(8,128)S(1)}, f32[1280,1280]{1,0:T(8,128)}, u32[]{:S(2)}) %copy-start.1) | copy-done | bytes 6553624
  85.0 2.7 %score_second.1 = f32[16,1,128]{2,1,0:T(1,128)} custom-call(bf16[16,80,256]{2,1,0:T(8,128)(2,1)S(1)} %all-to-all-done.4.got_ref, f32[1280,1280]{1,0:T(8,128)S(1)} %copy-done.1), custom_call_target="tpu_custom_call" | custom-call | tf_op jit(solution)/shard_map/score_second/pallas_call | solution.py:309
  87.7 4.8 %all-to-all-start.5 = ((f32[16,1,128]{2,1,0:T(1,128)}), f32[16,1,128]{2,1,0:T(1,128)S(1)}, u32[]{:S(2)}, u32[]{:S(2)}) async-start(f32[16,1,128]{2,1,0:T(1,128)} %score_second.1), calls=%async_computation.5 | async-start | bytes 16384 | tf_op jit(solution)/shard_map/all_to_all | solution.py:447
  93.2 5.7 %all-to-all-done.5.back_ref = f32[16,1,128]{2,1,0:T(1,128)S(1)} async-done(((f32[16,1,128]{2,1,0:T(1,128)}), f32[16,1,128]{2,1,0:T(1,128)S(1)}, u32[]{:S(2)}, u32[]{:S(2)}) %all-to-all-start.5) | async-done | bytes 8224 | tf_op jit(solution)/shard_map/all_to_all | solution.py:447
  98.9 0.0 copy-start.7
  98.9 0.6 copy-done.7
  99.5 0.0 copy-done.5
  99.5 0.0 copy-done.6
  99.5 0.8 place.1
  100.3 0.2 conditional.1
  100.6 0.0 copy-start.8
  100.6 0.6 copy-done.8
Async XLA Ops:
  7.9 0.6 copy-start.3
  8.5 7.5 %copy-start.2 = (bf16[1024,256]{1,0:T(8,128)(2,1)S(1)}, bf16[1024,256]{1,0:T(8,128)(2,1)}, u32[]{:S(2)}) copy-start(bf16[1024,256]{1,0:T(8,128)(2,1)} %get-tuple-element.90.unit_ref) | copy-start | bytes 1572868
  8.5 46.3 %all-to-all-start.3 = ((bf16[16,80,768]{2,1,0:T(8,128)(2,1)}), bf16[16,80,768]{2,1,0:T(8,128)(2,1)S(1)}, u32[]{:S(2)}, u32[]{:S(2)}) async-start(bf16[16,80,768]{2,1,0:T(8,128)(2,1)} %bitcast.36), calls=%async_computation.3 | async-start | bytes 3932160 | tf_op jit(solution)/shard_map/all_to_all | solution.py:437
  54.9 27.3 %all-to-all-start.4 = ((bf16[16,80,256]{2,1,0:T(8,128)(2,1)}), bf16[16,80,256]{2,1,0:T(8,128)(2,1)S(1)}, u32[]{:S(2)}, u32[]{:S(2)}) async-start(bf16[16,80,256]{2,1,0:T(8,128)(2,1)} %bitcast.35), calls=%async_computation.4 | async-start | bytes 1310720 | tf_op jit(solution)/shard_map/all_to_all | solution.py:437
  65.6 34.0 %copy-start.5 = (s32[1024]{0:T(1024)S(1)}, s32[1024]{0:T(1024)}, u32[]{:S(2)}) copy-start(s32[1024]{0:T(1024)} %param.8) | copy-start | bytes 12292
  65.6 34.0 %copy-start.6 = (s32[1024]{0:T(1024)S(1)}, s32[1024]{0:T(1024)}, u32[]{:S(2)}) copy-start(s32[1024]{0:T(1024)} %param.9) | copy-start | bytes 12292
  71.7 2.7 %copy-start = (f32[1280,1280]{1,0:T(8,128)}, f32[1280,1280]{1,0:T(8,128)S(1)}, u32[]{:S(2)}) copy-start(f32[1280,1280]{1,0:T(8,128)S(1)} %get-tuple-element.91.part_ref) | copy-start | bytes 19660804
  82.2 2.9 %copy-start.1 = (f32[1280,1280]{1,0:T(8,128)S(1)}, f32[1280,1280]{1,0:T(8,128)}, u32[]{:S(2)}) copy-start(f32[1280,1280]{1,0:T(8,128)} %copy-done) | copy-start | bytes 19660804
  87.7 11.2 %all-to-all-start.5 = ((f32[16,1,128]{2,1,0:T(1,128)}), f32[16,1,128]{2,1,0:T(1,128)S(1)}, u32[]{:S(2)}, u32[]{:S(2)}) async-start(f32[16,1,128]{2,1,0:T(1,128)} %score_second.1), calls=%async_computation.5 | async-start | bytes 16384 | tf_op jit(solution)/shard_map/all_to_all | solution.py:447
  98.9 0.6 copy-start.7
  100.6 0.6 copy-start.8

commit v5 on v3

v5 whole, which is shorter than its diff:
```python
import functools

import jax
import jax.numpy as jnp
from jax import lax
from jax.experimental import pallas as pl
from jax.experimental.pallas import tpu as pltpu
from jax.sharding import PartitionSpec as P

CL_DEV = 8
SLOT = 16
LANES = 128
SIZE = 80
TILE = 1280
STEP = 256
MB = 1024 * 1024
BF = jnp.bfloat16
F32 = jnp.float32
ANY = pl.BlockSpec(memory_space=pltpu.HBM)
IN_VMEM = pl.BlockSpec(memory_space=pltpu.VMEM)


def iota(shape, dim):
    return lax.broadcasted_iota(jnp.int32, shape, dim)


def bits(mask):
    return mask.astype(F32).astype(BF)


def product(left, right):
    return jnp.dot(left, right, preferred_element_type=F32)


def product_t(left, right):
    return lax.dot_general(left, right, (((1,), (1,)), ((), ())), preferred_element_type=F32)


def before():
    return bits(iota((LANES, LANES), 0) < iota((LANES, LANES), 1))


def fill(choose, dest, begin):
    index = iota((choose.shape[0], LANES), 0) + begin
    for line in range(dest.shape[0]):
        at = slice(line * LANES, (line + 1) * LANES)
        choose[:, at] = bits(index == dest[line : line + 1])


def pack_kernel(
    owners, cid_ref, valid_ref, rows_ref, blocks_ref, code_ref, held, unit, choose, out, in_sems, out_sems
):
    rows, width = held.shape
    total = out.shape[0]
    tile = choose.shape[0]
    lines = rows // LANES
    parts = rows // STEP
    loads = []
    for part in range(parts):
        at = pl.ds(part * STEP, STEP)
        loads.append(pltpu.make_async_copy(rows_ref.at[at], held.at[at], in_sems.at[part]))
        loads[-1].start()

    cid = cid_ref[...]
    live = valid_ref[...] == 1
    owner = lax.shift_right_logical(cid, 3)
    name = (cid & (CL_DEV - 1)) + 1
    target = jnp.where(live, owner, -1)
    index = iota((owners, LANES), 0)
    mine = [(index == target[line : line + 1]).astype(F32) for line in range(lines)]
    stacked = jnp.concatenate(mine, axis=0).astype(BF)
    inside = product(stacked, before())
    whole = product(stacked, jnp.ones((LANES, LANES), BF))
    offset = jnp.zeros((owners, LANES), F32)
    ranks = []
    for line in range(lines):
        at = slice(line * owners, (line + 1) * owners)
        ranks.append(jnp.sum(mine[line] * (inside[at] + offset), axis=0, keepdims=True))
        offset = offset + whole[at]
    pos = jnp.concatenate(ranks, axis=0).astype(jnp.int32)
    fits = live & (pos < SIZE - 1)
    lost = jnp.max((live & (pos >= SIZE - 1)).astype(F32))
    code = jnp.where(fits, pos, LANES - 1)
    code_ref[...] = code
    dest = jnp.where(fits, owner * SIZE + pos, -1)

    names = jnp.concatenate(
        [mine[line] * name[line : line + 1].astype(F32) for line in range(lines)], axis=1
    ).astype(BF)
    index = iota((LANES, LANES), 0)
    places = jnp.concatenate([bits(index == code[line : line + 1]) for line in range(lines)], axis=1)
    meta = product_t(names, places)
    meta = jnp.where(iota((owners, LANES), 1) == LANES - 1, lost, meta).astype(BF)

    fill(choose, dest, 0)
    for part in range(parts):
        loads[part].wait()
        for chunk in range(part * STEP, (part + 1) * STEP, 64):
            values = held[chunk : chunk + 64, :].astype(F32)
            squares = jnp.sum(values * values, axis=1, keepdims=True)
            unit[chunk : chunk + 64, :] = (values * lax.rsqrt(squares + 1e-06)).astype(BF)

    stores = []
    for first in range(0, total, tile):
        if first:
            fill(choose, dest, first)
        for column in range(0, width, STEP):
            at = slice(column, column + STEP)
            packed = product(choose[...], unit[:, at])
            if column == 0:
                line = iota((tile, owners), 0) + first
                last = (iota((1, owners), 1) + 1) * SIZE - 1
                packed = jnp.concatenate(
                    [packed[:, :LANES] + product(bits(line == last), meta), packed[:, LANES:]], axis=1
                )
            out[pl.ds(first, tile), at] = packed.astype(BF)
            where = (pl.ds(first, tile), at)
            stores.append(
                pltpu.make_async_copy(out.at[where], blocks_ref.at[where], out_sems.at[len(stores)])
            )
            stores[-1].start()
    for store in stores:
        store.wait()


def pack(embeddings, cluster_id, valid, owners):
    rows, width = embeddings.shape
    total = owners * SIZE
    tile = min(total, TILE)
    lines = (rows // LANES, LANES)
    return pl.pallas_call(
        functools.partial(pack_kernel, owners),
        out_shape=(
            pltpu.HBM((total, width), BF),
            jax.ShapeDtypeStruct(lines, jnp.int32),
        ),
        in_specs=[IN_VMEM, IN_VMEM, ANY],
        out_specs=(ANY, IN_VMEM),
        scratch_shapes=[
            pltpu.VMEM((rows, width), BF),
            pltpu.VMEM((rows, width), BF),
            pltpu.VMEM((tile, rows), BF),
            pltpu.VMEM((total, width), BF),
            pltpu.SemaphoreType.DMA((rows // STEP,)),
            pltpu.SemaphoreType.DMA((total // tile * (width // STEP),)),
        ],
        compiler_params=pltpu.CompilerParams(vmem_limit_bytes=52 * MB),
        name="pack",
    )(cluster_id.reshape(lines), valid.reshape(lines), embeddings)


def score_kernel(owners, got_ref, best_ref, lost_ref, tags, rows, side, line, sems):
    total = rows.shape[0]
    tag_copy = pltpu.make_async_copy(
        got_ref.at[:, pl.ds(SIZE - 16, 16), pl.ds(0, LANES)], tags, sems.at[owners]
    )
    tag_copy.start()
    moves = []
    for source in range(owners):
        moves.append(
            pltpu.make_async_copy(
                got_ref.at[source], rows.at[pl.ds(source * SIZE, SIZE)], sems.at[source]
            )
        )
        moves[-1].start()
    tag_copy.wait()

    flat = tags[...].reshape(owners * 16, LANES)
    pick = bits(iota((owners, owners * 16), 1) == iota((owners, owners * 16), 0) * 16 + 15)
    names = product(pick, flat)
    lost = jnp.max(jnp.where(iota((owners, LANES), 1) == LANES - 1, names, 0.0))
    lost_ref[0, 0] = (lost > 0.0).astype(jnp.int32)
    same = iota((SIZE, LANES), 0) == iota((SIZE, LANES), 1)
    wide = jnp.concatenate(
        [jnp.where(same, names[source : source + 1], 0.0) for source in range(owners)], axis=0
    ).astype(BF)
    found = product(wide, jnp.ones((LANES, LANES), BF))
    side[...] = jnp.where(found == 0.0, -1.0, found)
    tops = product_t(jnp.ones((8, LANES), BF), wide)
    for move in moves:
        move.wait()

    apart = iota((8, LANES), 1) - iota((8, LANES), 0)

    def columns(here, top, diagonal):
        scores = product_t(rows[...], rows[here, :])
        for part in range(STEP // LANES):
            lanes = slice(part * LANES, (part + 1) * LANES)
            result = jnp.full((8, LANES), -1.0, F32)
            for block in range(0, total, 8):
                at = slice(block, block + 8)
                allowed = side[at, :] == top[:, lanes]
                own = diagonal(block, part)
                if own is not None:
                    allowed = allowed & (apart != own)
                result = jnp.maximum(result, jnp.where(allowed, scores[at, lanes], -1.0))
            line[:, pl.ds(here.start + part * LANES, LANES)] = jnp.max(result, axis=0, keepdims=True)

    if total <= 2048:
        for first in range(0, total, STEP):

            def diagonal(block, part):
                own = block - first - part * LANES
                return own if 0 <= own < LANES else None

            columns(pl.ds(first, STEP), tops[:, first : first + STEP], diagonal)
    else:
        line[...] = tops[0:1]

        @pl.loop(0, total // STEP)
        def _(number):
            first = pl.multiple_of(number * STEP, STEP)
            here = pl.ds(first, STEP)
            top = jnp.broadcast_to(line[:, here], (8, STEP))
            columns(here, top, lambda block, part: block - first - part * LANES)

    for source in range(owners):
        base, shift = divmod(source * SIZE, LANES)
        base *= LANES
        piece = line[:, base : min(base + 2 * LANES, total)]
        if shift:
            piece = pltpu.roll(piece, piece.shape[1] - shift, 1)
        best_ref[source] = piece[:, :LANES]


def score(got, owners):
    width = got.shape[2]
    total = owners * SIZE
    return pl.pallas_call(
        functools.partial(score_kernel, owners),
        out_shape=(
            pltpu.VMEM((owners, 1, LANES), F32),
            jax.ShapeDtypeStruct((1, 1), jnp.int32),
        ),
        in_specs=[ANY],
        out_specs=(IN_VMEM, pl.BlockSpec(memory_space=pltpu.SMEM)),
        scratch_shapes=[
            pltpu.VMEM((owners, 16, LANES), BF),
            pltpu.VMEM((total, width), BF),
            pltpu.VMEM((total, LANES), F32),
            pltpu.VMEM((1, total), F32),
            pltpu.SemaphoreType.DMA((owners + 1,)),
        ],
        compiler_params=pltpu.CompilerParams(vmem_limit_bytes=48 * MB),
        name="score",
    )(got)


def place_kernel(owners, back_ref, cid_ref, code_ref, valid_ref, out_ref, back, cid, code, valid, out, sems):
    moves = []
    for source, sink in ((back_ref, back), (cid_ref, cid), (code_ref, code), (valid_ref, valid)):
        moves.append(pltpu.make_async_copy(source, sink, sems.at[len(moves)]))
        moves[-1].start()
    for move in moves:
        move.wait()
    for start in range(0, cid.shape[0], 8):
        at = slice(start, start + 8)
        owner = lax.shift_right_logical(cid[at, :], 3)
        place = code[at, :]
        result = jnp.zeros((8, LANES), F32)
        for source in range(owners):
            line = jnp.broadcast_to(back[source], (8, LANES))
            value = jnp.take_along_axis(line, place, axis=1, mode="promise_in_bounds")
            result = jnp.where(owner == source, value, result)
        out[at, :] = jnp.where(valid[at, :] == 1, result, 0.0)
    store = pltpu.make_async_copy(out, out_ref, sems.at[4])
    store.start()
    store.wait()


def place(back, cluster_id, code, valid, owners):
    rows = cluster_id.shape[0]
    shape = (rows // LANES, LANES)
    return pl.pallas_call(
        functools.partial(place_kernel, owners),
        out_shape=pltpu.HBM(shape, F32),
        in_specs=[ANY] * 4,
        out_specs=ANY,
        scratch_shapes=[
            pltpu.VMEM((owners, 1, LANES), F32),
            pltpu.VMEM(shape, jnp.int32),
            pltpu.VMEM(shape, jnp.int32),
            pltpu.VMEM(shape, jnp.int32),
            pltpu.VMEM(shape, F32),
            pltpu.SemaphoreType.DMA((5,)),
        ],
        name="place",
    )(back, cluster_id.reshape(shape), code, valid.reshape(shape)).reshape(rows)


def every_slot(embeddings, cluster_id, valid, owners):
    width = embeddings.shape[1]
    clusters = CL_DEV * owners
    values = embeddings.astype(F32)
    squares = jnp.sum(values * values, axis=1, keepdims=True)
    unit_rows = (values * lax.rsqrt(squares + 1e-06)).astype(BF)
    one_hot = (cluster_id[:, None] == jnp.arange(clusters, dtype=jnp.int32)[None, :]).astype(jnp.int32)
    ranking = jnp.sum(jnp.cumsum(one_hot, axis=0) * one_hot, axis=1) - 1
    target = cluster_id * SLOT + ranking
    outgoing = jnp.zeros((clusters * SLOT, width), BF).at[target].set(unit_rows)
    live_out = jnp.zeros((clusters * SLOT,), BF).at[target].set(valid.astype(BF))
    got = lax.all_to_all(
        outgoing.reshape(owners, CL_DEV * SLOT, width), "owners", split_axis=0, concat_axis=0, tiled=True
    )
    live = lax.all_to_all(
        live_out.reshape(owners, CL_DEV, SLOT), "owners", split_axis=0, concat_axis=0, tiled=True
    )
    got = got.reshape(owners, CL_DEV, SLOT, width).transpose(1, 0, 2, 3)
    got = got.reshape(CL_DEV, owners * SLOT, width)
    live = live.transpose(1, 0, 2).reshape(CL_DEV, owners * SLOT) > 0.5
    diagonal = jnp.eye(owners * SLOT, dtype=bool)

    def one_cluster(args):
        rows, flags = args
        scores = jnp.einsum("md,nd->mn", rows, rows, preferred_element_type=F32)
        allowed = flags[:, None] & flags[None, :] & ~diagonal
        return jnp.max(jnp.where(allowed, scores, -1.0), axis=1)

    best = lax.map(one_cluster, (got, live)).reshape(CL_DEV, owners, SLOT).transpose(1, 0, 2)
    back = lax.all_to_all(best, "owners", split_axis=0, concat_axis=0, tiled=True)
    return jnp.where(valid == 1, back.reshape(-1)[target], 0.0)


def swap(blocks, owners):
    split = blocks.reshape(owners, blocks.shape[0] // owners, blocks.shape[1])
    return lax.all_to_all(split, "owners", split_axis=0, concat_axis=0, tiled=True)


def shards(embeddings, cluster_id, valid):
    owners = lax.axis_size("owners")
    blocks, code = pack(embeddings, cluster_id, valid, owners)
    best, lost = score(swap(blocks, owners), owners)
    back = lax.all_to_all(best, "owners", split_axis=0, concat_axis=0, tiled=True)
    nearest = place(back, cluster_id, code, valid, owners)
    return lax.cond(
        lost[0, 0] > 0,
        lambda: every_slot(embeddings, cluster_id, valid, owners),
        lambda: nearest,
    )


def solution(mesh):
    placed = (P(("groups", "owners"), None), P(("groups", "owners")), P(("groups", "owners")))
    return jax.shard_map(
        shards, mesh=mesh, in_specs=placed, out_specs=P(("groups", "owners")), check_vma=False
    )
```

time: 128 us -> 96.4 us (0.75)
  blocking collectives: 0 us -> 66.1 us
  starting transfers between devices: 63.5 us -> 5.15 us
  waiting for transfers between devices: 41.4 us -> 5.76 us
  Pallas kernels: 19.9 us -> 17.3 us
    all_to_all x0 -> x1, blocking collectives: none -> 66.1 us  [swap(): lax.all_to_all(split, 'owners', split_axis=0, concat_axis=0, tiled=True)]
    ppermute x30 -> x0, starting transfers between devices: 63.5 us -> none  [swap(): return lax.ppermute(block, 'owners', [(i, i ^ k) for i in range(owners)])]
    ppermute x30 -> x0, waiting for transfers between devices: 41.4 us -> none  [swap(): return lax.ppermute(block, 'owners', [(i, i ^ k) for i in range(owners)])]
    all_to_all x0 -> x1, waiting for transfers between devices: none -> 5.76 us  [shards(): lax.all_to_all(best, 'owners', split_axis=0, concat_axis=0, tiled=True)]
    all_to_all x0 -> x1, starting transfers between devices: none -> 5.15 us  [shards(): lax.all_to_all(best, 'owners', split_axis=0, concat_axis=0, tiled=True)]
    pallas_call x3, Pallas kernels: 19.9 us -> 17.3 us  [the longest x1 8.33 us: score(): pl.pallas_call(functools.partial(score_kernel, owners), out_shape=(pltpu....]
  transfers between devices with their start and end apart: 30 -> 1, of which waited for: 9 -> 1; matrix products, arithmetic and copies ran while one was open for 0% -> 0% of each run, Pallas kernels for 0% -> 0%
where the time goes in v5:
time: 96.4 us; the launch traced here: 96.1 us
  blocking collectives  66.1 us (69%)
  Pallas kernels  17.3 us (18%)
  waiting for transfers between devices  5.76 us (6%)
  starting transfers between devices  5.15 us (5%)
    all_to_all x1, blocking collectives, swap(): lax.all_to_all(split, 'owners', split_axis=0, concat_axis=0, tiled=True)  66.1 us
    pallas_call x1, Pallas kernels, score(): pl.pallas_call(functools.partial(score_kernel, owners), out_shape=(pltpu....  8.33 us
    pallas_call x1, Pallas kernels, pack(): pl.pallas_call(functools.partial(pack_kernel, owners), out_shape=(pltpu.H...  7.56 us
    all_to_all x1, waiting for transfers between devices, shards(): lax.all_to_all(best, 'owners', split_axis=0, concat_axis=0, tiled=True)  5.76 us
    all_to_all x1, starting transfers between devices, shards(): lax.all_to_all(best, 'owners', split_axis=0, concat_axis=0, tiled=True)  5.15 us
  transfers between devices with their start and end apart: 1, of which 1 were waited for; matrix products, arithmetic and copies ran while one was open for 0% of the time, Pallas kernels for 0%

profile of v5, /device:TPU:0, one launch (start us, length us, event | category | flops | bytes accessed | tf_op | source)
XLA Modules:
  0.0 96.1 jit_solution(14684027186406148027)
XLA Ops:
  0.0 7.6 %pack.1 = (bf16[1280,1024]{1,0:T(8,128)(2,1)}, s32[8,128]{1,0:T(8,128)S(1)}) custom-call(s32[8,128]{1,0:T(8,128)} %bitcast.36, s32[8,128]{1,0:T(8,128)} %bitcast.39, bf16[1024,1024]{1,0:T(8,128)(2,1)} %rows_ref.1), custom_call_target="tpu_custom_call" | custom-call | tf_op jit(solution)/shard_map/pack/pallas_call | solution.py:131
  7.6 0.0 copy-start
  7.6 0.0 copy-start.2
  7.6 0.0 copy-start.3
  7.6 0.0 copy-start.1
  7.6 66.1 %all_to_all.23.got_ref = bf16[16,80,1024]{2,1,0:T(8,128)(2,1)S(1)} all-to-all(bf16[16,80,1024]{2,1,0:T(8,128)(2,1)} %bitcast.34), channel_id=1, replica_groups=mesh['groups'=2,'owners'=16] {'owners'}, dimensions={0} | all-to-all | bytes 5242880 | tf_op jit(solution)/shard_map/all_to_all | solution.py:326
  73.7 8.3 %score.1 = (f32[16,1,128]{2,1,0:T(1,128)}, s32[1,1]{1,0:T(1,128)}) custom-call(bf16[16,80,1024]{2,1,0:T(8,128)(2,1)S(1)} %all_to_all.23.got_ref), custom_call_target="tpu_custom_call" | custom-call | tf_op jit(solution)/shard_map/score/pallas_call | solution.py:229
  82.0 0.0 copy-done
  82.0 5.2 %all-to-all-start.4 = ((f32[16,1,128]{2,1,0:T(1,128)}), f32[16,1,128]{2,1,0:T(1,128)S(1)}, u32[]{:S(2)}, u32[]{:S(2)}) async-start(f32[16,1,128]{2,1,0:T(1,128)} %get-tuple-element.87), calls=%async_computation.4 | async-start | bytes 16384 | tf_op jit(solution)/shard_map/all_to_all | solution.py:333
  87.8 5.8 %all-to-all-done.4.back_ref = f32[16,1,128]{2,1,0:T(1,128)S(1)} async-done(((f32[16,1,128]{2,1,0:T(1,128)}), f32[16,1,128]{2,1,0:T(1,128)S(1)}, u32[]{:S(2)}, u32[]{:S(2)}) %all-to-all-start.4) | async-done | bytes 8224 | tf_op jit(solution)/shard_map/all_to_all | solution.py:333
  93.6 0.0 copy-start.4
  93.6 0.6 copy-done.4
  94.2 0.0 copy-done.2
  94.2 0.0 copy-done.3
  94.2 1.4 %place.1 = f32[8,128]{1,0:T(8,128)} custom-call(f32[16,1,128]{2,1,0:T(1,128)} %copy-done.4, s32[8,128]{1,0:T(8,128)S(1)} %bitcast.37, s32[8,128]{1,0:T(8,128)} %copy-done, s32[8,128]{1,0:T(8,128)S(1)} %bitcast.40), custom_call_target="tpu_custom_call" | custom-call | tf_op jit(solution)/shard_map/place/pallas_call | solution.py:274
  95.6 0.0 copy-done.1
  95.6 0.2 conditional.1
Async XLA Ops:
  7.6 74.5 %copy-start = (s32[8,128]{1,0:T(8,128)}, s32[8,128]{1,0:T(8,128)S(1)}, u32[]{:S(2)}) copy-start(s32[8,128]{1,0:T(8,128)S(1)} %get-tuple-element.88.code_ref) | copy-start | bytes 12292
  7.6 86.6 %copy-start.2 = (s32[1024]{0:T(1024)S(1)}, s32[1024]{0:T(1024)}, u32[]{:S(2)}) copy-start(s32[1024]{0:T(1024)} %param.8) | copy-start | bytes 12292
  7.6 86.6 %copy-start.3 = (s32[1024]{0:T(1024)S(1)}, s32[1024]{0:T(1024)}, u32[]{:S(2)}) copy-start(s32[1024]{0:T(1024)} %param.9) | copy-start | bytes 12292
  7.6 88.0 %copy-start.1 = (bf16[1024,1024]{1,0:T(8,128)(2,1)S(1)}, bf16[1024,1024]{1,0:T(8,128)(2,1)}, u32[]{:S(2)}) copy-start(bf16[1024,1024]{1,0:T(8,128)(2,1)} %rows_ref.1) | copy-start | bytes 6291460
  82.0 11.6 %all-to-all-start.4 = ((f32[16,1,128]{2,1,0:T(1,128)}), f32[16,1,128]{2,1,0:T(1,128)S(1)}, u32[]{:S(2)}, u32[]{:S(2)}) async-start(f32[16,1,128]{2,1,0:T(1,128)} %get-tuple-element.87), calls=%async_computation.4 | async-start | bytes 16384 | tf_op jit(solution)/shard_map/all_to_all | solution.py:333
  93.6 0.6 copy-start.4

commit v6 on v5

--- a/solution.py
+++ b/solution.py
@@ -149,7 +149,81 @@
     )(cluster_id.reshape(lines), valid.reshape(lines), embeddings)
 
 
-def score_kernel(owners, got_ref, best_ref, lost_ref, tags, rows, side, line, sems):
+def on_units(size, count, multiply, use):
+    def body(*accs):
+        for number in range(count + 2):
+            if number < count:
+                multiply(number, number % 2, accs[number % 4])
+            if number >= 2:
+                use(number - 2, pltpu.matmul_pop(accs[(number - 2) % 4]))
+
+    pl.run_scoped(body, *[pltpu.ACC(mxu_id=number % 2)((size, STEP), F32) for number in range(4)])
+
+
+def triangle(total, rows, side, tops, line, across, down):
+    width = rows.shape[1]
+    blocks = total // STEP
+    seen = set()
+
+    def keep(ref, at, value):
+        if (id(ref), at) in seen:
+            value = jnp.maximum(value, ref[at : at + 8, :])
+        seen.add((id(ref), at))
+        ref[at : at + 8, :] = value
+
+    work = []
+    for column in range(blocks):
+        for row in range(column, blocks, 2):
+            work.append((column, row, min(2, blocks - row)))
+
+    def run(work, count):
+        def multiply(number, unit, acc):
+            column, row, _ = work[number]
+            for piece in range(width // STEP):
+                at = slice(piece * STEP, (piece + 1) * STEP)
+                pltpu.matmul_push_rhs(
+                    rows[column * STEP : (column + 1) * STEP, at], piece % 2, unit, transpose=True
+                )
+                pltpu.matmul_acc_lhs(
+                    acc, rows[row * STEP : (row + count) * STEP, at], load_staged_rhs=piece % 2
+                )
+
+        def use(number, scores):
+            column, row, _ = work[number]
+            apart = iota((8, LANES), 1) - iota((8, LANES), 0)
+            best = [jnp.full((8, LANES), -1.0, F32)] * (STEP // LANES)
+            for block in range(0, count * STEP, 8):
+                start = row * STEP + block
+                found = []
+                for part in range(STEP // LANES):
+                    first = column * STEP + part * LANES
+                    allowed = side[start : start + 8, :] == tops[:, first : first + LANES]
+                    if 0 <= start - first < LANES:
+                        allowed = allowed & (apart != start - first)
+                    here = scores[block : block + 8, part * LANES : (part + 1) * LANES]
+                    found.append(jnp.where(allowed, here, -1.0))
+                    best[part] = jnp.maximum(best[part], found[part])
+                if start // STEP > column:
+                    keep(across, start, functools.reduce(jnp.maximum, found))
+            for part in range(STEP // LANES):
+                keep(down, (column * (STEP // LANES) + part) * 8, best[part])
+
+        on_units(count * STEP, len(work), multiply, use)
+
+    run([item for item in work if item[2] == 2], 2)
+    run([item for item in work if item[2] == 1], 1)
+    for column in range(blocks):
+        for part in range(STEP // LANES):
+            first = column * STEP + part * LANES
+            at = (column * (STEP // LANES) + part) * 8
+            most = jnp.max(down[at : at + 8, :], axis=0, keepdims=True)
+            if column:
+                turned = across[first : first + LANES, :].T
+                most = jnp.maximum(most, jnp.max(turned, axis=0, keepdims=True))
+            line[:, first : first + LANES] = most
+
+
+def score_kernel(owners, got_ref, best_ref, lost_ref, tags, rows, side, line, sems, *more):
     total = rows.shape[0]
     tag_copy = pltpu.make_async_copy(
         got_ref.at[:, pl.ds(SIZE - 16, 16), pl.ds(0, LANES)], tags, sems.at[owners]
@@ -165,54 +239,48 @@
         moves[-1].start()
     tag_copy.wait()
 
-    flat = tags[...].reshape(owners * 16, LANES)
-    pick = bits(iota((owners, owners * 16), 1) == iota((owners, owners * 16), 0) * 16 + 15)
-    names = product(pick, flat)
-    lost = jnp.max(jnp.where(iota((owners, LANES), 1) == LANES - 1, names, 0.0))
+    same = iota((SIZE, LANES), 0) == iota((SIZE, LANES), 1)
+    lanes = iota((1, 2 * LANES), 1)
+    lost = jnp.zeros((1, LANES), F32)
+    line[...] = jnp.zeros((1, total), F32)
+    for source in range(owners):
+        name = tags[source].astype(F32)[15:16]
+        lost = jnp.maximum(lost, name)
+        found = jnp.sum(jnp.where(same, name, 0.0), axis=1, keepdims=True)
+        side[source * SIZE : (source + 1) * SIZE, :] = jnp.broadcast_to(
+            jnp.where(found == 0.0, -1.0, found), (SIZE, LANES)
+        )
+        base, shift = divmod(source * SIZE, LANES)
+        base *= LANES
+        name = jnp.where(lanes < SIZE, jnp.concatenate([name, name], axis=1), 0.0)
+        if shift:
+            name = pltpu.roll(name, shift, 1)
+        size = min(2 * LANES, total - base)
+        line[:, base : base + size] = line[:, base : base + size] + name[:, :size]
+    lost = jnp.max(jnp.where(lanes[:, :LANES] == LANES - 1, lost, 0.0))
     lost_ref[0, 0] = (lost > 0.0).astype(jnp.int32)
-    same = iota((SIZE, LANES), 0) == iota((SIZE, LANES), 1)
-    wide = jnp.concatenate(
-        [jnp.where(same, names[source : source + 1], 0.0) for source in range(owners)], axis=0
-    ).astype(BF)
-    found = product(wide, jnp.ones((LANES, LANES), BF))
-    side[...] = jnp.where(found == 0.0, -1.0, found)
-    tops = product_t(jnp.ones((8, LANES), BF), wide)
+    tops = jnp.broadcast_to(line[...], (8, total))
     for move in moves:
         move.wait()
 
-    apart = iota((8, LANES), 1) - iota((8, LANES), 0)
-
-    def columns(here, top, diagonal):
-        scores = product_t(rows[...], rows[here, :])
-        for part in range(STEP // LANES):
-            lanes = slice(part * LANES, (part + 1) * LANES)
-            result = jnp.full((8, LANES), -1.0, F32)
-            for block in range(0, total, 8):
-                at = slice(block, block + 8)
-                allowed = side[at, :] == top[:, lanes]
-                own = diagonal(block, part)
-                if own is not None:
-                    allowed = allowed & (apart != own)
-                result = jnp.maximum(result, jnp.where(allowed, scores[at, lanes], -1.0))
-            line[:, pl.ds(here.start + part * LANES, LANES)] = jnp.max(result, axis=0, keepdims=True)
-
     if total <= 2048:
-        for first in range(0, total, STEP):
-
-            def diagonal(block, part):
-                own = block - first - part * LANES
-                return own if 0 <= own < LANES else None
-
-            columns(pl.ds(first, STEP), tops[:, first : first + STEP], diagonal)
+        triangle(total, rows, side, tops, line, *more)
     else:
-        line[...] = tops[0:1]
-
         @pl.loop(0, total // STEP)
         def _(number):
             first = pl.multiple_of(number * STEP, STEP)
             here = pl.ds(first, STEP)
             top = jnp.broadcast_to(line[:, here], (8, STEP))
-            columns(here, top, lambda block, part: block - first - part * LANES)
+            scores = product_t(rows[...], rows[here, :])
+            apart = iota((8, LANES), 1) - iota((8, LANES), 0)
+            for part in range(STEP // LANES):
+                lanes = slice(part * LANES, (part + 1) * LANES)
+                result = jnp.full((8, LANES), -1.0, F32)
+                for block in range(0, total, 8):
+                    at = slice(block, block + 8)
+                    allowed = (side[at, :] == top[:, lanes]) & (apart != block - first - part * LANES)
+                    result = jnp.maximum(result, jnp.where(allowed, scores[at, lanes], -1.0))
+                line[:, pl.ds(first + part * LANES, LANES)] = jnp.max(result, axis=0, keepdims=True)
 
     for source in range(owners):
         base, shift = divmod(source * SIZE, LANES)
@@ -240,30 +308,28 @@
             pltpu.VMEM((total, LANES), F32),
             pltpu.VMEM((1, total), F32),
             pltpu.SemaphoreType.DMA((owners + 1,)),
-        ],
+        ]
+        + ([] if total > 2048 else [pltpu.VMEM((total, LANES), F32), pltpu.VMEM((total // 16, LANES), F32)]),
         compiler_params=pltpu.CompilerParams(vmem_limit_bytes=48 * MB),
         name="score",
     )(got)
 
 
-def place_kernel(owners, back_ref, cid_ref, code_ref, valid_ref, out_ref, back, cid, code, valid, out, sems):
-    moves = []
-    for source, sink in ((back_ref, back), (cid_ref, cid), (code_ref, code), (valid_ref, valid)):
-        moves.append(pltpu.make_async_copy(source, sink, sems.at[len(moves)]))
-        moves[-1].start()
-    for move in moves:
-        move.wait()
-    for start in range(0, cid.shape[0], 8):
+def place_kernel(owners, back_ref, cid_ref, code_ref, valid_ref, out_ref, back, out, sems):
+    move = pltpu.make_async_copy(back_ref, back, sems.at[0])
+    move.start()
+    move.wait()
+    for start in range(0, cid_ref.shape[0], 8):
         at = slice(start, start + 8)
-        owner = lax.shift_right_logical(cid[at, :], 3)
-        place = code[at, :]
+        owner = lax.shift_right_logical(cid_ref[at, :], 3)
+        code = code_ref[at, :]
         result = jnp.zeros((8, LANES), F32)
         for source in range(owners):
             line = jnp.broadcast_to(back[source], (8, LANES))
-            value = jnp.take_along_axis(line, place, axis=1, mode="promise_in_bounds")
+            value = jnp.take_along_axis(line, code, axis=1, mode="promise_in_bounds")
             result = jnp.where(owner == source, value, result)
-        out[at, :] = jnp.where(valid[at, :] == 1, result, 0.0)
-    store = pltpu.make_async_copy(out, out_ref, sems.at[4])
+        out[at, :] = jnp.where(valid_ref[at, :] == 1, result, 0.0)
+    store = pltpu.make_async_copy(out, out_ref, sems.at[1])
     store.start()
     store.wait()
 
@@ -271,18 +337,16 @@
 def place(back, cluster_id, code, valid, owners):
     rows = cluster_id.shape[0]
     shape = (rows // LANES, LANES)
+    back = pltpu.with_memory_space_constraint(back, pltpu.HBM)
     return pl.pallas_call(
         functools.partial(place_kernel, owners),
         out_shape=pltpu.HBM(shape, F32),
-        in_specs=[ANY] * 4,
+        in_specs=[ANY, IN_VMEM, IN_VMEM, IN_VMEM],
         out_specs=ANY,
         scratch_shapes=[
             pltpu.VMEM((owners, 1, LANES), F32),
-            pltpu.VMEM(shape, jnp.int32),
-            pltpu.VMEM(shape, jnp.int32),
-            pltpu.VMEM(shape, jnp.int32),
             pltpu.VMEM(shape, F32),
-            pltpu.SemaphoreType.DMA((5,)),
+            pltpu.SemaphoreType.DMA((2,)),
         ],
         name="place",
     )(back, cluster_id.reshape(shape), code, valid.reshape(shape)).reshape(rows)

time: 96.4 us -> 95.9 us (level)
    pallas_call x1, Pallas kernels: 8.33 us -> 7.12 us  [score(): pl.pallas_call(functools.partial(score_kernel, owners), out_shape=(pltpu....]
where the time goes in v6:
time: 95.9 us; the launch traced here: 95.5 us
  blocking collectives  66.1 us (69%)
  Pallas kernels  16.7 us (17%)
  waiting for transfers between devices  5.76 us (6%)
  starting transfers between devices  5.16 us (5%)
    all_to_all x1, blocking collectives, swap(): lax.all_to_all(split, 'owners', split_axis=0, concat_axis=0, tiled=True)  66.1 us
    pallas_call x1, Pallas kernels, pack(): pl.pallas_call(functools.partial(pack_kernel, owners), out_shape=(pltpu.H...  7.56 us
    pallas_call x1, Pallas kernels, score(): pl.pallas_call(functools.partial(score_kernel, owners), out_shape=(pltpu....  7.12 us
    all_to_all x1, waiting for transfers between devices, shards(): lax.all_to_all(best, 'owners', split_axis=0, concat_axis=0, tiled=True)  5.76 us
    all_to_all x1, starting transfers between devices, shards(): lax.all_to_all(best, 'owners', split_axis=0, concat_axis=0, tiled=True)  5.16 us
    pallas_call x1, Pallas kernels, place(): pl.pallas_call(functools.partial(place_kernel, owners), out_shape=pltpu.H...  2.07 us
  transfers between devices with their start and end apart: 1, of which 1 were waited for; matrix products, arithmetic and copies ran while one was open for 0% of the time, Pallas kernels for 0%

profile of v6, /device:TPU:0, one launch (start us, length us, event | category | flops | bytes accessed | tf_op | source)
XLA Modules:
  0.0 95.5 jit_solution(4916263526847580382)
XLA Ops:
  0.0 7.6 %pack.1 = (bf16[1280,1024]{1,0:T(8,128)(2,1)}, s32[8,128]{1,0:T(8,128)S(1)}) custom-call(s32[8,128]{1,0:T(8,128)} %bitcast.36, s32[8,128]{1,0:T(8,128)} %bitcast.39, bf16[1024,1024]{1,0:T(8,128)(2,1)} %rows_ref.1), custom_call_target="tpu_custom_call" | custom-call | tf_op jit(solution)/shard_map/pack/pallas_call | solution.py:131
  7.6 0.0 copy-start
  7.6 0.0 copy-start.2
  7.6 0.0 copy-start.3
  7.6 0.0 copy-start.1
  7.6 66.1 %all_to_all.23.got_ref = bf16[16,80,1024]{2,1,0:T(8,128)(2,1)S(1)} all-to-all(bf16[16,80,1024]{2,1,0:T(8,128)(2,1)} %bitcast.34), channel_id=1, replica_groups=mesh['groups'=2,'owners'=16] {'owners'}, dimensions={0} | all-to-all | bytes 5242880 | tf_op jit(solution)/shard_map/all_to_all | solution.py:390
  73.7 7.1 %score.1 = (f32[16,1,128]{2,1,0:T(1,128)}, s32[1,1]{1,0:T(1,128)}) custom-call(bf16[16,80,1024]{2,1,0:T(8,128)(2,1)S(1)} %all_to_all.23.got_ref), custom_call_target="tpu_custom_call" | custom-call | tf_op jit(solution)/shard_map/score/pallas_call | solution.py:297
  80.8 0.0 copy-done
  80.8 5.2 %all-to-all-start.4 = ((f32[16,1,128]{2,1,0:T(1,128)}), f32[16,1,128]{2,1,0:T(1,128)S(1)}, u32[]{:S(2)}, u32[]{:S(2)}) async-start(f32[16,1,128]{2,1,0:T(1,128)} %get-tuple-element.87), calls=%async_computation.4 | async-start | bytes 16384 | tf_op jit(solution)/shard_map/all_to_all | solution.py:397
  86.6 5.8 %all-to-all-done.4.back_ref = f32[16,1,128]{2,1,0:T(1,128)S(1)} async-done(((f32[16,1,128]{2,1,0:T(1,128)}), f32[16,1,128]{2,1,0:T(1,128)S(1)}, u32[]{:S(2)}, u32[]{:S(2)}) %all-to-all-start.4) | async-done | bytes 8224 | tf_op jit(solution)/shard_map/all_to_all | solution.py:397
  92.4 0.0 copy-start.4
  92.4 0.6 copy-done.4
  93.0 0.0 copy-done.2
  93.0 0.0 copy-done.3
  93.0 2.1 %place.1 = f32[8,128]{1,0:T(8,128)} custom-call(f32[16,1,128]{2,1,0:T(1,128)} %copy-done.4, s32[8,128]{1,0:T(8,128)S(1)} %bitcast.37, s32[8,128]{1,0:T(8,128)} %copy-done, s32[8,128]{1,0:T(8,128)S(1)} %bitcast.40), custom_call_target="tpu_custom_call" | custom-call | tf_op jit(solution)/shard_map/place/pallas_call | solution.py:341
  95.1 0.0 copy-done.1
  95.1 0.2 conditional.1
Async XLA Ops:
  7.6 73.3 %copy-start = (s32[8,128]{1,0:T(8,128)}, s32[8,128]{1,0:T(8,128)S(1)}, u32[]{:S(2)}) copy-start(s32[8,128]{1,0:T(8,128)S(1)} %get-tuple-element.88.code_ref) | copy-start | bytes 12292
  7.6 85.4 %copy-start.2 = (s32[1024]{0:T(1024)S(1)}, s32[1024]{0:T(1024)}, u32[]{:S(2)}) copy-start(s32[1024]{0:T(1024)} %param.8) | copy-start | bytes 12292
  7.6 85.4 %copy-start.3 = (s32[1024]{0:T(1024)S(1)}, s32[1024]{0:T(1024)}, u32[]{:S(2)}) copy-start(s32[1024]{0:T(1024)} %param.9) | copy-start | bytes 12292
  7.6 87.5 %copy-start.1 = (bf16[1024,1024]{1,0:T(8,128)(2,1)S(1)}, bf16[1024,1024]{1,0:T(8,128)(2,1)}, u32[]{:S(2)}) copy-start(bf16[1024,1024]{1,0:T(8,128)(2,1)} %rows_ref.1) | copy-start | bytes 6291460
  80.8 11.6 %all-to-all-start.4 = ((f32[16,1,128]{2,1,0:T(1,128)}), f32[16,1,128]{2,1,0:T(1,128)S(1)}, u32[]{:S(2)}, u32[]{:S(2)}) async-start(f32[16,1,128]{2,1,0:T(1,128)} %get-tuple-element.87), calls=%async_computation.4 | async-start | bytes 16384 | tf_op jit(solution)/shard_map/all_to_all | solution.py:397
  92.4 0.6 copy-start.4

commit v7 on v6

--- a/solution.py
+++ b/solution.py
@@ -123,13 +123,150 @@
         store.wait()
 
 
+def count_before(flags):
+    lane = iota(flags.shape, 1)
+    counts = flags
+    shift = 1
+    while shift < LANES:
+        counts = counts + jnp.where(lane >= shift, pltpu.roll(counts, shift, 1), 0.0)
+        shift *= 2
+    whole = jnp.broadcast_to(jnp.sum(flags, axis=1, keepdims=True), flags.shape)
+    return counts - flags, whole
+
+
+def pack_direct(
+    owners, cid_ref, valid_ref, rows_ref, blocks_ref, code_ref, held, unit, choose, out, tags, *sems
+):
+    rows, width = held.shape
+    total = out.shape[0]
+    lines = rows // LANES
+    parts = rows // STEP
+    in_sems, out_sems = sems[:parts], sems[parts:]
+    loads = []
+    for part in range(parts):
+        at = pl.ds(part * STEP, STEP)
+        loads.append(pltpu.make_async_copy(rows_ref.at[at], held.at[at], in_sems[part]))
+        loads[-1].start()
+
+    cid = cid_ref[...]
+    live = valid_ref[...] == 1
+    owner = lax.shift_right_logical(cid, 3)
+    name = (cid & (CL_DEV - 1)) + 1
+    target = jnp.where(live, owner, -1)
+    index = iota((owners, LANES), 0)
+    mine = [(index == target[line : line + 1]).astype(F32) for line in range(lines)]
+    inside, whole = count_before(jnp.concatenate(mine, axis=0))
+    offset = jnp.zeros((owners, LANES), F32)
+    ranks = []
+    for line in range(lines):
+        at = slice(line * owners, (line + 1) * owners)
+        ranks.append(jnp.sum(mine[line] * (inside[at] + offset), axis=0, keepdims=True))
+        offset = offset + whole[at]
+    pos = jnp.concatenate(ranks, axis=0).astype(jnp.int32)
+    fits = live & (pos < SIZE - 1)
+    lost = jnp.max((live & (pos >= SIZE - 1)).astype(F32))
+    code = jnp.where(fits, pos, LANES - 1)
+    code_ref[...] = code
+    dest = jnp.where(fits, owner * SIZE + pos, -1)
+
+    def name_rows(acc):
+        index = iota((STEP, LANES), 0)
+        pieces = STEP // LANES
+        for piece in range(lines // pieces):
+            here = range(piece * pieces, (piece + 1) * pieces)
+            places = [bits(index == code[line : line + 1]) for line in here]
+            names = [mine[line] * name[line : line + 1].astype(F32) for line in here]
+            pltpu.matmul_push_rhs(jnp.concatenate(places, axis=1), piece % 2, 0, transpose=True)
+            pltpu.matmul_acc_lhs(
+                acc, jnp.concatenate(names, axis=1).astype(BF), load_staged_rhs=piece % 2
+            )
+        meta = pltpu.matmul_pop(acc)
+        lane = iota((owners, STEP), 1)
+        tags[...] = jnp.where(lane < LANES - 1, meta, jnp.where(lane == LANES - 1, lost, 0.0))
+
+    pl.run_scoped(name_rows, pltpu.ACC(mxu_id=0)((owners, STEP), F32))
+    fill(choose, dest, 0)
+
+    def scale(part):
+        loads[part].wait()
+        for chunk in range(part * STEP, (part + 1) * STEP, 64):
+            values = held[chunk : chunk + 64, :].astype(F32)
+            squares = jnp.sum(values * values, axis=1, keepdims=True)
+            unit[chunk : chunk + 64, :] = (values * lax.rsqrt(squares + 1e-06)).astype(BF)
+
+    stores = []
+
+    def multiply(part, number, column, chunks, accs):
+        kept = slice(part * STEP, (part + 1) * STEP)
+        at = slice(column * STEP, (column + 1) * STEP)
+        pltpu.matmul_push_rhs(unit[kept, at], part % 2, number)
+        for chunk, (first, count) in enumerate(chunks):
+            pltpu.matmul_acc_lhs(
+                accs[number][chunk],
+                choose[first : first + count, kept],
+                load_staged_rhs=part % 2 if chunk == 0 else None,
+            )
+
+    def write(column, first, count, packed):
+        at = slice(column * STEP, (column + 1) * STEP)
+        for row in range(first, first + count, 16):
+            piece = packed[row - first : row - first + 16]
+            source, place = divmod(row, SIZE)
+            if column == 0 and place + 16 == SIZE:
+                piece = jnp.where(iota((16, STEP), 0) == 15, tags[...][source : source + 1], piece)
+            out[row : row + 16, at] = piece.astype(BF)
+        where = (pl.ds(first, count), at)
+        stores.append(pltpu.make_async_copy(out.at[where], blocks_ref.at[where], out_sems[len(stores)]))
+        stores[-1].start()
+
+    columns = width // STEP
+    chunks = [(first, 512) for first in range(0, total - 511, 512)]
+    rest = total - 512 * len(chunks)
+
+    def wide(*accs):
+        accs = (accs[:2], accs[2:])
+        scaled = False
+        for first in range(0, len(chunks), 2):
+            some = chunks[first : first + 2]
+            for column in range(0, columns, 2):
+                if not scaled:
+                    scale(0)
+                for part in range(parts):
+                    if not scaled and part + 1 < parts:
+                        scale(part + 1)
+                    for number in range(2):
+                        multiply(part, number, column + number, some, accs)
+                scaled = True
+                for number in range(2):
+                    for chunk, (begin, count) in enumerate(some):
+                        write(column + number, begin, count, pltpu.matmul_pop(accs[number][chunk]))
+
+    def narrow(*accs):
+        accs = (accs[:2], accs[2:])
+        for column in range(0, columns, 2):
+            turn = column // 2 % 2
+            for part in range(parts):
+                for number in range(2):
+                    one = ((accs[0][turn],), (accs[1][turn],))
+                    multiply(part, number, column + number, [(total - rest, rest)], one)
+            for number in range(2):
+                write(column + number, total - rest, rest, pltpu.matmul_pop(accs[number][turn]))
+
+    pl.run_scoped(wide, *[pltpu.ACC(mxu_id=number // 2)((512, STEP), F32) for number in range(4)])
+    if rest:
+        pl.run_scoped(narrow, *[pltpu.ACC(mxu_id=number // 2)((rest, STEP), F32) for number in range(4)])
+    for store in stores:
+        store.wait()
+
+
 def pack(embeddings, cluster_id, valid, owners):
     rows, width = embeddings.shape
     total = owners * SIZE
     tile = min(total, TILE)
     lines = (rows // LANES, LANES)
+    small = total <= 2048
     return pl.pallas_call(
-        functools.partial(pack_kernel, owners),
+        functools.partial(pack_direct if small else pack_kernel, owners),
         out_shape=(
             pltpu.HBM((total, width), BF),
             jax.ShapeDtypeStruct(lines, jnp.int32),
@@ -141,9 +278,16 @@
             pltpu.VMEM((rows, width), BF),
             pltpu.VMEM((tile, rows), BF),
             pltpu.VMEM((total, width), BF),
-            pltpu.SemaphoreType.DMA((rows // STEP,)),
-            pltpu.SemaphoreType.DMA((total // tile * (width // STEP),)),
-        ],
+        ]
+        + (
+            [pltpu.VMEM((owners, STEP), F32)]
+            + [pltpu.SemaphoreType.DMA] * (rows // STEP + (total + 511) // 512 * (width // STEP))
+            if small
+            else [
+                pltpu.SemaphoreType.DMA((rows // STEP,)),
+                pltpu.SemaphoreType.DMA((total // tile * (width // STEP),)),
+            ]
+        ),
         compiler_params=pltpu.CompilerParams(vmem_limit_bytes=52 * MB),
         name="pack",
     )(cluster_id.reshape(lines), valid.reshape(lines), embeddings)
@@ -223,28 +367,16 @@
             line[:, first : first + LANES] = most
 
 
-def score_kernel(owners, got_ref, best_ref, lost_ref, tags, rows, side, line, sems, *more):
-    total = rows.shape[0]
-    tag_copy = pltpu.make_async_copy(
-        got_ref.at[:, pl.ds(SIZE - 16, 16), pl.ds(0, LANES)], tags, sems.at[owners]
-    )
-    tag_copy.start()
-    moves = []
-    for source in range(owners):
-        moves.append(
-            pltpu.make_async_copy(
-                got_ref.at[source], rows.at[pl.ds(source * SIZE, SIZE)], sems.at[source]
-            )
-        )
-        moves[-1].start()
-    tag_copy.wait()
+def score_kernel(owners, got_ref, best_ref, lost_ref, side, line, *more):
+    total = line.shape[1]
+    rows = got_ref.reshape(total, got_ref.shape[2])
 
     same = iota((SIZE, LANES), 0) == iota((SIZE, LANES), 1)
     lanes = iota((1, 2 * LANES), 1)
     lost = jnp.zeros((1, LANES), F32)
     line[...] = jnp.zeros((1, total), F32)
     for source in range(owners):
-        name = tags[source].astype(F32)[15:16]
+        name = got_ref[source, SIZE - 16 : SIZE, :LANES].astype(F32)[15:16]
         lost = jnp.maximum(lost, name)
         found = jnp.sum(jnp.where(same, name, 0.0), axis=1, keepdims=True)
         side[source * SIZE : (source + 1) * SIZE, :] = jnp.broadcast_to(
@@ -260,9 +392,6 @@
     lost = jnp.max(jnp.where(lanes[:, :LANES] == LANES - 1, lost, 0.0))
     lost_ref[0, 0] = (lost > 0.0).astype(jnp.int32)
     tops = jnp.broadcast_to(line[...], (8, total))
-    for move in moves:
-        move.wait()
-
     if total <= 2048:
         triangle(total, rows, side, tops, line, *more)
     else:
@@ -300,14 +429,11 @@
             pltpu.VMEM((owners, 1, LANES), F32),
             jax.ShapeDtypeStruct((1, 1), jnp.int32),
         ),
-        in_specs=[ANY],
+        in_specs=[IN_VMEM],
         out_specs=(IN_VMEM, pl.BlockSpec(memory_space=pltpu.SMEM)),
         scratch_shapes=[
-            pltpu.VMEM((owners, 16, LANES), BF),
-            pltpu.VMEM((total, width), BF),
             pltpu.VMEM((total, LANES), F32),
             pltpu.VMEM((1, total), F32),
-            pltpu.SemaphoreType.DMA((owners + 1,)),
         ]
         + ([] if total > 2048 else [pltpu.VMEM((total, LANES), F32), pltpu.VMEM((total // 16, LANES), F32)]),
         compiler_params=pltpu.CompilerParams(vmem_limit_bytes=48 * MB),
@@ -315,21 +441,18 @@
     )(got)
 
 
-def place_kernel(owners, back_ref, cid_ref, code_ref, valid_ref, out_ref, back, out, sems):
-    move = pltpu.make_async_copy(back_ref, back, sems.at[0])
-    move.start()
-    move.wait()
+def place_kernel(owners, back_ref, cid_ref, code_ref, valid_ref, out_ref, out, sem):
     for start in range(0, cid_ref.shape[0], 8):
         at = slice(start, start + 8)
         owner = lax.shift_right_logical(cid_ref[at, :], 3)
         code = code_ref[at, :]
         result = jnp.zeros((8, LANES), F32)
         for source in range(owners):
-            line = jnp.broadcast_to(back[source], (8, LANES))
+            line = jnp.broadcast_to(back_ref[source], (8, LANES))
             value = jnp.take_along_axis(line, code, axis=1, mode="promise_in_bounds")
             result = jnp.where(owner == source, value, result)
         out[at, :] = jnp.where(valid_ref[at, :] == 1, result, 0.0)
-    store = pltpu.make_async_copy(out, out_ref, sems.at[1])
+    store = pltpu.make_async_copy(out, out_ref, sem)
     store.start()
     store.wait()
 
@@ -337,17 +460,13 @@
 def place(back, cluster_id, code, valid, owners):
     rows = cluster_id.shape[0]
     shape = (rows // LANES, LANES)
-    back = pltpu.with_memory_space_constraint(back, pltpu.HBM)
     return pl.pallas_call(
         functools.partial(place_kernel, owners),
         out_shape=pltpu.HBM(shape, F32),
-        in_specs=[ANY, IN_VMEM, IN_VMEM, IN_VMEM],
+        in_specs=[IN_VMEM] * 4,
         out_specs=ANY,
-        scratch_shapes=[
-            pltpu.VMEM((owners, 1, LANES), F32),
-            pltpu.VMEM(shape, F32),
-            pltpu.SemaphoreType.DMA((2,)),
-        ],
+        scratch_shapes=[pltpu.VMEM(shape, F32), pltpu.SemaphoreType.DMA],
+        compiler_params=pltpu.CompilerParams(vmem_limit_bytes=4 * MB),
         name="place",
     )(back, cluster_id.reshape(shape), code, valid.reshape(shape)).reshape(rows)
 

time: 95.9 us -> 90.5 us (0.944)
  Pallas kernels: 16.7 us -> 12.1 us
    pallas_call x1, Pallas kernels: 7.12 us -> 3.33 us  [score(): pl.pallas_call(functools.partial(score_kernel, owners), out_shape=(pltpu....]
    pallas_call x1, Pallas kernels: 2.07 us -> 0.69 us  [place(): pl.pallas_call(functools.partial(place_kernel, owners), out_shape=pltpu.H...]
where the time goes in v7:
time: 90.5 us; the launch traced here: 90.2 us
  blocking collectives  66.1 us (73%)
  Pallas kernels  12.1 us (13%)
  waiting for transfers between devices  5.76 us (6%)
  starting transfers between devices  5.15 us (6%)
    all_to_all x1, blocking collectives, swap(): lax.all_to_all(split, 'owners', split_axis=0, concat_axis=0, tiled=True)  66.1 us
    pallas_call x1, Pallas kernels, pack(): pl.pallas_call(functools.partial(pack_direct if small else pack_kernel, o...  8.06 us
    all_to_all x1, waiting for transfers between devices, shards(): lax.all_to_all(best, 'owners', split_axis=0, concat_axis=0, tiled=True)  5.76 us
    all_to_all x1, starting transfers between devices, shards(): lax.all_to_all(best, 'owners', split_axis=0, concat_axis=0, tiled=True)  5.15 us
    pallas_call x1, Pallas kernels, score(): pl.pallas_call(functools.partial(score_kernel, owners), out_shape=(pltpu....  3.33 us
  transfers between devices with their start and end apart: 1, of which 1 were waited for; matrix products, arithmetic and copies ran while one was open for 0% of the time, Pallas kernels for 0%

profile of v7, /device:TPU:0, one launch (start us, length us, event | category | flops | bytes accessed | tf_op | source)
XLA Modules:
  0.0 90.2 jit_solution(4035822925823602231)
XLA Ops:
  0.0 8.1 %pack.1 = (bf16[1280,1024]{1,0:T(8,128)(2,1)}, s32[8,128]{1,0:T(8,128)S(1)}) custom-call(s32[8,128]{1,0:T(8,128)} %bitcast.36, s32[8,128]{1,0:T(8,128)} %bitcast.39, bf16[1024,1024]{1,0:T(8,128)(2,1)} %rows_ref.1), custom_call_target="tpu_custom_call" | custom-call | tf_op jit(solution)/shard_map/pack/pallas_call | solution.py:268
  8.1 0.0 copy-start.1
  8.1 0.0 copy-start.2
  8.1 0.0 copy-start
  8.1 66.1 %all_to_all.23.got_ref = bf16[16,80,1024]{2,1,0:T(8,128)(2,1)S(1)} all-to-all(bf16[16,80,1024]{2,1,0:T(8,128)(2,1)} %bitcast.34), channel_id=1, replica_groups=mesh['groups'=2,'owners'=16] {'owners'}, dimensions={0} | all-to-all | bytes 5242880 | tf_op jit(solution)/shard_map/all_to_all | solution.py:509
  74.2 3.3 %score.1 = (f32[16,1,128]{2,1,0:T(1,128)}, s32[1,1]{1,0:T(1,128)}) custom-call(bf16[16,80,1024]{2,1,0:T(8,128)(2,1)S(1)} %all_to_all.23.got_ref), custom_call_target="tpu_custom_call" | custom-call | tf_op jit(solution)/shard_map/score/pallas_call | solution.py:426
  77.5 5.2 %all-to-all-start.4 = ((f32[16,1,128]{2,1,0:T(1,128)}), f32[16,1,128]{2,1,0:T(1,128)S(1)}, u32[]{:S(2)}, u32[]{:S(2)}) async-start(f32[16,1,128]{2,1,0:T(1,128)} %get-tuple-element.87), calls=%async_computation.4 | async-start | bytes 16384 | tf_op jit(solution)/shard_map/all_to_all | solution.py:516
  83.3 5.8 %all-to-all-done.4.back_ref = f32[16,1,128]{2,1,0:T(1,128)S(1)} async-done(((f32[16,1,128]{2,1,0:T(1,128)}), f32[16,1,128]{2,1,0:T(1,128)S(1)}, u32[]{:S(2)}, u32[]{:S(2)}) %all-to-all-start.4) | async-done | bytes 8224 | tf_op jit(solution)/shard_map/all_to_all | solution.py:516
  89.1 0.0 copy-done.1
  89.1 0.0 copy-done.2
  89.1 0.7 place.1
  89.8 0.0 copy-done
  89.8 0.2 conditional.1
Async XLA Ops:
  8.1 81.0 %copy-start.1 = (s32[1024]{0:T(1024)S(1)}, s32[1024]{0:T(1024)}, u32[]{:S(2)}) copy-start(s32[1024]{0:T(1024)} %param.8) | copy-start | bytes 12292
  8.1 81.0 %copy-start.2 = (s32[1024]{0:T(1024)S(1)}, s32[1024]{0:T(1024)}, u32[]{:S(2)}) copy-start(s32[1024]{0:T(1024)} %param.9) | copy-start | bytes 12292
  8.1 81.7 %copy-start = (bf16[1024,1024]{1,0:T(8,128)(2,1)S(1)}, bf16[1024,1024]{1,0:T(8,128)(2,1)}, u32[]{:S(2)}) copy-start(bf16[1024,1024]{1,0:T(8,128)(2,1)} %rows_ref.1) | copy-start | bytes 6291460
  77.5 11.6 %all-to-all-start.4 = ((f32[16,1,128]{2,1,0:T(1,128)}), f32[16,1,128]{2,1,0:T(1,128)S(1)}, u32[]{:S(2)}, u32[]{:S(2)}) async-start(f32[16,1,128]{2,1,0:T(1,128)} %get-tuple-element.87), calls=%async_computation.4 | async-start | bytes 16384 | tf_op jit(solution)/shard_map/all_to_all | solution.py:516

commit v8 on v6

--- a/solution.py
+++ b/solution.py
@@ -123,13 +123,151 @@
         store.wait()
 
 
+def pack_direct(
+    owners, cid_ref, valid_ref, rows_ref, blocks_ref, code_ref, held, unit, choose, out, tags, *sems
+):
+    rows, width = held.shape
+    total = out.shape[0]
+    lines = rows // LANES
+    parts = rows // STEP
+    pairs = STEP // LANES
+    chunk = 4 * SIZE
+    columns = width // STEP
+    in_sems, out_sems = sems[:parts], sems[parts:]
+    loads = []
+    for part in range(parts):
+        at = pl.ds(part * STEP, STEP)
+        loads.append(pltpu.make_async_copy(rows_ref.at[at], held.at[at], in_sems[part]))
+        loads[-1].start()
+    stores = []
+
+    def body(count_acc, tag_acc, *accs):
+        cid = cid_ref[...]
+        live = valid_ref[...] == 1
+        owner = lax.shift_right_logical(cid, 3)
+        name = (cid & (CL_DEV - 1)) + 1
+        target = jnp.where(live, owner, -1)
+        index = iota((owners, LANES), 0)
+        mine = [(index == target[line : line + 1]).astype(F32) for line in range(lines)]
+        mine = [jnp.concatenate(mine[i : i + pairs], axis=1) for i in range(0, lines, pairs)]
+        stacked = jnp.concatenate(mine, axis=0)
+        pltpu.matmul_push_rhs(bits(iota((STEP, STEP), 0) < iota((STEP, STEP), 1)), 0, 0)
+        pltpu.matmul_acc_lhs(count_acc, stacked.astype(BF), load_staged_rhs=0)
+        whole = jnp.sum(stacked, axis=1, keepdims=True)
+        inside = pltpu.matmul_pop(count_acc)
+        offset = jnp.zeros((owners, 1), F32)
+        ranks = []
+        for part in range(parts):
+            at = slice(part * owners, (part + 1) * owners)
+            rank = jnp.sum(mine[part] * (inside[at] + offset), axis=0, keepdims=True)
+            ranks += [rank[:, i * LANES : (i + 1) * LANES] for i in range(pairs)]
+            offset = offset + whole[at]
+        pos = jnp.concatenate(ranks, axis=0).astype(jnp.int32)
+        fits = live & (pos < SIZE - 1)
+        lost = jnp.max((live & (pos >= SIZE - 1)).astype(F32))
+        code = jnp.where(fits, pos, LANES - 1)
+        code_ref[...] = code
+        dest = jnp.where(fits, owner * SIZE + pos, -1)
+
+        def prepare(part):
+            loads[part].wait()
+            for begin in range(part * STEP, (part + 1) * STEP, 64):
+                values = held[begin : begin + 64, :].astype(F32)
+                squares = jnp.sum(values * values, axis=1, keepdims=True)
+                unit[begin : begin + 64, :] = (values * lax.rsqrt(squares + 1e-06)).astype(BF)
+            index = iota((total, LANES), 0)
+            for line in range(part * pairs, (part + 1) * pairs):
+                at = slice(line * LANES, (line + 1) * LANES)
+                choose[:, at] = bits(index == dest[line : line + 1])
+
+        def multiply(part, number, column, chunks):
+            kept = slice(part * STEP, (part + 1) * STEP)
+            at = slice(column * STEP, (column + 1) * STEP)
+            pltpu.matmul_push_rhs(unit[kept, at], part % 2, number)
+            first = True
+            for place, slot in chunks:
+                pltpu.matmul_acc_lhs(
+                    accs[number * 3 + slot],
+                    choose[place * chunk : (place + 1) * chunk, kept],
+                    load_staged_rhs=part % 2 if first else None,
+                )
+                first = False
+
+        def write(number, column, place, slot):
+            packed = pltpu.matmul_pop(accs[number * 3 + slot])
+            at = slice(column * STEP, (column + 1) * STEP)
+            first = place * chunk
+            for row in range(first, first + chunk, 16):
+                piece = packed[row - first : row - first + 16]
+                source, spot = divmod(row, SIZE)
+                if column == 0 and spot + 16 == SIZE:
+                    piece = jnp.where(iota((16, STEP), 0) == 15, tags[...][source : source + 1], piece)
+                out[row : row + 16, at] = piece.astype(BF)
+            where = (pl.ds(first, chunk), at)
+            stores.append(
+                pltpu.make_async_copy(out.at[where], blocks_ref.at[where], out_sems[len(stores)])
+            )
+            stores[-1].start()
+
+        opening = [(place, place) for place in range(3)]
+        for part in range(parts):
+            prepare(part)
+            if part:
+                for number in range(2):
+                    multiply(part - 1, number, number, opening)
+        for number in range(2):
+            multiply(parts - 1, number, number, opening)
+
+        index = iota((STEP, LANES), 0)
+        for part in range(parts):
+            here = range(part * pairs, (part + 1) * pairs)
+            places = [bits(index == code[line : line + 1]) for line in here]
+            named = [name[line : line + 1].astype(F32) for line in here]
+            pltpu.matmul_push_rhs(jnp.concatenate(places, axis=1), part % 2, 1, transpose=True)
+            pltpu.matmul_acc_lhs(
+                tag_acc,
+                (mine[part] * jnp.concatenate(named, axis=1)).astype(BF),
+                load_staged_rhs=part % 2,
+            )
+        lane = iota((owners, STEP), 1)
+        tags[...] = jnp.where(
+            lane < LANES - 1, pltpu.matmul_pop(tag_acc), jnp.where(lane == LANES - 1, lost, 0.0)
+        )
+
+        done = [(0, place) for place in range(3)]
+        left = [(0, place) for place in range(3, total // chunk)]
+        for column in range(2, columns, 2):
+            left += [(column, place) for place in range(total // chunk)]
+        for turn, (column, place) in enumerate(left):
+            before = done[turn]
+            for number in range(2):
+                write(number, before[0] + number, before[1], turn % 3)
+            for part in range(parts):
+                for number in range(2):
+                    multiply(part, number, column + number, [(place, turn % 3)])
+            done.append((column, place))
+        for turn in range(len(left), len(done)):
+            for number in range(2):
+                write(number, done[turn][0] + number, done[turn][1], turn % 3)
+
+    pl.run_scoped(
+        body,
+        pltpu.ACC(mxu_id=0)((parts * owners, STEP), F32),
+        pltpu.ACC(mxu_id=1)((owners, STEP), F32),
+        *[pltpu.ACC(mxu_id=number // 3)((chunk, STEP), F32) for number in range(6)],
+    )
+    for store in stores:
+        store.wait()
+
+
 def pack(embeddings, cluster_id, valid, owners):
     rows, width = embeddings.shape
     total = owners * SIZE
     tile = min(total, TILE)
     lines = (rows // LANES, LANES)
+    small = total <= 2048
     return pl.pallas_call(
-        functools.partial(pack_kernel, owners),
+        functools.partial(pack_direct if small else pack_kernel, owners),
         out_shape=(
             pltpu.HBM((total, width), BF),
             jax.ShapeDtypeStruct(lines, jnp.int32),
@@ -141,9 +279,16 @@
             pltpu.VMEM((rows, width), BF),
             pltpu.VMEM((tile, rows), BF),
             pltpu.VMEM((total, width), BF),
-            pltpu.SemaphoreType.DMA((rows // STEP,)),
-            pltpu.SemaphoreType.DMA((total // tile * (width // STEP),)),
-        ],
+        ]
+        + (
+            [pltpu.VMEM((owners, STEP), F32)]
+            + [pltpu.SemaphoreType.DMA] * (rows // STEP + owners // 4 * (width // STEP))
+            if small
+            else [
+                pltpu.SemaphoreType.DMA((rows // STEP,)),
+                pltpu.SemaphoreType.DMA((total // tile * (width // STEP),)),
+            ]
+        ),
         compiler_params=pltpu.CompilerParams(vmem_limit_bytes=52 * MB),
         name="pack",
     )(cluster_id.reshape(lines), valid.reshape(lines), embeddings)
@@ -223,28 +368,16 @@
             line[:, first : first + LANES] = most
 
 
-def score_kernel(owners, got_ref, best_ref, lost_ref, tags, rows, side, line, sems, *more):
-    total = rows.shape[0]
-    tag_copy = pltpu.make_async_copy(
-        got_ref.at[:, pl.ds(SIZE - 16, 16), pl.ds(0, LANES)], tags, sems.at[owners]
-    )
-    tag_copy.start()
-    moves = []
-    for source in range(owners):
-        moves.append(
-            pltpu.make_async_copy(
-                got_ref.at[source], rows.at[pl.ds(source * SIZE, SIZE)], sems.at[source]
-            )
-        )
-        moves[-1].start()
-    tag_copy.wait()
+def score_kernel(owners, got_ref, best_ref, lost_ref, side, line, *more):
+    total = line.shape[1]
+    rows = got_ref.reshape(total, got_ref.shape[2])
 
     same = iota((SIZE, LANES), 0) == iota((SIZE, LANES), 1)
     lanes = iota((1, 2 * LANES), 1)
     lost = jnp.zeros((1, LANES), F32)
     line[...] = jnp.zeros((1, total), F32)
     for source in range(owners):
-        name = tags[source].astype(F32)[15:16]
+        name = got_ref[source, SIZE - 16 : SIZE, :LANES].astype(F32)[15:16]
         lost = jnp.maximum(lost, name)
         found = jnp.sum(jnp.where(same, name, 0.0), axis=1, keepdims=True)
         side[source * SIZE : (source + 1) * SIZE, :] = jnp.broadcast_to(
@@ -260,9 +393,6 @@
     lost = jnp.max(jnp.where(lanes[:, :LANES] == LANES - 1, lost, 0.0))
     lost_ref[0, 0] = (lost > 0.0).astype(jnp.int32)
     tops = jnp.broadcast_to(line[...], (8, total))
-    for move in moves:
-        move.wait()
-
     if total <= 2048:
         triangle(total, rows, side, tops, line, *more)
     else:
@@ -300,14 +430,11 @@
             pltpu.VMEM((owners, 1, LANES), F32),
             jax.ShapeDtypeStruct((1, 1), jnp.int32),
         ),
-        in_specs=[ANY],
+        in_specs=[IN_VMEM],
         out_specs=(IN_VMEM, pl.BlockSpec(memory_space=pltpu.SMEM)),
         scratch_shapes=[
-            pltpu.VMEM((owners, 16, LANES), BF),
-            pltpu.VMEM((total, width), BF),
             pltpu.VMEM((total, LANES), F32),
             pltpu.VMEM((1, total), F32),
-            pltpu.SemaphoreType.DMA((owners + 1,)),
         ]
         + ([] if total > 2048 else [pltpu.VMEM((total, LANES), F32), pltpu.VMEM((total // 16, LANES), F32)]),
         compiler_params=pltpu.CompilerParams(vmem_limit_bytes=48 * MB),
@@ -315,21 +442,18 @@
     )(got)
 
 
-def place_kernel(owners, back_ref, cid_ref, code_ref, valid_ref, out_ref, back, out, sems):
-    move = pltpu.make_async_copy(back_ref, back, sems.at[0])
-    move.start()
-    move.wait()
+def place_kernel(owners, back_ref, cid_ref, code_ref, valid_ref, out_ref, out, sem):
     for start in range(0, cid_ref.shape[0], 8):
         at = slice(start, start + 8)
         owner = lax.shift_right_logical(cid_ref[at, :], 3)
         code = code_ref[at, :]
         result = jnp.zeros((8, LANES), F32)
         for source in range(owners):
-            line = jnp.broadcast_to(back[source], (8, LANES))
+            line = jnp.broadcast_to(back_ref[source], (8, LANES))
             value = jnp.take_along_axis(line, code, axis=1, mode="promise_in_bounds")
             result = jnp.where(owner == source, value, result)
         out[at, :] = jnp.where(valid_ref[at, :] == 1, result, 0.0)
-    store = pltpu.make_async_copy(out, out_ref, sems.at[1])
+    store = pltpu.make_async_copy(out, out_ref, sem)
     store.start()
     store.wait()
 
@@ -337,17 +461,13 @@
 def place(back, cluster_id, code, valid, owners):
     rows = cluster_id.shape[0]
     shape = (rows // LANES, LANES)
-    back = pltpu.with_memory_space_constraint(back, pltpu.HBM)
     return pl.pallas_call(
         functools.partial(place_kernel, owners),
         out_shape=pltpu.HBM(shape, F32),
-        in_specs=[ANY, IN_VMEM, IN_VMEM, IN_VMEM],
+        in_specs=[IN_VMEM] * 4,
         out_specs=ANY,
-        scratch_shapes=[
-            pltpu.VMEM((owners, 1, LANES), F32),
-            pltpu.VMEM(shape, F32),
-            pltpu.SemaphoreType.DMA((2,)),
-        ],
+        scratch_shapes=[pltpu.VMEM(shape, F32), pltpu.SemaphoreType.DMA],
+        compiler_params=pltpu.CompilerParams(vmem_limit_bytes=4 * MB),
         name="place",
     )(back, cluster_id.reshape(shape), code, valid.reshape(shape)).reshape(rows)
 

time: 95.9 us -> 89.9 us (0.937)
  Pallas kernels: 16.7 us -> 11.5 us
    pallas_call x1, Pallas kernels: 7.12 us -> 3.33 us  [score(): pl.pallas_call(functools.partial(score_kernel, owners), out_shape=(pltpu....]
    pallas_call x1, Pallas kernels: 2.07 us -> 0.69 us  [place(): pl.pallas_call(functools.partial(place_kernel, owners), out_shape=pltpu.H...]
where the time goes in v8:
time: 89.9 us; the launch traced here: 89.6 us
  blocking collectives  66.1 us (74%)
  Pallas kernels  11.5 us (13%)
  waiting for transfers between devices  5.76 us (6%)
  starting transfers between devices  5.16 us (6%)
  between operations  0.9 us (1%)
    all_to_all x1, blocking collectives, swap(): lax.all_to_all(split, 'owners', split_axis=0, concat_axis=0, tiled=True)  66.1 us
    pallas_call x1, Pallas kernels, pack(): pl.pallas_call(functools.partial(pack_direct if small else pack_kernel, o...  7.45 us
    all_to_all x1, waiting for transfers between devices, shards(): lax.all_to_all(best, 'owners', split_axis=0, concat_axis=0, tiled=True)  5.76 us
    all_to_all x1, starting transfers between devices, shards(): lax.all_to_all(best, 'owners', split_axis=0, concat_axis=0, tiled=True)  5.16 us
    pallas_call x1, Pallas kernels, score(): pl.pallas_call(functools.partial(score_kernel, owners), out_shape=(pltpu....  3.33 us
  transfers between devices with their start and end apart: 1, of which 1 were waited for; matrix products, arithmetic and copies ran while one was open for 0% of the time, Pallas kernels for 0%

profile of v8, /device:TPU:0, one launch (start us, length us, event | category | flops | bytes accessed | tf_op | source)
XLA Modules:
  0.0 89.6 jit_solution(92412120744167167)
XLA Ops:
  0.0 7.5 %pack.1 = (bf16[1280,1024]{1,0:T(8,128)(2,1)}, s32[8,128]{1,0:T(8,128)S(1)}) custom-call(s32[8,128]{1,0:T(8,128)} %bitcast.36, s32[8,128]{1,0:T(8,128)} %bitcast.39, bf16[1024,1024]{1,0:T(8,128)(2,1)} %rows_ref.1), custom_call_target="tpu_custom_call" | custom-call | tf_op jit(solution)/shard_map/pack/pallas_call | solution.py:269
  7.5 0.0 copy-start.1
  7.5 0.0 copy-start.2
  7.5 0.0 copy-start
  7.5 66.1 %all_to_all.23.got_ref = bf16[16,80,1024]{2,1,0:T(8,128)(2,1)S(1)} all-to-all(bf16[16,80,1024]{2,1,0:T(8,128)(2,1)} %bitcast.34), channel_id=1, replica_groups=mesh['groups'=2,'owners'=16] {'owners'}, dimensions={0} | all-to-all | bytes 5242880 | tf_op jit(solution)/shard_map/all_to_all | solution.py:510
  73.6 3.3 %score.1 = (f32[16,1,128]{2,1,0:T(1,128)}, s32[1,1]{1,0:T(1,128)}) custom-call(bf16[16,80,1024]{2,1,0:T(8,128)(2,1)S(1)} %all_to_all.23.got_ref), custom_call_target="tpu_custom_call" | custom-call | tf_op jit(solution)/shard_map/score/pallas_call | solution.py:427
  76.9 5.2 %all-to-all-start.4 = ((f32[16,1,128]{2,1,0:T(1,128)}), f32[16,1,128]{2,1,0:T(1,128)S(1)}, u32[]{:S(2)}, u32[]{:S(2)}) async-start(f32[16,1,128]{2,1,0:T(1,128)} %get-tuple-element.87), calls=%async_computation.4 | async-start | bytes 16384 | tf_op jit(solution)/shard_map/all_to_all | solution.py:517
  82.7 5.8 %all-to-all-done.4.back_ref = f32[16,1,128]{2,1,0:T(1,128)S(1)} async-done(((f32[16,1,128]{2,1,0:T(1,128)}), f32[16,1,128]{2,1,0:T(1,128)S(1)}, u32[]{:S(2)}, u32[]{:S(2)}) %all-to-all-start.4) | async-done | bytes 8224 | tf_op jit(solution)/shard_map/all_to_all | solution.py:517
  88.5 0.0 copy-done.1
  88.5 0.0 copy-done.2
  88.5 0.7 place.1
  89.2 0.0 copy-done
  89.2 0.2 conditional.1
Async XLA Ops:
  7.5 81.0 %copy-start.1 = (s32[1024]{0:T(1024)S(1)}, s32[1024]{0:T(1024)}, u32[]{:S(2)}) copy-start(s32[1024]{0:T(1024)} %param.8) | copy-start | bytes 12292
  7.5 81.0 %copy-start.2 = (s32[1024]{0:T(1024)S(1)}, s32[1024]{0:T(1024)}, u32[]{:S(2)}) copy-start(s32[1024]{0:T(1024)} %param.9) | copy-start | bytes 12292
  7.5 81.7 %copy-start = (bf16[1024,1024]{1,0:T(8,128)(2,1)S(1)}, bf16[1024,1024]{1,0:T(8,128)(2,1)}, u32[]{:S(2)}) copy-start(bf16[1024,1024]{1,0:T(8,128)(2,1)} %rows_ref.1) | copy-start | bytes 6291460
  76.9 11.6 %all-to-all-start.4 = ((f32[16,1,128]{2,1,0:T(1,128)}), f32[16,1,128]{2,1,0:T(1,128)S(1)}, u32[]{:S(2)}, u32[]{:S(2)}) async-start(f32[16,1,128]{2,1,0:T(1,128)} %get-tuple-element.87), calls=%async_computation.4 | async-start | bytes 16384 | tf_op jit(solution)/shard_map/all_to_all | solution.py:517

commit v9 on v8

--- a/solution.py
+++ b/solution.py
@@ -171,10 +171,10 @@
 
         def prepare(part):
             loads[part].wait()
-            for begin in range(part * STEP, (part + 1) * STEP, 64):
-                values = held[begin : begin + 64, :].astype(F32)
+            for begin in range(part * STEP, (part + 1) * STEP, 16):
+                values = held[begin : begin + 16, :].astype(F32)
                 squares = jnp.sum(values * values, axis=1, keepdims=True)
-                unit[begin : begin + 64, :] = (values * lax.rsqrt(squares + 1e-06)).astype(BF)
+                unit[begin : begin + 16, :] = (values * lax.rsqrt(squares + 1e-06)).astype(BF)
             index = iota((total, LANES), 0)
             for line in range(part * pairs, (part + 1) * pairs):
                 at = slice(line * LANES, (line + 1) * LANES)

time: 89.9 us -> 89.9 us (level)
  no operation moved by 1% of the time
where the time goes in v9:
time: 89.9 us; the launch traced here: 89.6 us
  blocking collectives  66.1 us (74%)
  Pallas kernels  11.5 us (13%)
  waiting for transfers between devices  5.76 us (6%)
  starting transfers between devices  5.16 us (6%)
  between operations  0.9 us (1%)
    all_to_all x1, blocking collectives, swap(): lax.all_to_all(split, 'owners', split_axis=0, concat_axis=0, tiled=True)  66.1 us
    pallas_call x1, Pallas kernels, pack(): pl.pallas_call(functools.partial(pack_direct if small else pack_kernel, o...  7.45 us
    all_to_all x1, waiting for transfers between devices, shards(): lax.all_to_all(best, 'owners', split_axis=0, concat_axis=0, tiled=True)  5.76 us
    all_to_all x1, starting transfers between devices, shards(): lax.all_to_all(best, 'owners', split_axis=0, concat_axis=0, tiled=True)  5.16 us
    pallas_call x1, Pallas kernels, score(): pl.pallas_call(functools.partial(score_kernel, owners), out_shape=(pltpu....  3.33 us
  transfers between devices with their start and end apart: 1, of which 1 were waited for; matrix products, arithmetic and copies ran while one was open for 0% of the time, Pallas kernels for 0%

profile of v9, /device:TPU:0, one launch (start us, length us, event | category | flops | bytes accessed | tf_op | source)
XLA Modules:
  0.0 89.6 jit_solution(92412120744167167)
XLA Ops:
  0.0 7.5 %pack.1 = (bf16[1280,1024]{1,0:T(8,128)(2,1)}, s32[8,128]{1,0:T(8,128)S(1)}) custom-call(s32[8,128]{1,0:T(8,128)} %bitcast.36, s32[8,128]{1,0:T(8,128)} %bitcast.39, bf16[1024,1024]{1,0:T(8,128)(2,1)} %rows_ref.1), custom_call_target="tpu_custom_call" | custom-call | tf_op jit(solution)/shard_map/pack/pallas_call | solution.py:269
  7.5 0.0 copy-start.1
  7.5 0.0 copy-start.2
  7.5 0.0 copy-start
  7.5 66.1 %all_to_all.23.got_ref = bf16[16,80,1024]{2,1,0:T(8,128)(2,1)S(1)} all-to-all(bf16[16,80,1024]{2,1,0:T(8,128)(2,1)} %bitcast.34), channel_id=1, replica_groups=mesh['groups'=2,'owners'=16] {'owners'}, dimensions={0} | all-to-all | bytes 5242880 | tf_op jit(solution)/shard_map/all_to_all | solution.py:510
  73.6 3.3 %score.1 = (f32[16,1,128]{2,1,0:T(1,128)}, s32[1,1]{1,0:T(1,128)}) custom-call(bf16[16,80,1024]{2,1,0:T(8,128)(2,1)S(1)} %all_to_all.23.got_ref), custom_call_target="tpu_custom_call" | custom-call | tf_op jit(solution)/shard_map/score/pallas_call | solution.py:427
  76.9 5.2 %all-to-all-start.4 = ((f32[16,1,128]{2,1,0:T(1,128)}), f32[16,1,128]{2,1,0:T(1,128)S(1)}, u32[]{:S(2)}, u32[]{:S(2)}) async-start(f32[16,1,128]{2,1,0:T(1,128)} %get-tuple-element.87), calls=%async_computation.4 | async-start | bytes 16384 | tf_op jit(solution)/shard_map/all_to_all | solution.py:517
  82.7 5.8 %all-to-all-done.4.back_ref = f32[16,1,128]{2,1,0:T(1,128)S(1)} async-done(((f32[16,1,128]{2,1,0:T(1,128)}), f32[16,1,128]{2,1,0:T(1,128)S(1)}, u32[]{:S(2)}, u32[]{:S(2)}) %all-to-all-start.4) | async-done | bytes 8224 | tf_op jit(solution)/shard_map/all_to_all | solution.py:517
  88.5 0.0 copy-done.1
  88.5 0.0 copy-done.2
  88.5 0.7 place.1
  89.2 0.0 copy-done
  89.2 0.2 conditional.1
Async XLA Ops:
  7.5 81.0 %copy-start.1 = (s32[1024]{0:T(1024)S(1)}, s32[1024]{0:T(1024)}, u32[]{:S(2)}) copy-start(s32[1024]{0:T(1024)} %param.8) | copy-start | bytes 12292
  7.5 81.0 %copy-start.2 = (s32[1024]{0:T(1024)S(1)}, s32[1024]{0:T(1024)}, u32[]{:S(2)}) copy-start(s32[1024]{0:T(1024)} %param.9) | copy-start | bytes 12292
  7.5 81.7 %copy-start = (bf16[1024,1024]{1,0:T(8,128)(2,1)S(1)}, bf16[1024,1024]{1,0:T(8,128)(2,1)}, u32[]{:S(2)}) copy-start(bf16[1024,1024]{1,0:T(8,128)(2,1)} %rows_ref.1) | copy-start | bytes 6291460
  76.9 11.6 %all-to-all-start.4 = ((f32[16,1,128]{2,1,0:T(1,128)}), f32[16,1,128]{2,1,0:T(1,128)S(1)}, u32[]{:S(2)}, u32[]{:S(2)}) async-start(f32[16,1,128]{2,1,0:T(1,128)} %get-tuple-element.87), calls=%async_computation.4 | async-start | bytes 16384 | tf_op jit(solution)/shard_map/all_to_all | solution.py:517

commit v10 on v8

--- a/solution.py
+++ b/solution.py
@@ -124,7 +124,7 @@
 
 
 def pack_direct(
-    owners, cid_ref, valid_ref, rows_ref, blocks_ref, code_ref, held, unit, choose, out, tags, *sems
+    owners, cid_ref, valid_ref, rows_ref, blocks_ref, code_ref, held, unit, choose, out, tags, marks, *sems
 ):
     rows, width = held.shape
     total = out.shape[0]
@@ -133,17 +133,23 @@
     pairs = STEP // LANES
     chunk = 4 * SIZE
     columns = width // STEP
-    in_sems, out_sems = sems[:parts], sems[parts:]
+    in_sems, mark_sems, out_sems = sems[:parts], sems[parts : parts + 2], sems[parts + 2 :]
+    fetches = []
+    for number, source in enumerate((cid_ref, valid_ref)):
+        fetches.append(pltpu.make_async_copy(source, marks.at[number], mark_sems[number]))
+        fetches[-1].start()
     loads = []
     for part in range(parts):
         at = pl.ds(part * STEP, STEP)
         loads.append(pltpu.make_async_copy(rows_ref.at[at], held.at[at], in_sems[part]))
         loads[-1].start()
     stores = []
+    for fetch in fetches:
+        fetch.wait()
 
     def body(count_acc, tag_acc, *accs):
-        cid = cid_ref[...]
-        live = valid_ref[...] == 1
+        cid = marks[0]
+        live = marks[1] == 1
         owner = lax.shift_right_logical(cid, 3)
         name = (cid & (CL_DEV - 1)) + 1
         target = jnp.where(live, owner, -1)
@@ -272,7 +278,7 @@
             pltpu.HBM((total, width), BF),
             jax.ShapeDtypeStruct(lines, jnp.int32),
         ),
-        in_specs=[IN_VMEM, IN_VMEM, ANY],
+        in_specs=[ANY if small else IN_VMEM] * 2 + [ANY],
         out_specs=(ANY, IN_VMEM),
         scratch_shapes=[
             pltpu.VMEM((rows, width), BF),
@@ -281,8 +287,8 @@
             pltpu.VMEM((total, width), BF),
         ]
         + (
-            [pltpu.VMEM((owners, STEP), F32)]
-            + [pltpu.SemaphoreType.DMA] * (rows // STEP + owners // 4 * (width // STEP))
+            [pltpu.VMEM((owners, STEP), F32), pltpu.VMEM((2,) + lines, jnp.int32)]
+            + [pltpu.SemaphoreType.DMA] * (rows // STEP + 2 + owners // 4 * (width // STEP))
             if small
             else [
                 pltpu.SemaphoreType.DMA((rows // STEP,)),

time: 89.9 us -> 89.6 us (level)
  no operation moved by 1% of the time
where the time goes in v10:
time: 89.6 us; the launch traced here: 89.3 us
  blocking collectives  66.1 us (74%)
  Pallas kernels  11.2 us (12%)
  waiting for transfers between devices  5.76 us (6%)
  starting transfers between devices  5.16 us (6%)
  between operations  0.9 us (1%)
    all_to_all x1, blocking collectives, swap(): lax.all_to_all(split, 'owners', split_axis=0, concat_axis=0, tiled=True)  66.1 us
    pallas_call x1, Pallas kernels, pack(): pl.pallas_call(functools.partial(pack_direct if small else pack_kernel, o...  7.17 us
    all_to_all x1, waiting for transfers between devices, shards(): lax.all_to_all(best, 'owners', split_axis=0, concat_axis=0, tiled=True)  5.76 us
    all_to_all x1, starting transfers between devices, shards(): lax.all_to_all(best, 'owners', split_axis=0, concat_axis=0, tiled=True)  5.16 us
    pallas_call x1, Pallas kernels, score(): pl.pallas_call(functools.partial(score_kernel, owners), out_shape=(pltpu....  3.33 us
  transfers between devices with their start and end apart: 1, of which 1 were waited for; matrix products, arithmetic and copies ran while one was open for 0% of the time, Pallas kernels for 0%

profile of v10, /device:TPU:0, one launch (start us, length us, event | category | flops | bytes accessed | tf_op | source)
XLA Modules:
  0.0 89.3 jit_solution(8516763585518815296)
XLA Ops:
  0.0 7.2 %pack.1 = (bf16[1280,1024]{1,0:T(8,128)(2,1)}, s32[8,128]{1,0:T(8,128)S(1)}) custom-call(s32[8,128]{1,0:T(8,128)} %bitcast.36, s32[8,128]{1,0:T(8,128)} %bitcast.39, bf16[1024,1024]{1,0:T(8,128)(2,1)} %rows_ref.1), custom_call_target="tpu_custom_call" | custom-call | tf_op jit(solution)/shard_map/pack/pallas_call | solution.py:275
  7.2 0.0 copy-start.1
  7.2 0.0 copy-start.2
  7.2 0.0 copy-start
  7.2 66.1 %all_to_all.23.got_ref = bf16[16,80,1024]{2,1,0:T(8,128)(2,1)S(1)} all-to-all(bf16[16,80,1024]{2,1,0:T(8,128)(2,1)} %bitcast.34), channel_id=1, replica_groups=mesh['groups'=2,'owners'=16] {'owners'}, dimensions={0} | all-to-all | bytes 5242880 | tf_op jit(solution)/shard_map/all_to_all | solution.py:516
  73.3 3.3 %score.1 = (f32[16,1,128]{2,1,0:T(1,128)}, s32[1,1]{1,0:T(1,128)}) custom-call(bf16[16,80,1024]{2,1,0:T(8,128)(2,1)S(1)} %all_to_all.23.got_ref), custom_call_target="tpu_custom_call" | custom-call | tf_op jit(solution)/shard_map/score/pallas_call | solution.py:433
  76.7 5.2 %all-to-all-start.4 = ((f32[16,1,128]{2,1,0:T(1,128)}), f32[16,1,128]{2,1,0:T(1,128)S(1)}, u32[]{:S(2)}, u32[]{:S(2)}) async-start(f32[16,1,128]{2,1,0:T(1,128)} %get-tuple-element.87), calls=%async_computation.4 | async-start | bytes 16384 | tf_op jit(solution)/shard_map/all_to_all | solution.py:523
  82.5 5.8 %all-to-all-done.4.back_ref = f32[16,1,128]{2,1,0:T(1,128)S(1)} async-done(((f32[16,1,128]{2,1,0:T(1,128)}), f32[16,1,128]{2,1,0:T(1,128)S(1)}, u32[]{:S(2)}, u32[]{:S(2)}) %all-to-all-start.4) | async-done | bytes 8224 | tf_op jit(solution)/shard_map/all_to_all | solution.py:523
  88.2 0.0 copy-done.1
  88.2 0.0 copy-done.2
  88.2 0.7 place.1
  88.9 0.0 copy-done
  88.9 0.2 conditional.1
Async XLA Ops:
  7.2 81.0 %copy-start.1 = (s32[1024]{0:T(1024)S(1)}, s32[1024]{0:T(1024)}, u32[]{:S(2)}) copy-start(s32[1024]{0:T(1024)} %param.8) | copy-start | bytes 12292
  7.2 81.0 %copy-start.2 = (s32[1024]{0:T(1024)S(1)}, s32[1024]{0:T(1024)}, u32[]{:S(2)}) copy-start(s32[1024]{0:T(1024)} %param.9) | copy-start | bytes 12292
  7.2 81.7 %copy-start = (bf16[1024,1024]{1,0:T(8,128)(2,1)S(1)}, bf16[1024,1024]{1,0:T(8,128)(2,1)}, u32[]{:S(2)}) copy-start(bf16[1024,1024]{1,0:T(8,128)(2,1)} %rows_ref.1) | copy-start | bytes 6291460
  76.7 11.6 %all-to-all-start.4 = ((f32[16,1,128]{2,1,0:T(1,128)}), f32[16,1,128]{2,1,0:T(1,128)S(1)}, u32[]{:S(2)}, u32[]{:S(2)}) async-start(f32[16,1,128]{2,1,0:T(1,128)} %get-tuple-element.87), calls=%async_computation.4 | async-start | bytes 16384 | tf_op jit(solution)/shard_map/all_to_all | solution.py:523

commit v11 on v10

--- a/solution.py
+++ b/solution.py
@@ -300,18 +300,20 @@
     )(cluster_id.reshape(lines), valid.reshape(lines), embeddings)
 
 
-def on_units(size, count, multiply, use):
+def on_units(size, count, multiply, use, meanwhile=None):
     def body(*accs):
         for number in range(count + 2):
             if number < count:
                 multiply(number, number % 2, accs[number % 4])
+            if number == 1 and meanwhile is not None:
+                meanwhile()
             if number >= 2:
                 use(number - 2, pltpu.matmul_pop(accs[(number - 2) % 4]))
 
     pl.run_scoped(body, *[pltpu.ACC(mxu_id=number % 2)((size, STEP), F32) for number in range(4)])
 
 
-def triangle(total, rows, side, tops, line, across, down):
+def triangle(total, rows, side, mark, line, across, down):
     width = rows.shape[1]
     blocks = total // STEP
     seen = set()
@@ -327,7 +329,7 @@
         for row in range(column, blocks, 2):
             work.append((column, row, min(2, blocks - row)))
 
-    def run(work, count):
+    def run(work, count, meanwhile=None):
         def multiply(number, unit, acc):
             column, row, _ = work[number]
             for piece in range(width // STEP):
@@ -343,12 +345,13 @@
             column, row, _ = work[number]
             apart = iota((8, LANES), 1) - iota((8, LANES), 0)
             best = [jnp.full((8, LANES), -1.0, F32)] * (STEP // LANES)
+            tops = jnp.broadcast_to(line[:, column * STEP : (column + 1) * STEP], (8, STEP))
             for block in range(0, count * STEP, 8):
                 start = row * STEP + block
                 found = []
                 for part in range(STEP // LANES):
                     first = column * STEP + part * LANES
-                    allowed = side[start : start + 8, :] == tops[:, first : first + LANES]
+                    allowed = side[start : start + 8, :] == tops[:, part * LANES : (part + 1) * LANES]
                     if 0 <= start - first < LANES:
                         allowed = allowed & (apart != start - first)
                     here = scores[block : block + 8, part * LANES : (part + 1) * LANES]
@@ -359,9 +362,9 @@
             for part in range(STEP // LANES):
                 keep(down, (column * (STEP // LANES) + part) * 8, best[part])
 
-        on_units(count * STEP, len(work), multiply, use)
-
-    run([item for item in work if item[2] == 2], 2)
+        on_units(count * STEP, len(work), multiply, use, meanwhile)
+
+    run([item for item in work if item[2] == 2], 2, mark)
     run([item for item in work if item[2] == 1], 1)
     for column in range(blocks):
         for part in range(STEP // LANES):
@@ -378,30 +381,32 @@
     total = line.shape[1]
     rows = got_ref.reshape(total, got_ref.shape[2])
 
-    same = iota((SIZE, LANES), 0) == iota((SIZE, LANES), 1)
-    lanes = iota((1, 2 * LANES), 1)
-    lost = jnp.zeros((1, LANES), F32)
-    line[...] = jnp.zeros((1, total), F32)
-    for source in range(owners):
-        name = got_ref[source, SIZE - 16 : SIZE, :LANES].astype(F32)[15:16]
-        lost = jnp.maximum(lost, name)
-        found = jnp.sum(jnp.where(same, name, 0.0), axis=1, keepdims=True)
-        side[source * SIZE : (source + 1) * SIZE, :] = jnp.broadcast_to(
-            jnp.where(found == 0.0, -1.0, found), (SIZE, LANES)
-        )
-        base, shift = divmod(source * SIZE, LANES)
-        base *= LANES
-        name = jnp.where(lanes < SIZE, jnp.concatenate([name, name], axis=1), 0.0)
-        if shift:
-            name = pltpu.roll(name, shift, 1)
-        size = min(2 * LANES, total - base)
-        line[:, base : base + size] = line[:, base : base + size] + name[:, :size]
-    lost = jnp.max(jnp.where(lanes[:, :LANES] == LANES - 1, lost, 0.0))
-    lost_ref[0, 0] = (lost > 0.0).astype(jnp.int32)
-    tops = jnp.broadcast_to(line[...], (8, total))
+    def mark():
+        same = iota((SIZE, LANES), 0) == iota((SIZE, LANES), 1)
+        lanes = iota((1, 2 * LANES), 1)
+        lost = jnp.zeros((1, LANES), F32)
+        line[...] = jnp.zeros((1, total), F32)
+        for source in range(owners):
+            name = got_ref[source, SIZE - 16 : SIZE, :LANES].astype(F32)[15:16]
+            lost = jnp.maximum(lost, name)
+            found = jnp.sum(jnp.where(same, name, 0.0), axis=1, keepdims=True)
+            side[source * SIZE : (source + 1) * SIZE, :] = jnp.broadcast_to(
+                jnp.where(found == 0.0, -1.0, found), (SIZE, LANES)
+            )
+            base, shift = divmod(source * SIZE, LANES)
+            base *= LANES
+            name = jnp.where(lanes < SIZE, jnp.concatenate([name, name], axis=1), 0.0)
+            if shift:
+                name = pltpu.roll(name, shift, 1)
+            size = min(2 * LANES, total - base)
+            line[:, base : base + size] = line[:, base : base + size] + name[:, :size]
+        lost = jnp.max(jnp.where(lanes[:, :LANES] == LANES - 1, lost, 0.0))
+        lost_ref[0, 0] = (lost > 0.0).astype(jnp.int32)
+
     if total <= 2048:
-        triangle(total, rows, side, tops, line, *more)
+        triangle(total, rows, side, mark, line, *more)
     else:
+        mark()
         @pl.loop(0, total // STEP)
         def _(number):
             first = pl.multiple_of(number * STEP, STEP)

time: 89.6 us -> 89.6 us (level)
  no operation moved by 1% of the time
where the time goes in v11:
time: 89.6 us; the launch traced here: 89.4 us
  blocking collectives  66.1 us (74%)
  Pallas kernels  11.2 us (12%)
  waiting for transfers between devices  5.76 us (6%)
  starting transfers between devices  5.16 us (6%)
  between operations  0.9 us (1%)
    all_to_all x1, blocking collectives, swap(): lax.all_to_all(split, 'owners', split_axis=0, concat_axis=0, tiled=True)  66.1 us
    pallas_call x1, Pallas kernels, pack(): pl.pallas_call(functools.partial(pack_direct if small else pack_kernel, o...  7.17 us
    all_to_all x1, waiting for transfers between devices, shards(): lax.all_to_all(best, 'owners', split_axis=0, concat_axis=0, tiled=True)  5.76 us
    all_to_all x1, starting transfers between devices, shards(): lax.all_to_all(best, 'owners', split_axis=0, concat_axis=0, tiled=True)  5.16 us
    pallas_call x1, Pallas kernels, score(): pl.pallas_call(functools.partial(score_kernel, owners), out_shape=(pltpu....  3.36 us
  transfers between devices with their start and end apart: 1, of which 1 were waited for; matrix products, arithmetic and copies ran while one was open for 0% of the time, Pallas kernels for 0%

profile of v11, /device:TPU:0, one launch (start us, length us, event | category | flops | bytes accessed | tf_op | source)
XLA Modules:
  0.0 89.4 jit_solution(425557700902067246)
XLA Ops:
  0.0 7.2 %pack.1 = (bf16[1280,1024]{1,0:T(8,128)(2,1)}, s32[8,128]{1,0:T(8,128)S(1)}) custom-call(s32[8,128]{1,0:T(8,128)} %bitcast.36, s32[8,128]{1,0:T(8,128)} %bitcast.39, bf16[1024,1024]{1,0:T(8,128)(2,1)} %rows_ref.1), custom_call_target="tpu_custom_call" | custom-call | tf_op jit(solution)/shard_map/pack/pallas_call | solution.py:275
  7.2 0.0 copy-start.1
  7.2 0.0 copy-start.2
  7.2 0.0 copy-start
  7.2 66.1 %all_to_all.23.got_ref = bf16[16,80,1024]{2,1,0:T(8,128)(2,1)S(1)} all-to-all(bf16[16,80,1024]{2,1,0:T(8,128)(2,1)} %bitcast.34), channel_id=1, replica_groups=mesh['groups'=2,'owners'=16] {'owners'}, dimensions={0} | all-to-all | bytes 5242880 | tf_op jit(solution)/shard_map/all_to_all | solution.py:521
  73.3 3.4 %score.1 = (f32[16,1,128]{2,1,0:T(1,128)}, s32[1,1]{1,0:T(1,128)}) custom-call(bf16[16,80,1024]{2,1,0:T(8,128)(2,1)S(1)} %all_to_all.23.got_ref), custom_call_target="tpu_custom_call" | custom-call | tf_op jit(solution)/shard_map/score/pallas_call | solution.py:438
  76.7 5.2 %all-to-all-start.4 = ((f32[16,1,128]{2,1,0:T(1,128)}), f32[16,1,128]{2,1,0:T(1,128)S(1)}, u32[]{:S(2)}, u32[]{:S(2)}) async-start(f32[16,1,128]{2,1,0:T(1,128)} %get-tuple-element.87), calls=%async_computation.4 | async-start | bytes 16384 | tf_op jit(solution)/shard_map/all_to_all | solution.py:528
  82.5 5.8 %all-to-all-done.4.back_ref = f32[16,1,128]{2,1,0:T(1,128)S(1)} async-done(((f32[16,1,128]{2,1,0:T(1,128)}), f32[16,1,128]{2,1,0:T(1,128)S(1)}, u32[]{:S(2)}, u32[]{:S(2)}) %all-to-all-start.4) | async-done | bytes 8224 | tf_op jit(solution)/shard_map/all_to_all | solution.py:528
  88.3 0.0 copy-done.1
  88.3 0.0 copy-done.2
  88.3 0.7 place.1
  89.0 0.0 copy-done
  89.0 0.2 conditional.1
Async XLA Ops:
  7.2 81.1 %copy-start.1 = (s32[1024]{0:T(1024)S(1)}, s32[1024]{0:T(1024)}, u32[]{:S(2)}) copy-start(s32[1024]{0:T(1024)} %param.8) | copy-start | bytes 12292
  7.2 81.1 %copy-start.2 = (s32[1024]{0:T(1024)S(1)}, s32[1024]{0:T(1024)}, u32[]{:S(2)}) copy-start(s32[1024]{0:T(1024)} %param.9) | copy-start | bytes 12292
  7.2 81.8 %copy-start = (bf16[1024,1024]{1,0:T(8,128)(2,1)S(1)}, bf16[1024,1024]{1,0:T(8,128)(2,1)}, u32[]{:S(2)}) copy-start(bf16[1024,1024]{1,0:T(8,128)(2,1)} %rows_ref.1) | copy-start | bytes 6291460
  76.7 11.6 %all-to-all-start.4 = ((f32[16,1,128]{2,1,0:T(1,128)}), f32[16,1,128]{2,1,0:T(1,128)S(1)}, u32[]{:S(2)}, u32[]{:S(2)}) async-start(f32[16,1,128]{2,1,0:T(1,128)} %get-tuple-element.87), calls=%async_computation.4 | async-start | bytes 16384 | tf_op jit(solution)/shard_map/all_to_all | solution.py:528
